TPU v7x, 256 devices: a whole 4x4x8 slice. The times are simulated.
256 devices in a mesh: inst: 16 (over x_hi, z), px: 2 (over x_lo), pz: 8 (over y, core).
Axes of the slice: x: 4 (x_hi: 2, x_lo: 2; x = x_hi * 2 + x_lo), y: 4, z: 8, core: 2. Of those that a mesh axis runs over, the one named last changes fastest.
Arguments:
- stream_vel: bfloat16 [16, 16, 384, 1024], P('inst', 'px', None, 'pz'), may hold values from -6 to 6
- normal_vel: bfloat16 [16, 16, 384, 1024], P('inst', 'px', None, 'pz'), may hold values from -6 to 6
- span_vel: bfloat16 [16, 16, 384, 1024], P('inst', 'px', None, 'pz'), may hold values from -6 to 6
- adjoint_buoy: float32 [16, 16, 384, 1024], P('inst', 'px', None, 'pz'), may hold values from -6 to 6
- adjoint_normal: float32 [16, 16, 384, 1024], P('inst', 'px', None, 'pz'), may hold values from -6 to 6
Outputs:
- pseudo_update: float32 [16, 16, 384, 1024], P('inst', 'px', None, 'pz')
All inputs are finite; a program needn't handle non-finite values.
Results may differ from a plain program's by a relative error of at most 0.0003.
Values sent between devices are 32-bit elements; how exact they have to be, the bound alone decides.
No kernel may reach another device: no remote copies, remote signals or barrier semaphores. Data moves between devices by JAX's collectives and lax.ppermute only.
A program may use at most 128 MiB of HBM per device.

v0:
```python
import functools
import math

import jax
import jax.numpy as jnp
import ml_dtypes
import numpy as np
from jax import lax
from jax.experimental import pallas as pl
from jax.experimental.pallas import tpu as pltpu
from jax.sharding import PartitionSpec as P

box_length = 4.0 * math.pi
diffusivity = 0.01
omega_tide = 4.0
coupling = 50.0
span_step = 0.05

f32 = jnp.float32
bf16 = jnp.bfloat16


def first_line(count):
    d = np.arange(count)
    sign = 1.0 - 2.0 * (d % 2)
    safe = np.where(d == 0, 1.0, np.tan(np.pi * d / count))
    return np.where(d == 0, 0.0, 0.5 * sign / safe)


def second_line(count):
    d = np.arange(count)
    sign = 1.0 - 2.0 * (d % 2)
    safe = np.where(d == 0, 1.0, np.sin(np.pi * d / count))
    return np.where(d == 0, -(count * count) / 12.0 - 1.0 / 6.0, -0.5 * sign / (safe * safe))


def wall_table(count):
    order = count - 1
    j = np.arange(count)
    angle = np.pi * j / order
    ends = (j == 0) | (j == order)
    c = np.where(ends, 2.0, 1.0) * (1.0 - 2.0 * (j % 2))
    total = j[:, None] + j[None, :]
    differ = j[:, None] - j[None, :]
    gap = -2.0 * np.sin(np.pi * total / (2 * order)) * np.sin(np.pi * differ / (2 * order))
    table = c[:, None] / c[None, :] / np.where(differ == 0, 1.0, gap)
    corner = (2.0 * order * order + 1.0) / 6.0
    sine_sq = np.where(ends, 1.0, np.sin(angle) ** 2)
    centre = -np.cos(angle) / (2.0 * sine_sq)
    centre[0], centre[order] = corner, -corner
    table = np.where(differ == 0, np.diag(centre), table)
    spacing = np.pi / order * (np.sin(angle) + np.pi / order)
    return table, spacing


def three_parts(table, axis):
    high = table.astype(np.float32).astype(ml_dtypes.bfloat16)
    low = (table - high.astype(np.float64)).astype(np.float32).astype(ml_dtypes.bfloat16)
    return np.concatenate([high, high, low], axis=axis)


def split(x):
    high = x.astype(bf16)
    return high, (x - high.astype(f32)).astype(bf16)


def derivatives(blocks, table):
    planes, rows, width = blocks[0].shape
    parts = [split(x.reshape(planes * rows, width)) for x in blocks]
    high, low = ([p[i] for p in parts] for i in range(2))
    both = jnp.dot(jnp.concatenate(high + low + high, axis=1), table, preferred_element_type=f32)
    return both[:, :width].reshape(planes, rows, width), both[:, width:].reshape(planes, rows, width)


def wall_kernel(dx, core_ref, wall_ref, line_ref, scale_ref, b_ref, edge_ref, other_ref, u_ref, v_ref, w_ref, n_ref, part_ref, inv_ref, token_ref):
    count, rows, width = b_ref.shape
    pair = u_ref.shape[0]
    start = pl.program_id(0) * pair
    here = b_ref[pl.ds(start, pair)]
    high, low = split(jnp.concatenate([here[i] for i in range(pair)], axis=1))
    both = jnp.dot(wall_ref[...], jnp.concatenate([high, low, high], axis=0), preferred_element_type=f32)
    grad_x, curv_x = derivatives([here, other_ref[...]], line_ref[0])
    for i in range(pair):
        z = start + i
        lanes = slice(i * width, (i + 1) * width)
        u, v, w = (r[i].astype(f32) for r in (u_ref, v_ref, w_ref))
        above = jnp.where(z == count - 1, edge_ref[0], b_ref[jnp.minimum(z + 1, count - 1)])
        below = jnp.where(z == 0, edge_ref[1], b_ref[jnp.maximum(z - 1, 0)])
        grad_z = (above - below) * (1.0 / (2.0 * span_step))
        curv_z = (above - 2.0 * here[i] + below) * (diffusivity / (span_step * span_step))
        radius = scale_ref[1] + jnp.abs(u) * (1.0 / dx) + jnp.abs(v) * scale_ref[0] + jnp.abs(w) * (1.0 / span_step)
        inv_ref[i] = 1.0 / radius
        advect = u * grad_x[i] + v * both[:rows, lanes] + w * grad_z
        part_ref[i] = -advect - (curv_x[i] + both[rows:, lanes] + curv_z) - coupling * n_ref[i]
    token_ref[...] = jnp.zeros_like(token_ref)


def early_kernel(core_ref, table_ref, *refs):
    blocks, (u_ref, part_ref, out_ref, token_ref) = refs[:4], refs[4:]
    grad_x, curv_x = derivatives([r[...] for r in blocks], table_ref[0])
    out_ref[...] = part_ref[...] - (u_ref[...].astype(f32) * grad_x + curv_x)
    token_ref[...] = jnp.zeros_like(token_ref)


def late_kernel(half, core_ref, table_ref, *refs):
    lower, upper = refs[:2], refs[2:4]
    u_ref, steps_ref, out_ref, token_ref = refs[4:]
    second = pl.program_id(0) >= half
    grad_x, curv_x = derivatives([jnp.where(second, y[...], x[...]) for x, y in zip(lower, upper)], table_ref[0])
    out_ref[...] = steps_ref[...] - (u_ref[...].astype(f32) * grad_x + curv_x)
    token_ref[...] = jnp.zeros_like(token_ref)


def halves_kernel(before_ref, after_ref, onward_ref, return_ref, sems):
    half = onward_ref.shape[0]
    copies = [pltpu.make_async_copy(before_ref.at[k], onward_ref.at[k], sems.at[0, k]) for k in range(half)]
    copies += [pltpu.make_async_copy(after_ref.at[half + k], return_ref.at[k], sems.at[1, k]) for k in range(half)]
    for copy in copies:
        copy.start()
    for copy in copies:
        copy.wait()


def follow_kernel(*refs):
    pass


def in_parts(count, sources, buffers, result, target, in_sems, out_sems, work):
    def part(k):
        return [pltpu.make_async_copy(x.at[at], y.at[at], in_sems.at[i, k]) for i, (x, y) in enumerate(zip(sources, buffers))]

    def out(k):
        return pltpu.make_async_copy(result.at[at], target.at[at], out_sems.at[k])

    for k in range(count):
        at = work.where(k)
        for copy in part(k):
            copy.start()
    for k in range(count):
        at = work.where(k)
        for copy in part(k):
            copy.wait()
        work.do(k)
        out(k).start()
    for k in range(count):
        at = work.where(k)
        out(k).wait()


class TimePart:
    def __init__(self, weights, size, source, result):
        self.weights, self.size, self.source, self.result = weights, size, source, result

    def where(self, k):
        return (slice(None), pl.ds(k * self.size, self.size))

    def do(self, k):
        weights, count = self.weights, self.source.shape[0]
        half = count // 2

        def body(step, carry):
            rows = pl.ds(pl.multiple_of(k * self.size + step * 8, 8), 8)
            b = [self.source[i, rows, :] for i in range(count)]
            totals = [weights[half] * b[(i + half) % count] for i in range(count)]
            for i in range(half):
                for d in range(1, half):
                    differ = b[(i + d) % count] - b[(i - d) % count]
                    totals[i] = totals[i] + weights[d] * differ
                    totals[i + half] = totals[i + half] - weights[half - d] * differ
            for i in range(count):
                self.result[i, rows, :] = totals[i]
            return carry

        lax.fori_loop(0, self.size // 8, body, 0)


class LastPart:
    def __init__(self, size, steps, time, inv, result):
        self.size, self.steps, self.time, self.inv, self.result = size, steps, time, inv, result

    def where(self, k):
        return (pl.ds(k * self.size, self.size),)

    def do(self, k):
        at = self.where(k)
        self.result[at] = (self.steps[at] - self.time[at]) * self.inv[at]


def time_kernel(weights, parts, in_ref, *refs):
    out_ref, source, result, in_sems, out_sems = refs[-5:]
    work = TimePart(weights, in_ref.shape[1] // parts, source, result)
    in_parts(parts, [in_ref], [source], result, out_ref, in_sems, out_sems, work)


def last_kernel(parts, time_ref, inv_ref, steps_ref, out_ref, steps, result, in_sems, out_sems):
    work = LastPart(steps_ref.shape[0] // parts, steps, time_ref, inv_ref, result)
    in_parts(parts, [steps_ref], [steps], result, out_ref, in_sems, out_sems, work)


def on_device(stream_vel, normal_vel, span_vel, adjoint_buoy, adjoint_normal):
    _, planes, rows, width = adjoint_buoy.shape
    count_x, count_i, count_p = (lax.axis_size(a) for a in ("pz", "inst", "px"))
    full = width * count_x
    dx = box_length / full
    wave = 2.0 * math.pi / box_length

    cores = 2
    groups = (0,), (-1, 1), (2,)

    def line_table(core, chips):
        offsets = [cores * step + other - core for step in chips for other in (core, 1 - core)]
        k = np.concatenate([np.arange(width) + width * o for o in offsets])
        d = (np.arange(width)[None, :] - k[:, None]) % full
        table = np.concatenate([wave * first_line(full)[d], diffusivity * wave * wave * second_line(full)[d]], axis=1)
        return three_parts(table, 0)

    first, early, late = (jnp.asarray(np.stack([line_table(c, t) for c in range(cores)])) for t in groups)
    normal_table, spacing = wall_table(rows)
    wall = np.concatenate([normal_table, diffusivity * (normal_table @ normal_table)], axis=0)
    wall = jnp.asarray(three_parts(wall, 1))
    steady = 1.0 + omega_tide * count_i / 2.0 + 2.0 * diffusivity * (1.0 / dx**2 + 1.0 / spacing**2 + 1.0 / span_step**2)
    scale = np.stack([1.0 / spacing, steady]).astype(np.float32)[:, :, None]
    scale = np.broadcast_to(scale, (2, rows, width))
    weights = [float(x) for x in omega_tide * first_line(count_i)]

    core = (lax.axis_index("pz") % cores).astype(jnp.int32).reshape(1)

    b, u, v, w, n = (x[0] for x in (adjoint_buoy, stream_vel, normal_vel, span_vel, adjoint_normal))

    share = planes * rows // count_i
    exchange = functools.partial(lax.all_to_all, axis_name="inst", split_axis=0, concat_axis=0, tiled=True)
    sent = exchange(b.reshape(count_i, share, width))

    members = range(count_x)
    onward = [(i, (i + cores) % count_x) for i in members]
    return_ = [(j, i) for i, j in onward]
    partner = [(i, i ^ 1) for i in members]
    half = planes // 2
    before = lax.ppermute(b, "pz", onward)
    after = lax.ppermute(b, "pz", return_)
    other = lax.ppermute(b, "pz", partner)
    swap = [(i, (i + 1) % count_p) for i in range(count_p)]
    back = [(j, i) for i, j in swap]
    if count_p == 2:
        edge = lax.ppermute(jnp.stack([b[0], b[planes - 1]]), "px", swap)
    else:
        edge = jnp.stack([lax.ppermute(b[0], "px", back), lax.ppermute(b[planes - 1], "px", swap)])

    pair = 2
    anywhere, in_memory = pl.BlockSpec(memory_space=pl.ANY), pl.BlockSpec(memory_space=pltpu.HBM)
    params = lambda size: pltpu.CompilerParams(vmem_limit_bytes=size * 2**20)
    spec = lambda f: pl.BlockSpec((pair, rows, width), lambda s, c: (f(s), 0, 0))
    two = spec(lambda s: s)
    fixed = lambda *shape: pl.BlockSpec(shape, lambda s, c: (0,) * len(shape))
    table = lambda t: pl.BlockSpec((1,) + t.shape[1:], lambda s, c: (c[0], 0, 0))
    part, inv, token = pl.pallas_call(
        functools.partial(wall_kernel, dx),
        out_shape=[jax.ShapeDtypeStruct(b.shape, f32)] * 2 + [jax.ShapeDtypeStruct((8, width), f32)],
        grid_spec=pltpu.PrefetchScalarGridSpec(
            num_scalar_prefetch=1,
            grid=(planes // pair,),
            in_specs=[fixed(*wall.shape), table(first), fixed(*scale.shape), fixed(*b.shape), fixed(2, rows, width)] + [two] * 5,
            out_specs=[two] * 2 + [fixed(8, width)],
        ),
        compiler_params=params(24),
        cost_estimate=pl.CostEstimate(flops=16 * rows * b.size, bytes_accessed=b.size * 28, transcendentals=0),
        name="wall_terms",
    )(core, wall, first, jnp.asarray(scale), b, edge, other, u, v, w, n)

    def follow(name, *arrays, after):
        return pl.pallas_call(
            follow_kernel,
            out_shape=[jax.ShapeDtypeStruct(x.shape, f32) for x in arrays],
            in_specs=[anywhere] * (len(arrays) + 1),
            out_specs=[anywhere] * len(arrays),
            input_output_aliases={i: i for i in range(len(arrays))},
            compiler_params=params(1),
            name=name,
        )(*arrays, after)

    onward_half, return_half = pl.pallas_call(
        halves_kernel,
        out_shape=[jax.ShapeDtypeStruct((half, rows, width), f32)] * 2,
        in_specs=[anywhere] * 2,
        out_specs=[anywhere] * 2,
        scratch_shapes=[pltpu.SemaphoreType.DMA((2, half))],
        compiler_params=params(1),
        cost_estimate=pl.CostEstimate(flops=0, bytes_accessed=b.size * 8, transcendentals=0),
        name="halves",
    )(before, after)
    far_0 = lax.ppermute(onward_half, "pz", onward)
    far_1 = lax.ppermute(return_half, "pz", return_)

    parts = 4
    applied = pl.pallas_call(
        functools.partial(time_kernel, weights, parts),
        out_shape=jax.ShapeDtypeStruct(sent.shape, f32),
        in_specs=[in_memory, anywhere],
        out_specs=in_memory,
        scratch_shapes=[pltpu.VMEM(sent.shape, f32)] * 2
        + [pltpu.SemaphoreType.DMA((1, parts)), pltpu.SemaphoreType.DMA((parts,))],
        compiler_params=params(60),
        cost_estimate=pl.CostEstimate(flops=sent.size * 16, bytes_accessed=sent.size * 8, transcendentals=0),
        name="time_term",
    )(sent, token)
    time_term = exchange(applied).reshape(planes, rows, width)

    with_other = lambda r: (r, lax.ppermute(r, "pz", partner))
    last_low = half // pair - 1
    in_lower, in_upper = spec(lambda s: jnp.minimum(s, last_low)), spec(lambda s: jnp.maximum(s - last_low - 1, 0))

    def line_terms(kernel, name, chips, size, specs, operands):
        return pl.pallas_call(
            kernel,
            out_shape=[jax.ShapeDtypeStruct(b.shape, f32), jax.ShapeDtypeStruct((8, width), f32)],
            grid_spec=pltpu.PrefetchScalarGridSpec(
                num_scalar_prefetch=1, grid=(planes // pair,), in_specs=specs, out_specs=[two, fixed(8, width)]
            ),
            compiler_params=params(size),
            cost_estimate=pl.CostEstimate(
                flops=12 * chips * cores * width * b.size, bytes_accessed=b.size * 4 * (3 + 2 * chips), transcendentals=0
            ),
            name=name,
        )(core, *operands)

    operands = (early, *with_other(before), *with_other(after), u, part)
    steps, token = line_terms(early_kernel, "early_terms", 2, 60, [table(early)] + [two] * 6, operands)
    far_0, far_1 = follow("follow_early", far_0, far_1, after=token)
    operands = (late, *with_other(far_0), *with_other(far_1), u, steps)
    specs = [table(late)] + [in_lower] * 2 + [in_upper] * 2 + [two] * 2
    steps, _ = line_terms(functools.partial(late_kernel, half // pair), "late_terms", 1, 60, specs, operands)

    out = pl.pallas_call(
        functools.partial(last_kernel, planes),
        out_shape=jax.ShapeDtypeStruct(b.shape, f32),
        in_specs=[pl.BlockSpec(memory_space=pltpu.VMEM)] * 2 + [in_memory],
        out_specs=in_memory,
        scratch_shapes=[pltpu.VMEM(b.shape, f32)] * 2
        + [pltpu.SemaphoreType.DMA((1, planes)), pltpu.SemaphoreType.DMA((planes,))],
        compiler_params=params(58),
        cost_estimate=pl.CostEstimate(flops=2 * b.size, bytes_accessed=b.size * 16, transcendentals=0),
        name="last",
    )(time_term, inv, steps)
    return out[None]


def solution(mesh):
    spec = P("inst", "px", None, "pz")
    return jax.shard_map(on_device, mesh=mesh, in_specs=(spec,) * 5, out_specs=spec, check_vma=False)
```

profile of v0, /device:TPU:56, one launch (start us, length us, event | category | flops | bytes accessed | tf_op | source)
XLA Modules:
  0.0 102.1 jit_solution(2831276251958502368)
XLA Ops:
  0.0 11.2 %all-to-all-start = ((f32[16,192,128]{2,1,0:T(8,128)}), f32[16,192,128]{2,1,0:T(8,128)}, u32[]{:S(2)}, u32[]{:S(2)}) async-start(f32[16,192,128]{2,1,0:T(8,128)} %bitcast.13), calls=%async_computation | async-start | bytes 3145728 | tf_op jit(solution)/shard_map/all_to_all | solution.py:232
  11.3 0.3 collective-permute-start.2
  11.6 1.8 %collective-permute-start.3 = (f32[8,384,128]{2,1,0:T(8,128)S(1)}, f32[8,384,128]{2,1,0:T(8,128)}, u32[]{:S(2)}, u32[]{:S(2)}) collective-permute-start(f32[8,384,128]{2,1,0:T(8,128)S(1)} %bitcast.16), channel_id=1, source_target_pairs={{2,0},{3,1},{4,2},{5,3},{6,4},{7,5},{0,6},{1,7},{10,8},{11,9},{12,... | collective-permute-start | bytes 4718600 | tf_op jit(solution)/shard_map/ppermute | solution.py:240
  13.5 0.8 pad_maximum_fusion
  14.2 0.6 collective-permute-start
  14.8 15.2 %collective-permute-done.edge_ref = f32[2,384,128]{2,1,0:T(8,128)S(1)} collective-permute-done((f32[2,384,128]{2,1,0:T(8,128)}, f32[2,384,128]{2,1,0:T(8,128)S(1)}, u32[]{:S(2)}, u32[]{:S(2)}) %collective-permute-start) | collective-permute-done | bytes 393248 | tf_op jit(solution)/shard_map/ppermute | solution.py:245
  30.2 1.5 %copy-done.4 = bf16[768,1152]{1,0:T(8,128)(2,1)S(1)} copy-done((bf16[768,1152]{1,0:T(8,128)(2,1)S(1)}, bf16[768,1152]{1,0:T(8,128)(2,1)}, u32[]{:S(2)}) %copy-start.4) | copy-done | bytes 1769496
  31.7 1.4 %copy-done.7 = f32[1,8,384,128]{3,2,1,0:T(8,128)S(1)} copy-done((f32[1,8,384,128]{3,2,1,0:T(8,128)S(1)}, f32[1,8,384,128]{3,2,1,0:T(8,128)}, u32[]{:S(2)}) %copy-start.7) | copy-done | bytes 1572888
  33.1 1.1 %copy-done.9 = bf16[1,8,384,128]{3,2,1,0:T(8,128)(2,1)S(1)} copy-done((bf16[1,8,384,128]{3,2,1,0:T(8,128)(2,1)S(1)}, bf16[1,8,384,128]{3,2,1,0:T(8,128)(2,1)}, u32[]{:S(2)}) %copy-start.9) | copy-done | bytes 786456
  34.2 1.1 %copy-done.10 = bf16[2,768,256]{2,1,0:T(8,128)(2,1)S(1)} copy-done((bf16[2,768,256]{2,1,0:T(8,128)(2,1)S(1)}, bf16[2,768,256]{2,1,0:T(8,128)(2,1)}, u32[]{:S(2)}) %copy-start.10) | copy-done | bytes 786456
  35.4 5.8 %wall_terms.1 = (f32[8,384,128]{2,1,0:T(8,128)S(1)}, f32[8,384,128]{2,1,0:T(8,128)S(1)}, f32[8,128]{1,0:T(8,128)S(1)}) custom-call(s32[1]{0:T(128)} %bitcast.1.core_ref, bf16[768,1152]{1,0:T(8,128)(2,1)S(1)} %copy-done.4, bf16[2,768,256]{2,1,0:T(8,128)(2,1)S(1)} %copy-done.10, f32[2,384,128]{2,1,0:T(8,128)S(1)} %jit_solution_.3.scale_ref, ...), custom_call_target="tpu_custom_call" | custom-call | flops 2415919104 | bytes 11010048 | tf_op jit(solution)/shard_map/wall_terms/pallas_call | solution.py:256
  41.2 1.2 %copy-done.5 = f32[8,384,128]{2,1,0:T(8,128)} copy-done((f32[8,384,128]{2,1,0:T(8,128)}, f32[8,384,128]{2,1,0:T(8,128)S(1)}, u32[]{:S(2)}) %copy-start.5) | copy-done | bytes 1572888
  42.4 1.2 %copy-done.6 = f32[8,384,128]{2,1,0:T(8,128)} copy-done((f32[8,384,128]{2,1,0:T(8,128)}, f32[8,384,128]{2,1,0:T(8,128)S(1)}, u32[]{:S(2)}) %copy-start.6) | copy-done | bytes 1572888
  43.6 0.6 copy-done.12
  44.2 6.2 %all-to-all-done.in_ref = f32[16,192,128]{2,1,0:T(8,128)} async-done(((f32[16,192,128]{2,1,0:T(8,128)}), f32[16,192,128]{2,1,0:T(8,128)}, u32[]{:S(2)}, u32[]{:S(2)}) %all-to-all-start) | async-done | bytes 1572896 | tf_op jit(solution)/shard_map/all_to_all | solution.py:232
  50.4 3.0 %time_term.1 = f32[16,192,128]{2,1,0:T(8,128)} custom-call(f32[16,192,128]{2,1,0:T(8,128)} %all-to-all-done.in_ref, f32[8,128]{1,0:T(8,128)} %copy-done.12), custom_call_target="tpu_custom_call" | custom-call | flops 6291456 | bytes 3145728 | tf_op jit(solution)/shard_map/time_term/pallas_call | solution.py:295
  53.4 5.3 %all-to-all-start.1 = ((f32[16,192,128]{2,1,0:T(8,128)}), f32[16,192,128]{2,1,0:T(8,128)}, u32[]{:S(2)}, u32[]{:S(2)}) async-start(f32[16,192,128]{2,1,0:T(8,128)} %time_term.1), calls=%async_computation.1 | async-start | bytes 3145728 | tf_op jit(solution)/shard_map/all_to_all | solution.py:306
  58.9 0.5 collective-permute-start.7
  59.4 1.5 %halves.1 = (f32[4,384,128]{2,1,0:T(8,128)S(1)}, f32[4,384,128]{2,1,0:T(8,128)S(1)}) custom-call(f32[8,384,128]{2,1,0:T(8,128)} %collective-permute-done.2.before_ref.refs_0_, f32[8,384,128]{2,1,0:T(8,128)} %collective-permute-done.3.after_ref.refs_2_), custom_call_target="tpu_custom_call" | custom-call | bytes 3145728 | tf_op jit(solution)/shard_map/halves/pallas_call | solution.py:281
  61.2 1.8 %collective-permute-start.5 = (f32[4,384,128]{2,1,0:T(8,128)S(1)}, f32[4,384,128]{2,1,0:T(8,128)S(1)}, u32[]{:S(2)}, u32[]{:S(2)}) collective-permute-start(f32[4,384,128]{2,1,0:T(8,128)S(1)} %get-tuple-element.18), channel_id=1, source_target_pairs={{2,0},{3,1},{4,2},{5,3},{6,4},{7,5},{0,6},{1,7},{10,8},{11,9},{12,... | collective-permute-start | bytes 2359304 | tf_op jit(solution)/shard_map/ppermute | solution.py:292
  63.0 1.8 %collective-permute-done.7.refs_3_ = f32[8,384,128]{2,1,0:T(8,128)} collective-permute-done((f32[8,384,128]{2,1,0:T(8,128)}, f32[8,384,128]{2,1,0:T(8,128)}, u32[]{:S(2)}, u32[]{:S(2)}) %collective-permute-start.7) | collective-permute-done | bytes 1572896 | tf_op jit(solution)/shard_map/ppermute | solution.py:308
  64.9 7.1 %early_terms.1 = (f32[8,384,128]{2,1,0:T(8,128)}, f32[8,128]{1,0:T(8,128)}) custom-call(s32[1]{0:T(128)} %bitcast.1.core_ref, bf16[2,1536,256]{2,1,0:T(8,128)(2,1)} %constant.28.clone.table_ref, f32[8,384,128]{2,1,0:T(8,128)} %collective-permute-done.2.before_ref.refs_0_, f32[8,384,128]{2,1,0:T(8,128)} %collective-permute-done.6.refs_1_, ...), custom_call_target="tpu_custom_call" | custom-call | flops 2415919104 | bytes 11010048 | tf_op jit(solution)/shard_map/early_terms/pallas_call | solution.py:313
  72.0 8.6 %collective-permute-done.4.refs_0_ = f32[4,384,128]{2,1,0:T(8,128)S(1)} collective-permute-done((f32[4,384,128]{2,1,0:T(8,128)S(1)}, f32[4,384,128]{2,1,0:T(8,128)S(1)}, u32[]{:S(2)}, u32[]{:S(2)}) %collective-permute-start.4) | collective-permute-done | bytes 786464 | tf_op jit(solution)/shard_map/ppermute | solution.py:291
  80.5 1.3 %collective-permute-done.5.refs_1_ = f32[4,384,128]{2,1,0:T(8,128)S(1)} collective-permute-done((f32[4,384,128]{2,1,0:T(8,128)S(1)}, f32[4,384,128]{2,1,0:T(8,128)S(1)}, u32[]{:S(2)}, u32[]{:S(2)}) %collective-permute-start.5) | collective-permute-done | bytes 786464 | tf_op jit(solution)/shard_map/ppermute | solution.py:292
  81.8 0.7 copy-done.11
  82.5 0.5 collective-permute-start.9
  83.0 1.8 %collective-permute-done.8.refs_1_ = f32[4,384,128]{2,1,0:T(8,128)S(1)} collective-permute-done((f32[4,384,128]{2,1,0:T(8,128)S(1)}, f32[4,384,128]{2,1,0:T(8,128)S(1)}, u32[]{:S(2)}, u32[]{:S(2)}) %collective-permute-start.8) | collective-permute-done | bytes 786464 | tf_op jit(solution)/shard_map/ppermute | solution.py:308
  84.8 1.1 %collective-permute-done.9.refs_3_ = f32[4,384,128]{2,1,0:T(8,128)S(1)} collective-permute-done((f32[4,384,128]{2,1,0:T(8,128)S(1)}, f32[4,384,128]{2,1,0:T(8,128)S(1)}, u32[]{:S(2)}, u32[]{:S(2)}) %collective-permute-start.9) | collective-permute-done | bytes 786464 | tf_op jit(solution)/shard_map/ppermute | solution.py:308
  85.9 0.9 copy-done.14
  86.8 5.6 %late_terms.1 = (f32[8,384,128]{2,1,0:T(8,128)}, f32[8,128]{1,0:T(8,128)}) custom-call(s32[1]{0:T(128)} %bitcast.1.core_ref, bf16[2,768,256]{2,1,0:T(8,128)(2,1)} %constant.29.clone.table_ref, f32[4,384,128]{2,1,0:T(8,128)} %copy-done.2, f32[4,384,128]{2,1,0:T(8,128)} %copy-done.13, f32[4,384,128]{2,1,0:T(8,128)} %copy-done.3, f32[4,384,128]{2,1,0:T(8,128)} %copy-done.14, ...), custom_call_target="tpu_custom_call" | custom-call | flops 1207959552 | bytes 7864320 | tf_op jit(solution)/shard_map/late_terms/pallas_call | solution.py:313
  92.4 5.5 %all-to-all-done.1 = f32[16,192,128]{2,1,0:T(8,128)} async-done(((f32[16,192,128]{2,1,0:T(8,128)}), f32[16,192,128]{2,1,0:T(8,128)}, u32[]{:S(2)}, u32[]{:S(2)}) %all-to-all-start.1) | async-done | bytes 1572896 | tf_op jit(solution)/shard_map/all_to_all | solution.py:306
  97.9 4.2 %last.1 = f32[8,384,128]{2,1,0:T(8,128)} custom-call(f32[8,384,128]{2,1,0:T(8,128)} %bitcast.9.time_ref, f32[8,384,128]{2,1,0:T(8,128)} %copy-done.6, f32[8,384,128]{2,1,0:T(8,128)} %get-tuple-element.24.steps_ref), custom_call_target="tpu_custom_call" | custom-call | flops 786432 | bytes 6291456 | tf_op jit(solution)/shard_map/last/pallas_call | solution.py:333
  (34 shorter events, 0.7 us)
Async XLA Ops:
  0.0 11.2 %copy-start = (f32[1,8,384,128]{3,2,1,0:T(8,128)S(1)}, f32[1,8,384,128]{3,2,1,0:T(8,128)}, u32[]{:S(2)}) copy-start(f32[1,8,384,128]{3,2,1,0:T(8,128)} %param.13) | copy-start | bytes 4718596
  0.0 50.4 %all-to-all-start = ((f32[16,192,128]{2,1,0:T(8,128)}), f32[16,192,128]{2,1,0:T(8,128)}, u32[]{:S(2)}, u32[]{:S(2)}) async-start(f32[16,192,128]{2,1,0:T(8,128)} %bitcast.13), calls=%async_computation | async-start | bytes 3145728 | tf_op jit(solution)/shard_map/all_to_all | solution.py:232
  11.2 18.8 %copy-start.15 = (f32[2,384]{1,0:T(2,128)S(1)}, f32[2,384]{1,0:T(2,128)}, u32[]{:S(2)}) copy-start(f32[2,384]{1,0:T(2,128)} %constant.31.clone) | copy-start | bytes 9220
  11.2 19.0 %copy-start.1 = (bf16[1,8,384,128]{3,2,1,0:T(8,128)(2,1)S(1)}, bf16[1,8,384,128]{3,2,1,0:T(8,128)(2,1)}, u32[]{:S(2)}) copy-start(bf16[1,8,384,128]{3,2,1,0:T(8,128)(2,1)} %param.10) | copy-start | bytes 2359300
  11.2 19.0 %copy-start.8 = (bf16[1,8,384,128]{3,2,1,0:T(8,128)(2,1)S(1)}, bf16[1,8,384,128]{3,2,1,0:T(8,128)(2,1)}, u32[]{:S(2)}) copy-start(bf16[1,8,384,128]{3,2,1,0:T(8,128)(2,1)} %param.11) | copy-start | bytes 2359300
  11.2 18.8 %collective-permute-start.1 = (f32[8,384,128]{2,1,0:T(8,128)S(1)}, f32[8,384,128]{2,1,0:T(8,128)}, u32[]{:S(2)}, u32[]{:S(2)}) collective-permute-start(f32[8,384,128]{2,1,0:T(8,128)S(1)} %bitcast.14), channel_id=1, source_target_pairs={{0,1},{1,0},{2,3},{3,2},{4,5},{5,4},{6,7},{7,6},{8,9},{9,8},{10,11... | collective-permute-start | bytes 4718600 | tf_op jit(solution)/shard_map/ppermute | solution.py:241
  11.3 47.4 %collective-permute-start.2 = (f32[8,384,128]{2,1,0:T(8,128)S(1)}, f32[8,384,128]{2,1,0:T(8,128)}, u32[]{:S(2)}, u32[]{:S(2)}) collective-permute-start(f32[8,384,128]{2,1,0:T(8,128)S(1)} %bitcast.15), channel_id=1, source_target_pairs={{0,2},{1,3},{2,4},{3,5},{4,6},{5,7},{6,0},{7,1},{8,10},{9,11},{10,... | collective-permute-start | bytes 4718600 | tf_op jit(solution)/shard_map/ppermute | solution.py:239
  11.6 47.3 %collective-permute-start.3 = (f32[8,384,128]{2,1,0:T(8,128)S(1)}, f32[8,384,128]{2,1,0:T(8,128)}, u32[]{:S(2)}, u32[]{:S(2)}) collective-permute-start(f32[8,384,128]{2,1,0:T(8,128)S(1)} %bitcast.16), channel_id=1, source_target_pairs={{2,0},{3,1},{4,2},{5,3},{6,4},{7,5},{0,6},{1,7},{10,8},{11,9},{12,... | collective-permute-start | bytes 4718600 | tf_op jit(solution)/shard_map/ppermute | solution.py:240
  14.2 15.8 %collective-permute-start = (f32[2,384,128]{2,1,0:T(8,128)}, f32[2,384,128]{2,1,0:T(8,128)S(1)}, u32[]{:S(2)}, u32[]{:S(2)}) collective-permute-start(f32[2,384,128]{2,1,0:T(8,128)} %pad_maximum_fusion), channel_id=1, source_target_pairs={{0,8},{8,0},{1,9},{9,1},{2,10},{10,2},{3,11},{11,3},{4,12},{12,4},... | collective-permute-start | bytes 1179656 | tf_op jit(solution)/shard_map/ppermute | solution.py:245
  30.2 1.5 %copy-start.4 = (bf16[768,1152]{1,0:T(8,128)(2,1)S(1)}, bf16[768,1152]{1,0:T(8,128)(2,1)}, u32[]{:S(2)}) copy-start(bf16[768,1152]{1,0:T(8,128)(2,1)} %constant.30.clone.wall_ref) | copy-start | bytes 5308420
  31.7 1.4 %copy-start.7 = (f32[1,8,384,128]{3,2,1,0:T(8,128)S(1)}, f32[1,8,384,128]{3,2,1,0:T(8,128)}, u32[]{:S(2)}) copy-start(f32[1,8,384,128]{3,2,1,0:T(8,128)} %param.14) | copy-start | bytes 4718596
  33.1 1.1 %copy-start.9 = (bf16[1,8,384,128]{3,2,1,0:T(8,128)(2,1)S(1)}, bf16[1,8,384,128]{3,2,1,0:T(8,128)(2,1)}, u32[]{:S(2)}) copy-start(bf16[1,8,384,128]{3,2,1,0:T(8,128)(2,1)} %param.12) | copy-start | bytes 2359300
  34.2 1.1 %copy-start.10 = (bf16[2,768,256]{2,1,0:T(8,128)(2,1)S(1)}, bf16[2,768,256]{2,1,0:T(8,128)(2,1)}, u32[]{:S(2)}) copy-start(bf16[2,768,256]{2,1,0:T(8,128)(2,1)} %constant.27.clone.line_ref) | copy-start | bytes 2359300
  41.2 1.2 %copy-start.5 = (f32[8,384,128]{2,1,0:T(8,128)}, f32[8,384,128]{2,1,0:T(8,128)S(1)}, u32[]{:S(2)}) copy-start(f32[8,384,128]{2,1,0:T(8,128)S(1)} %get-tuple-element.19.refs_5_) | copy-start | bytes 4718596
  42.4 1.2 %copy-start.6 = (f32[8,384,128]{2,1,0:T(8,128)}, f32[8,384,128]{2,1,0:T(8,128)S(1)}, u32[]{:S(2)}) copy-start(f32[8,384,128]{2,1,0:T(8,128)S(1)} %get-tuple-element.16.inv_ref) | copy-start | bytes 4718596
  43.6 0.6 copy-start.12
  53.4 44.5 %all-to-all-start.1 = ((f32[16,192,128]{2,1,0:T(8,128)}), f32[16,192,128]{2,1,0:T(8,128)}, u32[]{:S(2)}, u32[]{:S(2)}) async-start(f32[16,192,128]{2,1,0:T(8,128)} %time_term.1), calls=%async_computation.1 | async-start | bytes 3145728 | tf_op jit(solution)/shard_map/all_to_all | solution.py:306
  58.8 4.2 %collective-permute-start.6 = (f32[8,384,128]{2,1,0:T(8,128)}, f32[8,384,128]{2,1,0:T(8,128)}, u32[]{:S(2)}, u32[]{:S(2)}) collective-permute-start(f32[8,384,128]{2,1,0:T(8,128)} %collective-permute-done.2.before_ref.refs_0_), channel_id=1, source_target_pairs={{0,1},{1,0},{2,3},{3,2},{4,5},{5,4},{6,7},{7,6},{8,9},{9,8},{10,11... | collective-permute-start | bytes 4718600 | tf_op jit(solution)/shard_map/ppermute | solution.py:308
  58.9 6.0 %collective-permute-start.7 = (f32[8,384,128]{2,1,0:T(8,128)}, f32[8,384,128]{2,1,0:T(8,128)}, u32[]{:S(2)}, u32[]{:S(2)}) collective-permute-start(f32[8,384,128]{2,1,0:T(8,128)} %collective-permute-done.3.after_ref.refs_2_), channel_id=1, source_target_pairs={{0,1},{1,0},{2,3},{3,2},{4,5},{5,4},{6,7},{7,6},{8,9},{9,8},{10,11... | collective-permute-start | bytes 4718600 | tf_op jit(solution)/shard_map/ppermute | solution.py:308
  60.9 19.6 %collective-permute-start.4 = (f32[4,384,128]{2,1,0:T(8,128)S(1)}, f32[4,384,128]{2,1,0:T(8,128)S(1)}, u32[]{:S(2)}, u32[]{:S(2)}) collective-permute-start(f32[4,384,128]{2,1,0:T(8,128)S(1)} %get-tuple-element.17), channel_id=1, source_target_pairs={{0,2},{1,3},{2,4},{3,5},{4,6},{5,7},{6,0},{7,1},{8,10},{9,11},{10,... | collective-permute-start | bytes 2359304 | tf_op jit(solution)/shard_map/ppermute | solution.py:291
  61.2 20.6 %collective-permute-start.5 = (f32[4,384,128]{2,1,0:T(8,128)S(1)}, f32[4,384,128]{2,1,0:T(8,128)S(1)}, u32[]{:S(2)}, u32[]{:S(2)}) collective-permute-start(f32[4,384,128]{2,1,0:T(8,128)S(1)} %get-tuple-element.18), channel_id=1, source_target_pairs={{2,0},{3,1},{4,2},{5,3},{6,4},{7,5},{0,6},{1,7},{10,8},{11,9},{12,... | collective-permute-start | bytes 2359304 | tf_op jit(solution)/shard_map/ppermute | solution.py:292
  81.8 0.7 copy-start.11
  82.5 3.4 %copy-start.2 = (f32[4,384,128]{2,1,0:T(8,128)}, f32[4,384,128]{2,1,0:T(8,128)S(1)}, u32[]{:S(2)}) copy-start(f32[4,384,128]{2,1,0:T(8,128)S(1)} %get-tuple-element.21.refs_0_) | copy-start | bytes 2359300
  82.5 3.4 %copy-start.3 = (f32[4,384,128]{2,1,0:T(8,128)}, f32[4,384,128]{2,1,0:T(8,128)S(1)}, u32[]{:S(2)}) copy-start(f32[4,384,128]{2,1,0:T(8,128)S(1)} %get-tuple-element.22.refs_2_) | copy-start | bytes 2359300
  82.5 2.3 %collective-permute-start.8 = (f32[4,384,128]{2,1,0:T(8,128)S(1)}, f32[4,384,128]{2,1,0:T(8,128)S(1)}, u32[]{:S(2)}, u32[]{:S(2)}) collective-permute-start(f32[4,384,128]{2,1,0:T(8,128)S(1)} %get-tuple-element.21.refs_0_), channel_id=1, source_target_pairs={{0,1},{1,0},{2,3},{3,2},{4,5},{5,4},{6,7},{7,6},{8,9},{9,8},{10,11... | collective-permute-start | bytes 2359304 | tf_op jit(solution)/shard_map/ppermute | solution.py:308
  82.5 3.4 %collective-permute-start.9 = (f32[4,384,128]{2,1,0:T(8,128)S(1)}, f32[4,384,128]{2,1,0:T(8,128)S(1)}, u32[]{:S(2)}, u32[]{:S(2)}) collective-permute-start(f32[4,384,128]{2,1,0:T(8,128)S(1)} %get-tuple-element.22.refs_2_), channel_id=1, source_target_pairs={{0,1},{1,0},{2,3},{3,2},{4,5},{5,4},{6,7},{7,6},{8,9},{9,8},{10,11... | collective-permute-start | bytes 2359304 | tf_op jit(solution)/shard_map/ppermute | solution.py:308
  84.8 1.1 %copy-start.13 = (f32[4,384,128]{2,1,0:T(8,128)}, f32[4,384,128]{2,1,0:T(8,128)S(1)}, u32[]{:S(2)}) copy-start(f32[4,384,128]{2,1,0:T(8,128)S(1)} %collective-permute-done.8.refs_1_) | copy-start | bytes 2359300
  85.9 0.9 copy-start.14
where the time goes:
time: 103 us; the launch traced here: 102 us
  waiting for transfers between devices  41.6 us (40%)
  Pallas kernels  27.2 us (26%)
  starting transfers between devices  22.5 us (22%)
  local copies, waits for them, and re-layouts  9.9 us (10%)
    ppermute x1, waiting for transfers between devices, on_device(): edge = lax.ppermute(jnp.stack([b[0], b[planes - 1]]), 'px', swap)  15.2 us
    pallas_call x2, Pallas kernels, line_terms(): pl.pallas_call(kernel, out_shape=[jax.ShapeDtypeStruct(b.shape, f32), jax...  12.7 us
    all_to_all x1, starting transfers between devices, on_device(): sent = exchange(b.reshape(count_i, share, width))  11.2 us
    unnamed x32, local copies, waits for them, and re-layouts  9.72 us
    ppermute x1, waiting for transfers between devices, on_device(): far_0 = lax.ppermute(onward_half, 'pz', onward)  8.58 us
    all_to_all x1, waiting for transfers between devices, on_device(): sent = exchange(b.reshape(count_i, share, width))  6.24 us
    pallas_call x1, Pallas kernels, on_device(): pl.pallas_call(functools.partial(wall_kernel, dx), out_shape=[jax.ShapeDt...  5.79 us
    all_to_all x1, waiting for transfers between devices, on_device(): time_term = exchange(applied).reshape(planes, rows, width)  5.5 us
  transfers between devices with their start and end apart: 12, of which 8 were waited for; matrix products, arithmetic and copies ran while one was open for 1% of the time, Pallas kernels for 23%

commit v1 on v0

--- a/solution.py
+++ b/solution.py
@@ -111,13 +111,18 @@
     token_ref[...] = jnp.zeros_like(token_ref)
 
 
-def halves_kernel(before_ref, after_ref, onward_ref, return_ref, sems):
+def halves_kernel(before_ref, after_ref, onward_ref, return_ref, held, in_sems, out_sems):
     half = onward_ref.shape[0]
-    copies = [pltpu.make_async_copy(before_ref.at[k], onward_ref.at[k], sems.at[0, k]) for k in range(half)]
-    copies += [pltpu.make_async_copy(after_ref.at[half + k], return_ref.at[k], sems.at[1, k]) for k in range(half)]
-    for copy in copies:
+    planes = [(before_ref.at[k], onward_ref.at[k]) for k in range(half)]
+    planes += [(after_ref.at[half + k], return_ref.at[k]) for k in range(half)]
+    come = [pltpu.make_async_copy(x, held.at[k], in_sems.at[k]) for k, (x, _) in enumerate(planes)]
+    go = [pltpu.make_async_copy(held.at[k], y, out_sems.at[k]) for k, (_, y) in enumerate(planes)]
+    for copy in come:
         copy.start()
-    for copy in copies:
+    for first, second in zip(come, go):
+        first.wait()
+        second.start()
+    for copy in go:
         copy.wait()
 
 
@@ -192,9 +197,9 @@
     in_parts(parts, [in_ref], [source], result, out_ref, in_sems, out_sems, work)
 
 
-def last_kernel(parts, time_ref, inv_ref, steps_ref, out_ref, steps, result, in_sems, out_sems):
-    work = LastPart(steps_ref.shape[0] // parts, steps, time_ref, inv_ref, result)
-    in_parts(parts, [steps_ref], [steps], result, out_ref, in_sems, out_sems, work)
+def last_kernel(parts, time_ref, inv_ref, steps_ref, out_ref, result, in_sems, out_sems):
+    work = LastPart(steps_ref.shape[0] // parts, steps_ref, time_ref, inv_ref, result)
+    in_parts(parts, [], [], result, out_ref, in_sems, out_sems, work)
 
 
 def on_device(stream_vel, normal_vel, span_vel, adjoint_buoy, adjoint_normal):
@@ -283,15 +288,15 @@
         out_shape=[jax.ShapeDtypeStruct((half, rows, width), f32)] * 2,
         in_specs=[anywhere] * 2,
         out_specs=[anywhere] * 2,
-        scratch_shapes=[pltpu.SemaphoreType.DMA((2, half))],
-        compiler_params=params(1),
+        scratch_shapes=[pltpu.VMEM(b.shape, f32)] + [pltpu.SemaphoreType.DMA((2 * half,))] * 2,
+        compiler_params=params(8),
         cost_estimate=pl.CostEstimate(flops=0, bytes_accessed=b.size * 8, transcendentals=0),
         name="halves",
     )(before, after)
     far_0 = lax.ppermute(onward_half, "pz", onward)
     far_1 = lax.ppermute(return_half, "pz", return_)
 
-    parts = 4
+    parts = 8
     applied = pl.pallas_call(
         functools.partial(time_kernel, weights, parts),
         out_shape=jax.ShapeDtypeStruct(sent.shape, f32),
@@ -333,11 +338,11 @@
     out = pl.pallas_call(
         functools.partial(last_kernel, planes),
         out_shape=jax.ShapeDtypeStruct(b.shape, f32),
-        in_specs=[pl.BlockSpec(memory_space=pltpu.VMEM)] * 2 + [in_memory],
+        in_specs=[pl.BlockSpec(memory_space=pltpu.VMEM)] * 3,
         out_specs=in_memory,
-        scratch_shapes=[pltpu.VMEM(b.shape, f32)] * 2
+        scratch_shapes=[pltpu.VMEM(b.shape, f32)]
         + [pltpu.SemaphoreType.DMA((1, planes)), pltpu.SemaphoreType.DMA((planes,))],
-        compiler_params=params(58),
+        compiler_params=params(8),
         cost_estimate=pl.CostEstimate(flops=2 * b.size, bytes_accessed=b.size * 16, transcendentals=0),
         name="last",
     )(time_term, inv, steps)

time: 103 us -> 103 us (level)
  local copies, waits for them, and re-layouts: 9.9 us -> 12.7 us
  Pallas kernels: 27.2 us -> 25.1 us
    pallas_call x1, Pallas kernels: 4.2 us -> 1.3 us  [on_device(): pl.pallas_call(functools.partial(last_kernel, planes), out_shape=jax.Shap...]
    unnamed x32 -> x36, local copies, waits for them, and re-layouts: 9.72 us -> 12.5 us
    all_to_all x1, waiting for transfers between devices: 5.5 us -> 4.28 us  [on_device(): time_term = exchange(applied).reshape(planes, rows, width)]
    ppermute x1, waiting for transfers between devices: 8.58 us -> 9.63 us  [on_device(): far_0 = lax.ppermute(onward_half, 'pz', onward)]
where the time goes in v1:
time: 103 us; the launch traced here: 102 us
  waiting for transfers between devices  40.6 us (39%)
  Pallas kernels  25.1 us (24%)
  starting transfers between devices  22.5 us (22%)
  local copies, waits for them, and re-layouts  12.7 us (12%)
    ppermute x1, waiting for transfers between devices, on_device(): edge = lax.ppermute(jnp.stack([b[0], b[planes - 1]]), 'px', swap)  15.2 us
    pallas_call x2, Pallas kernels, line_terms(): pl.pallas_call(kernel, out_shape=[jax.ShapeDtypeStruct(b.shape, f32), jax...  12.7 us
    unnamed x36, local copies, waits for them, and re-layouts  12.5 us
    all_to_all x1, starting transfers between devices, on_device(): sent = exchange(b.reshape(count_i, share, width))  11.2 us
    ppermute x1, waiting for transfers between devices, on_device(): far_0 = lax.ppermute(onward_half, 'pz', onward)  9.63 us
    all_to_all x1, waiting for transfers between devices, on_device(): sent = exchange(b.reshape(count_i, share, width))  6.29 us
    pallas_call x1, Pallas kernels, on_device(): pl.pallas_call(functools.partial(wall_kernel, dx), out_shape=[jax.ShapeDt...  5.79 us
    all_to_all x1, starting transfers between devices, on_device(): time_term = exchange(applied).reshape(planes, rows, width)  5.35 us
  transfers between devices with their start and end apart: 12, of which 8 were waited for; matrix products, arithmetic and copies ran while one was open for 1% of the time, Pallas kernels for 23%

profile of v1, /device:TPU:56, one launch (start us, length us, event | category | flops | bytes accessed | tf_op | source)
XLA Modules:
  0.0 101.9 jit_solution(7578479535562133028)
XLA Ops:
  0.0 11.2 %all-to-all-start = ((f32[16,192,128]{2,1,0:T(8,128)}), f32[16,192,128]{2,1,0:T(8,128)}, u32[]{:S(2)}, u32[]{:S(2)}) async-start(f32[16,192,128]{2,1,0:T(8,128)} %bitcast.13), calls=%async_computation | async-start | bytes 3145728 | tf_op jit(solution)/shard_map/all_to_all | solution.py:237
  11.6 1.8 %collective-permute-start.3 = (f32[8,384,128]{2,1,0:T(8,128)S(1)}, f32[8,384,128]{2,1,0:T(8,128)}, u32[]{:S(2)}, u32[]{:S(2)}) collective-permute-start(f32[8,384,128]{2,1,0:T(8,128)S(1)} %bitcast.16), channel_id=1, source_target_pairs={{2,0},{3,1},{4,2},{5,3},{6,4},{7,5},{0,6},{1,7},{10,8},{11,9},{12,... | collective-permute-start | bytes 4718600 | tf_op jit(solution)/shard_map/ppermute | solution.py:245
  13.5 0.8 pad_maximum_fusion
  14.2 0.6 collective-permute-start
  14.8 15.2 %collective-permute-done.edge_ref = f32[2,384,128]{2,1,0:T(8,128)S(1)} collective-permute-done((f32[2,384,128]{2,1,0:T(8,128)}, f32[2,384,128]{2,1,0:T(8,128)S(1)}, u32[]{:S(2)}, u32[]{:S(2)}) %collective-permute-start) | collective-permute-done | bytes 393248 | tf_op jit(solution)/shard_map/ppermute | solution.py:250
  30.2 1.5 %copy-done.4 = bf16[768,1152]{1,0:T(8,128)(2,1)S(1)} copy-done((bf16[768,1152]{1,0:T(8,128)(2,1)S(1)}, bf16[768,1152]{1,0:T(8,128)(2,1)}, u32[]{:S(2)}) %copy-start.4) | copy-done | bytes 1769496
  31.7 1.4 %copy-done.9 = f32[1,8,384,128]{3,2,1,0:T(8,128)S(1)} copy-done((f32[1,8,384,128]{3,2,1,0:T(8,128)S(1)}, f32[1,8,384,128]{3,2,1,0:T(8,128)}, u32[]{:S(2)}) %copy-start.9) | copy-done | bytes 1572888
  33.1 1.1 %copy-done.11 = bf16[1,8,384,128]{3,2,1,0:T(8,128)(2,1)S(1)} copy-done((bf16[1,8,384,128]{3,2,1,0:T(8,128)(2,1)S(1)}, bf16[1,8,384,128]{3,2,1,0:T(8,128)(2,1)}, u32[]{:S(2)}) %copy-start.11) | copy-done | bytes 786456
  34.2 1.1 %copy-done.12 = bf16[2,768,256]{2,1,0:T(8,128)(2,1)S(1)} copy-done((bf16[2,768,256]{2,1,0:T(8,128)(2,1)S(1)}, bf16[2,768,256]{2,1,0:T(8,128)(2,1)}, u32[]{:S(2)}) %copy-start.12) | copy-done | bytes 786456
  35.4 5.8 %wall_terms.1 = (f32[8,384,128]{2,1,0:T(8,128)S(1)}, f32[8,384,128]{2,1,0:T(8,128)S(1)}, f32[8,128]{1,0:T(8,128)S(1)}) custom-call(s32[1]{0:T(128)} %bitcast.1.core_ref, bf16[768,1152]{1,0:T(8,128)(2,1)S(1)} %copy-done.4, bf16[2,768,256]{2,1,0:T(8,128)(2,1)S(1)} %copy-done.12, f32[2,384,128]{2,1,0:T(8,128)S(1)} %jit_solution_.3.scale_ref, ...), custom_call_target="tpu_custom_call" | custom-call | flops 2415919104 | bytes 11010048 | tf_op jit(solution)/shard_map/wall_terms/pallas_call | solution.py:261
  41.2 1.2 %copy-done.5 = f32[8,384,128]{2,1,0:T(8,128)} copy-done((f32[8,384,128]{2,1,0:T(8,128)}, f32[8,384,128]{2,1,0:T(8,128)S(1)}, u32[]{:S(2)}) %copy-start.5) | copy-done | bytes 1572888
  42.3 1.2 %copy-done.6 = f32[8,384,128]{2,1,0:T(8,128)} copy-done((f32[8,384,128]{2,1,0:T(8,128)}, f32[8,384,128]{2,1,0:T(8,128)S(1)}, u32[]{:S(2)}) %copy-start.6) | copy-done | bytes 1572888
  43.5 0.6 copy-done.14
  44.1 6.3 %all-to-all-done.in_ref = f32[16,192,128]{2,1,0:T(8,128)} async-done(((f32[16,192,128]{2,1,0:T(8,128)}), f32[16,192,128]{2,1,0:T(8,128)}, u32[]{:S(2)}, u32[]{:S(2)}) %all-to-all-start) | async-done | bytes 1572896 | tf_op jit(solution)/shard_map/all_to_all | solution.py:237
  50.4 2.9 %time_term.1 = f32[16,192,128]{2,1,0:T(8,128)} custom-call(f32[16,192,128]{2,1,0:T(8,128)} %all-to-all-done.in_ref, f32[8,128]{1,0:T(8,128)} %copy-done.14), custom_call_target="tpu_custom_call" | custom-call | flops 6291456 | bytes 3145728 | tf_op jit(solution)/shard_map/time_term/pallas_call | solution.py:300
  53.4 5.3 %all-to-all-start.1 = ((f32[16,192,128]{2,1,0:T(8,128)}), f32[16,192,128]{2,1,0:T(8,128)S(1)}, u32[]{:S(2)}, u32[]{:S(2)}) async-start(f32[16,192,128]{2,1,0:T(8,128)} %time_term.1), calls=%async_computation.1 | async-start | bytes 3145728 | tf_op jit(solution)/shard_map/all_to_all | solution.py:311
  59.3 2.4 %halves.1 = (f32[4,384,128]{2,1,0:T(8,128)}, f32[4,384,128]{2,1,0:T(8,128)}) custom-call(f32[8,384,128]{2,1,0:T(8,128)} %collective-permute-done.2.before_ref.refs_0_, f32[8,384,128]{2,1,0:T(8,128)} %collective-permute-done.3.after_ref.refs_2_), custom_call_target="tpu_custom_call" | custom-call | bytes 3145728 | tf_op jit(solution)/shard_map/halves/pallas_call | solution.py:286
  62.0 1.8 %collective-permute-start.5 = (f32[4,384,128]{2,1,0:T(8,128)}, f32[4,384,128]{2,1,0:T(8,128)S(1)}, u32[]{:S(2)}, u32[]{:S(2)}) collective-permute-start(f32[4,384,128]{2,1,0:T(8,128)} %get-tuple-element.18), channel_id=1, source_target_pairs={{2,0},{3,1},{4,2},{5,3},{6,4},{7,5},{0,6},{1,7},{10,8},{11,9},{12,... | collective-permute-start | bytes 2359304 | tf_op jit(solution)/shard_map/ppermute | solution.py:297
  63.8 1.0 %collective-permute-done.7.refs_3_ = f32[8,384,128]{2,1,0:T(8,128)} collective-permute-done((f32[8,384,128]{2,1,0:T(8,128)}, f32[8,384,128]{2,1,0:T(8,128)}, u32[]{:S(2)}, u32[]{:S(2)}) %collective-permute-start.7) | collective-permute-done | bytes 1572896 | tf_op jit(solution)/shard_map/ppermute | solution.py:313
  64.8 7.1 %early_terms.1 = (f32[8,384,128]{2,1,0:T(8,128)}, f32[8,128]{1,0:T(8,128)}) custom-call(s32[1]{0:T(128)} %bitcast.1.core_ref, bf16[2,1536,256]{2,1,0:T(8,128)(2,1)} %constant.28.clone.table_ref, f32[8,384,128]{2,1,0:T(8,128)} %collective-permute-done.2.before_ref.refs_0_, f32[8,384,128]{2,1,0:T(8,128)} %collective-permute-done.6.refs_1_, ...), custom_call_target="tpu_custom_call" | custom-call | flops 2415919104 | bytes 11010048 | tf_op jit(solution)/shard_map/early_terms/pallas_call | solution.py:318
  71.9 9.6 %collective-permute-done.4.refs_0_ = f32[4,384,128]{2,1,0:T(8,128)S(1)} collective-permute-done((f32[4,384,128]{2,1,0:T(8,128)}, f32[4,384,128]{2,1,0:T(8,128)S(1)}, u32[]{:S(2)}, u32[]{:S(2)}) %collective-permute-start.4) | collective-permute-done | bytes 786464 | tf_op jit(solution)/shard_map/ppermute | solution.py:296
  81.5 1.3 %collective-permute-done.5.refs_1_ = f32[4,384,128]{2,1,0:T(8,128)S(1)} collective-permute-done((f32[4,384,128]{2,1,0:T(8,128)}, f32[4,384,128]{2,1,0:T(8,128)S(1)}, u32[]{:S(2)}, u32[]{:S(2)}) %collective-permute-start.5) | collective-permute-done | bytes 786464 | tf_op jit(solution)/shard_map/ppermute | solution.py:297
  82.8 0.7 copy-done.13
  83.5 0.5 collective-permute-start.9
  84.0 1.8 %collective-permute-done.8.refs_1_ = f32[4,384,128]{2,1,0:T(8,128)S(1)} collective-permute-done((f32[4,384,128]{2,1,0:T(8,128)S(1)}, f32[4,384,128]{2,1,0:T(8,128)S(1)}, u32[]{:S(2)}, u32[]{:S(2)}) %collective-permute-start.8) | collective-permute-done | bytes 786464 | tf_op jit(solution)/shard_map/ppermute | solution.py:313
  85.8 1.1 %collective-permute-done.9.refs_3_ = f32[4,384,128]{2,1,0:T(8,128)S(1)} collective-permute-done((f32[4,384,128]{2,1,0:T(8,128)S(1)}, f32[4,384,128]{2,1,0:T(8,128)S(1)}, u32[]{:S(2)}, u32[]{:S(2)}) %collective-permute-start.9) | collective-permute-done | bytes 786464 | tf_op jit(solution)/shard_map/ppermute | solution.py:313
  86.9 0.9 copy-done.16
  87.8 5.6 %late_terms.1 = (f32[8,384,128]{2,1,0:T(8,128)}, f32[8,128]{1,0:T(8,128)}) custom-call(s32[1]{0:T(128)} %bitcast.1.core_ref, bf16[2,768,256]{2,1,0:T(8,128)(2,1)} %constant.29.clone.table_ref, f32[4,384,128]{2,1,0:T(8,128)} %copy-done.2, f32[4,384,128]{2,1,0:T(8,128)} %copy-done.15, f32[4,384,128]{2,1,0:T(8,128)} %copy-done.3, f32[4,384,128]{2,1,0:T(8,128)} %copy-done.16, ...), custom_call_target="tpu_custom_call" | custom-call | flops 1207959552 | bytes 7864320 | tf_op jit(solution)/shard_map/late_terms/pallas_call | solution.py:318
  93.5 4.3 %all-to-all-done.1 = f32[16,192,128]{2,1,0:T(8,128)S(1)} async-done(((f32[16,192,128]{2,1,0:T(8,128)}), f32[16,192,128]{2,1,0:T(8,128)S(1)}, u32[]{:S(2)}, u32[]{:S(2)}) %all-to-all-start.1) | async-done | bytes 1572896 | tf_op jit(solution)/shard_map/all_to_all | solution.py:311
  97.8 1.4 %copy-done.7 = f32[8,384,128]{2,1,0:T(8,128)S(1)} copy-done((f32[8,384,128]{2,1,0:T(8,128)S(1)}, f32[8,384,128]{2,1,0:T(8,128)}, u32[]{:S(2)}) %copy-start.7) | copy-done | bytes 1572888
  99.2 1.4 %copy-done.8 = f32[8,384,128]{2,1,0:T(8,128)S(1)} copy-done((f32[8,384,128]{2,1,0:T(8,128)S(1)}, f32[8,384,128]{2,1,0:T(8,128)}, u32[]{:S(2)}) %copy-start.8) | copy-done | bytes 1572888
  100.6 1.3 %last.1 = f32[8,384,128]{2,1,0:T(8,128)} custom-call(f32[8,384,128]{2,1,0:T(8,128)S(1)} %bitcast.21, f32[8,384,128]{2,1,0:T(8,128)S(1)} %copy-done.7, f32[8,384,128]{2,1,0:T(8,128)S(1)} %copy-done.8), custom_call_target="tpu_custom_call" | custom-call | flops 786432 | bytes 6291456 | tf_op jit(solution)/shard_map/last/pallas_call | solution.py:338
  (38 shorter events, 1.5 us)
Async XLA Ops:
  0.0 11.2 %copy-start = (f32[1,8,384,128]{3,2,1,0:T(8,128)S(1)}, f32[1,8,384,128]{3,2,1,0:T(8,128)}, u32[]{:S(2)}) copy-start(f32[1,8,384,128]{3,2,1,0:T(8,128)} %param.13) | copy-start | bytes 4718596
  0.0 50.4 %all-to-all-start = ((f32[16,192,128]{2,1,0:T(8,128)}), f32[16,192,128]{2,1,0:T(8,128)}, u32[]{:S(2)}, u32[]{:S(2)}) async-start(f32[16,192,128]{2,1,0:T(8,128)} %bitcast.13), calls=%async_computation | async-start | bytes 3145728 | tf_op jit(solution)/shard_map/all_to_all | solution.py:237
  11.2 18.8 %copy-start.17 = (f32[2,384]{1,0:T(2,128)S(1)}, f32[2,384]{1,0:T(2,128)}, u32[]{:S(2)}) copy-start(f32[2,384]{1,0:T(2,128)} %constant.31.clone) | copy-start | bytes 9220
  11.2 19.0 %copy-start.1 = (bf16[1,8,384,128]{3,2,1,0:T(8,128)(2,1)S(1)}, bf16[1,8,384,128]{3,2,1,0:T(8,128)(2,1)}, u32[]{:S(2)}) copy-start(bf16[1,8,384,128]{3,2,1,0:T(8,128)(2,1)} %param.10) | copy-start | bytes 2359300
  11.2 19.0 %copy-start.10 = (bf16[1,8,384,128]{3,2,1,0:T(8,128)(2,1)S(1)}, bf16[1,8,384,128]{3,2,1,0:T(8,128)(2,1)}, u32[]{:S(2)}) copy-start(bf16[1,8,384,128]{3,2,1,0:T(8,128)(2,1)} %param.11) | copy-start | bytes 2359300
  11.2 18.8 %collective-permute-start.1 = (f32[8,384,128]{2,1,0:T(8,128)S(1)}, f32[8,384,128]{2,1,0:T(8,128)}, u32[]{:S(2)}, u32[]{:S(2)}) collective-permute-start(f32[8,384,128]{2,1,0:T(8,128)S(1)} %bitcast.14), channel_id=1, source_target_pairs={{0,1},{1,0},{2,3},{3,2},{4,5},{5,4},{6,7},{7,6},{8,9},{9,8},{10,11... | collective-permute-start | bytes 4718600 | tf_op jit(solution)/shard_map/ppermute | solution.py:246
  11.3 47.4 %collective-permute-start.2 = (f32[8,384,128]{2,1,0:T(8,128)S(1)}, f32[8,384,128]{2,1,0:T(8,128)}, u32[]{:S(2)}, u32[]{:S(2)}) collective-permute-start(f32[8,384,128]{2,1,0:T(8,128)S(1)} %bitcast.15), channel_id=1, source_target_pairs={{0,2},{1,3},{2,4},{3,5},{4,6},{5,7},{6,0},{7,1},{8,10},{9,11},{10,... | collective-permute-start | bytes 4718600 | tf_op jit(solution)/shard_map/ppermute | solution.py:244
  11.6 47.2 %collective-permute-start.3 = (f32[8,384,128]{2,1,0:T(8,128)S(1)}, f32[8,384,128]{2,1,0:T(8,128)}, u32[]{:S(2)}, u32[]{:S(2)}) collective-permute-start(f32[8,384,128]{2,1,0:T(8,128)S(1)} %bitcast.16), channel_id=1, source_target_pairs={{2,0},{3,1},{4,2},{5,3},{6,4},{7,5},{0,6},{1,7},{10,8},{11,9},{12,... | collective-permute-start | bytes 4718600 | tf_op jit(solution)/shard_map/ppermute | solution.py:245
  14.2 15.8 %collective-permute-start = (f32[2,384,128]{2,1,0:T(8,128)}, f32[2,384,128]{2,1,0:T(8,128)S(1)}, u32[]{:S(2)}, u32[]{:S(2)}) collective-permute-start(f32[2,384,128]{2,1,0:T(8,128)} %pad_maximum_fusion), channel_id=1, source_target_pairs={{0,8},{8,0},{1,9},{9,1},{2,10},{10,2},{3,11},{11,3},{4,12},{12,4},... | collective-permute-start | bytes 1179656 | tf_op jit(solution)/shard_map/ppermute | solution.py:250
  30.2 1.5 %copy-start.4 = (bf16[768,1152]{1,0:T(8,128)(2,1)S(1)}, bf16[768,1152]{1,0:T(8,128)(2,1)}, u32[]{:S(2)}) copy-start(bf16[768,1152]{1,0:T(8,128)(2,1)} %constant.30.clone.wall_ref) | copy-start | bytes 5308420
  31.7 1.4 %copy-start.9 = (f32[1,8,384,128]{3,2,1,0:T(8,128)S(1)}, f32[1,8,384,128]{3,2,1,0:T(8,128)}, u32[]{:S(2)}) copy-start(f32[1,8,384,128]{3,2,1,0:T(8,128)} %param.14) | copy-start | bytes 4718596
  33.1 1.1 %copy-start.11 = (bf16[1,8,384,128]{3,2,1,0:T(8,128)(2,1)S(1)}, bf16[1,8,384,128]{3,2,1,0:T(8,128)(2,1)}, u32[]{:S(2)}) copy-start(bf16[1,8,384,128]{3,2,1,0:T(8,128)(2,1)} %param.12) | copy-start | bytes 2359300
  34.2 1.1 %copy-start.12 = (bf16[2,768,256]{2,1,0:T(8,128)(2,1)S(1)}, bf16[2,768,256]{2,1,0:T(8,128)(2,1)}, u32[]{:S(2)}) copy-start(bf16[2,768,256]{2,1,0:T(8,128)(2,1)} %constant.27.clone.line_ref) | copy-start | bytes 2359300
  41.2 1.2 %copy-start.5 = (f32[8,384,128]{2,1,0:T(8,128)}, f32[8,384,128]{2,1,0:T(8,128)S(1)}, u32[]{:S(2)}) copy-start(f32[8,384,128]{2,1,0:T(8,128)S(1)} %get-tuple-element.19.refs_5_) | copy-start | bytes 4718596
  42.3 1.2 %copy-start.6 = (f32[8,384,128]{2,1,0:T(8,128)}, f32[8,384,128]{2,1,0:T(8,128)S(1)}, u32[]{:S(2)}) copy-start(f32[8,384,128]{2,1,0:T(8,128)S(1)} %get-tuple-element.16.inv_ref) | copy-start | bytes 4718596
  43.5 0.6 copy-start.14
  53.4 44.4 %all-to-all-start.1 = ((f32[16,192,128]{2,1,0:T(8,128)}), f32[16,192,128]{2,1,0:T(8,128)S(1)}, u32[]{:S(2)}, u32[]{:S(2)}) async-start(f32[16,192,128]{2,1,0:T(8,128)} %time_term.1), calls=%async_computation.1 | async-start | bytes 3145728 | tf_op jit(solution)/shard_map/all_to_all | solution.py:311
  58.7 5.1 %collective-permute-start.6 = (f32[8,384,128]{2,1,0:T(8,128)}, f32[8,384,128]{2,1,0:T(8,128)}, u32[]{:S(2)}, u32[]{:S(2)}) collective-permute-start(f32[8,384,128]{2,1,0:T(8,128)} %collective-permute-done.2.before_ref.refs_0_), channel_id=1, source_target_pairs={{0,1},{1,0},{2,3},{3,2},{4,5},{5,4},{6,7},{7,6},{8,9},{9,8},{10,11... | collective-permute-start | bytes 4718600 | tf_op jit(solution)/shard_map/ppermute | solution.py:313
  58.8 6.0 %collective-permute-start.7 = (f32[8,384,128]{2,1,0:T(8,128)}, f32[8,384,128]{2,1,0:T(8,128)}, u32[]{:S(2)}, u32[]{:S(2)}) collective-permute-start(f32[8,384,128]{2,1,0:T(8,128)} %collective-permute-done.3.after_ref.refs_2_), channel_id=1, source_target_pairs={{0,1},{1,0},{2,3},{3,2},{4,5},{5,4},{6,7},{7,6},{8,9},{9,8},{10,11... | collective-permute-start | bytes 4718600 | tf_op jit(solution)/shard_map/ppermute | solution.py:313
  61.7 19.8 %collective-permute-start.4 = (f32[4,384,128]{2,1,0:T(8,128)}, f32[4,384,128]{2,1,0:T(8,128)S(1)}, u32[]{:S(2)}, u32[]{:S(2)}) collective-permute-start(f32[4,384,128]{2,1,0:T(8,128)} %get-tuple-element.17), channel_id=1, source_target_pairs={{0,2},{1,3},{2,4},{3,5},{4,6},{5,7},{6,0},{7,1},{8,10},{9,11},{10,... | collective-permute-start | bytes 2359304 | tf_op jit(solution)/shard_map/ppermute | solution.py:296
  62.0 20.8 %collective-permute-start.5 = (f32[4,384,128]{2,1,0:T(8,128)}, f32[4,384,128]{2,1,0:T(8,128)S(1)}, u32[]{:S(2)}, u32[]{:S(2)}) collective-permute-start(f32[4,384,128]{2,1,0:T(8,128)} %get-tuple-element.18), channel_id=1, source_target_pairs={{2,0},{3,1},{4,2},{5,3},{6,4},{7,5},{0,6},{1,7},{10,8},{11,9},{12,... | collective-permute-start | bytes 2359304 | tf_op jit(solution)/shard_map/ppermute | solution.py:297
  82.8 0.7 copy-start.13
  83.5 4.4 %copy-start.2 = (f32[4,384,128]{2,1,0:T(8,128)}, f32[4,384,128]{2,1,0:T(8,128)S(1)}, u32[]{:S(2)}) copy-start(f32[4,384,128]{2,1,0:T(8,128)S(1)} %get-tuple-element.21.refs_0_) | copy-start | bytes 2359300
  83.5 4.4 %copy-start.3 = (f32[4,384,128]{2,1,0:T(8,128)}, f32[4,384,128]{2,1,0:T(8,128)S(1)}, u32[]{:S(2)}) copy-start(f32[4,384,128]{2,1,0:T(8,128)S(1)} %get-tuple-element.22.refs_2_) | copy-start | bytes 2359300
  83.5 2.3 %collective-permute-start.8 = (f32[4,384,128]{2,1,0:T(8,128)S(1)}, f32[4,384,128]{2,1,0:T(8,128)S(1)}, u32[]{:S(2)}, u32[]{:S(2)}) collective-permute-start(f32[4,384,128]{2,1,0:T(8,128)S(1)} %get-tuple-element.21.refs_0_), channel_id=1, source_target_pairs={{0,1},{1,0},{2,3},{3,2},{4,5},{5,4},{6,7},{7,6},{8,9},{9,8},{10,11... | collective-permute-start | bytes 2359304 | tf_op jit(solution)/shard_map/ppermute | solution.py:313
  83.5 3.4 %collective-permute-start.9 = (f32[4,384,128]{2,1,0:T(8,128)S(1)}, f32[4,384,128]{2,1,0:T(8,128)S(1)}, u32[]{:S(2)}, u32[]{:S(2)}) collective-permute-start(f32[4,384,128]{2,1,0:T(8,128)S(1)} %get-tuple-element.22.refs_2_), channel_id=1, source_target_pairs={{0,1},{1,0},{2,3},{3,2},{4,5},{5,4},{6,7},{7,6},{8,9},{9,8},{10,11... | collective-permute-start | bytes 2359304 | tf_op jit(solution)/shard_map/ppermute | solution.py:313
  85.8 1.1 %copy-start.15 = (f32[4,384,128]{2,1,0:T(8,128)}, f32[4,384,128]{2,1,0:T(8,128)S(1)}, u32[]{:S(2)}) copy-start(f32[4,384,128]{2,1,0:T(8,128)S(1)} %collective-permute-done.8.refs_1_) | copy-start | bytes 2359300
  86.9 0.9 copy-start.16
  97.8 1.4 %copy-start.7 = (f32[8,384,128]{2,1,0:T(8,128)S(1)}, f32[8,384,128]{2,1,0:T(8,128)}, u32[]{:S(2)}) copy-start(f32[8,384,128]{2,1,0:T(8,128)} %copy-done.6) | copy-start | bytes 4718596
  99.2 1.4 %copy-start.8 = (f32[8,384,128]{2,1,0:T(8,128)S(1)}, f32[8,384,128]{2,1,0:T(8,128)}, u32[]{:S(2)}) copy-start(f32[8,384,128]{2,1,0:T(8,128)} %get-tuple-element.24.steps_ref) | copy-start | bytes 4718596

commit v2 on v1

--- a/solution.py
+++ b/solution.py
@@ -153,8 +153,8 @@
 
 
 class TimePart:
-    def __init__(self, weights, size, source, result):
-        self.weights, self.size, self.source, self.result = weights, size, source, result
+    def __init__(self, weights, order, size, source, result):
+        self.weights, self.order, self.size, self.source, self.result = weights, order, size, source, result
 
     def where(self, k):
         return (slice(None), pl.ds(k * self.size, self.size))
@@ -165,7 +165,7 @@
 
         def body(step, carry):
             rows = pl.ds(pl.multiple_of(k * self.size + step * 8, 8), 8)
-            b = [self.source[i, rows, :] for i in range(count)]
+            b = [self.source[self.order.index(i), rows, :] for i in range(count)]
             totals = [weights[half] * b[(i + half) % count] for i in range(count)]
             for i in range(half):
                 for d in range(1, half):
@@ -173,7 +173,7 @@
                     totals[i] = totals[i] + weights[d] * differ
                     totals[i + half] = totals[i + half] - weights[half - d] * differ
             for i in range(count):
-                self.result[i, rows, :] = totals[i]
+                self.result[self.order.index(i), rows, :] = totals[i]
             return carry
 
         lax.fori_loop(0, self.size // 8, body, 0)
@@ -191,9 +191,9 @@
         self.result[at] = (self.steps[at] - self.time[at]) * self.inv[at]
 
 
-def time_kernel(weights, parts, in_ref, *refs):
+def time_kernel(weights, order, parts, in_ref, *refs):
     out_ref, source, result, in_sems, out_sems = refs[-5:]
-    work = TimePart(weights, in_ref.shape[1] // parts, source, result)
+    work = TimePart(weights, order, in_ref.shape[1] // parts, source, result)
     in_parts(parts, [in_ref], [source], result, out_ref, in_sems, out_sems, work)
 
 
@@ -233,7 +233,11 @@
     b, u, v, w, n = (x[0] for x in (adjoint_buoy, stream_vel, normal_vel, span_vel, adjoint_normal))
 
     share = planes * rows // count_i
-    exchange = functools.partial(lax.all_to_all, axis_name="inst", split_axis=0, concat_axis=0, tiled=True)
+    turn = count_i // 2
+    order = [j * 3 % turn + side * turn for j in range(turn) for side in range(2)]
+    exchange = functools.partial(
+        lax.all_to_all, axis_name="inst", split_axis=0, concat_axis=0, axis_index_groups=[order], tiled=True
+    )
     sent = exchange(b.reshape(count_i, share, width))
 
     members = range(count_x)
@@ -298,7 +302,7 @@
 
     parts = 8
     applied = pl.pallas_call(
-        functools.partial(time_kernel, weights, parts),
+        functools.partial(time_kernel, weights, order, parts),
         out_shape=jax.ShapeDtypeStruct(sent.shape, f32),
         in_specs=[in_memory, anywhere],
         out_specs=in_memory,

time: 103 us -> 103 us (level)
  waiting for transfers between devices: 40.6 us -> 42.1 us
  starting transfers between devices: 22.5 us -> 21.3 us
    all_to_all x1, waiting for transfers between devices: 6.29 us -> 8.57 us  [on_device(): sent = exchange(b.reshape(count_i, share, width))]
    ppermute x1, waiting for transfers between devices: 15.2 us -> 14 us  [on_device(): edge = lax.ppermute(jnp.stack([b[0], b[planes - 1]]), 'px', swap)]
    all_to_all x1, starting transfers between devices: 5.35 us -> 4.19 us  [on_device(): time_term = exchange(applied).reshape(planes, rows, width)]
where the time goes in v2:
time: 103 us; the launch traced here: 102 us
  waiting for transfers between devices  42.1 us (41%)
  Pallas kernels  25.1 us (24%)
  starting transfers between devices  21.3 us (21%)
  local copies, waits for them, and re-layouts  12.7 us (12%)
    ppermute x1, waiting for transfers between devices, on_device(): edge = lax.ppermute(jnp.stack([b[0], b[planes - 1]]), 'px', swap)  14 us
    pallas_call x2, Pallas kernels, line_terms(): pl.pallas_call(kernel, out_shape=[jax.ShapeDtypeStruct(b.shape, f32), jax...  12.7 us
    unnamed x36, local copies, waits for them, and re-layouts  12.5 us
    all_to_all x1, starting transfers between devices, on_device(): sent = exchange(b.reshape(count_i, share, width))  11.2 us
    ppermute x1, waiting for transfers between devices, on_device(): far_0 = lax.ppermute(onward_half, 'pz', onward)  9.63 us
    all_to_all x1, waiting for transfers between devices, on_device(): sent = exchange(b.reshape(count_i, share, width))  8.57 us
    pallas_call x1, Pallas kernels, on_device(): pl.pallas_call(functools.partial(wall_kernel, dx), out_shape=[jax.ShapeDt...  5.79 us
    all_to_all x1, waiting for transfers between devices, on_device(): time_term = exchange(applied).reshape(planes, rows, width)  4.73 us
  transfers between devices with their start and end apart: 12, of which 8 were waited for; matrix products, arithmetic and copies ran while one was open for 1% of the time, Pallas kernels for 23%

profile of v2, /device:TPU:56, one launch (start us, length us, event | category | flops | bytes accessed | tf_op | source)
XLA Modules:
  0.0 102.2 jit_solution(10646369955949423310)
XLA Ops:
  0.0 11.2 %all-to-all-start = ((f32[16,192,128]{2,1,0:T(8,128)}), f32[16,192,128]{2,1,0:T(8,128)}, u32[]{:S(2)}, u32[]{:S(2)}) async-start(f32[16,192,128]{2,1,0:T(8,128)} %bitcast.13), calls=%async_computation | async-start | bytes 3145728 | tf_op jit(solution)/shard_map/all_to_all | solution.py:241
  11.6 1.8 %collective-permute-start.3 = (f32[8,384,128]{2,1,0:T(8,128)S(1)}, f32[8,384,128]{2,1,0:T(8,128)}, u32[]{:S(2)}, u32[]{:S(2)}) collective-permute-start(f32[8,384,128]{2,1,0:T(8,128)S(1)} %bitcast.16), channel_id=1, source_target_pairs={{2,0},{3,1},{4,2},{5,3},{6,4},{7,5},{0,6},{1,7},{10,8},{11,9},{12,... | collective-permute-start | bytes 4718600 | tf_op jit(solution)/shard_map/ppermute | solution.py:249
  13.5 0.8 pad_maximum_fusion
  14.2 0.6 collective-permute-start
  14.8 14.0 %collective-permute-done.edge_ref = f32[2,384,128]{2,1,0:T(8,128)S(1)} collective-permute-done((f32[2,384,128]{2,1,0:T(8,128)}, f32[2,384,128]{2,1,0:T(8,128)S(1)}, u32[]{:S(2)}, u32[]{:S(2)}) %collective-permute-start) | collective-permute-done | bytes 393248 | tf_op jit(solution)/shard_map/ppermute | solution.py:254
  29.0 1.5 %copy-done.4 = bf16[768,1152]{1,0:T(8,128)(2,1)S(1)} copy-done((bf16[768,1152]{1,0:T(8,128)(2,1)S(1)}, bf16[768,1152]{1,0:T(8,128)(2,1)}, u32[]{:S(2)}) %copy-start.4) | copy-done | bytes 1769496
  30.5 1.4 %copy-done.9 = f32[1,8,384,128]{3,2,1,0:T(8,128)S(1)} copy-done((f32[1,8,384,128]{3,2,1,0:T(8,128)S(1)}, f32[1,8,384,128]{3,2,1,0:T(8,128)}, u32[]{:S(2)}) %copy-start.9) | copy-done | bytes 1572888
  31.9 1.1 %copy-done.11 = bf16[1,8,384,128]{3,2,1,0:T(8,128)(2,1)S(1)} copy-done((bf16[1,8,384,128]{3,2,1,0:T(8,128)(2,1)S(1)}, bf16[1,8,384,128]{3,2,1,0:T(8,128)(2,1)}, u32[]{:S(2)}) %copy-start.11) | copy-done | bytes 786456
  33.0 1.1 %copy-done.12 = bf16[2,768,256]{2,1,0:T(8,128)(2,1)S(1)} copy-done((bf16[2,768,256]{2,1,0:T(8,128)(2,1)S(1)}, bf16[2,768,256]{2,1,0:T(8,128)(2,1)}, u32[]{:S(2)}) %copy-start.12) | copy-done | bytes 786456
  34.1 5.8 %wall_terms.1 = (f32[8,384,128]{2,1,0:T(8,128)S(1)}, f32[8,384,128]{2,1,0:T(8,128)S(1)}, f32[8,128]{1,0:T(8,128)S(1)}) custom-call(s32[1]{0:T(128)} %bitcast.1.core_ref, bf16[768,1152]{1,0:T(8,128)(2,1)S(1)} %copy-done.4, bf16[2,768,256]{2,1,0:T(8,128)(2,1)S(1)} %copy-done.12, f32[2,384,128]{2,1,0:T(8,128)S(1)} %jit_solution_.3.scale_ref, ...), custom_call_target="tpu_custom_call" | custom-call | flops 2415919104 | bytes 11010048 | tf_op jit(solution)/shard_map/wall_terms/pallas_call | solution.py:265
  40.0 1.2 %copy-done.5 = f32[8,384,128]{2,1,0:T(8,128)} copy-done((f32[8,384,128]{2,1,0:T(8,128)}, f32[8,384,128]{2,1,0:T(8,128)S(1)}, u32[]{:S(2)}) %copy-start.5) | copy-done | bytes 1572888
  41.1 1.2 %copy-done.6 = f32[8,384,128]{2,1,0:T(8,128)} copy-done((f32[8,384,128]{2,1,0:T(8,128)}, f32[8,384,128]{2,1,0:T(8,128)S(1)}, u32[]{:S(2)}) %copy-start.6) | copy-done | bytes 1572888
  42.3 0.6 copy-done.14
  42.9 8.6 %all-to-all-done.in_ref = f32[16,192,128]{2,1,0:T(8,128)} async-done(((f32[16,192,128]{2,1,0:T(8,128)}), f32[16,192,128]{2,1,0:T(8,128)}, u32[]{:S(2)}, u32[]{:S(2)}) %all-to-all-start) | async-done | bytes 1572896 | tf_op jit(solution)/shard_map/all_to_all | solution.py:241
  51.5 2.9 %time_term.1 = f32[16,192,128]{2,1,0:T(8,128)} custom-call(f32[16,192,128]{2,1,0:T(8,128)} %all-to-all-done.in_ref, f32[8,128]{1,0:T(8,128)} %copy-done.14), custom_call_target="tpu_custom_call" | custom-call | flops 6291456 | bytes 3145728 | tf_op jit(solution)/shard_map/time_term/pallas_call | solution.py:304
  54.4 4.2 %all-to-all-start.1 = ((f32[16,192,128]{2,1,0:T(8,128)}), f32[16,192,128]{2,1,0:T(8,128)S(1)}, u32[]{:S(2)}, u32[]{:S(2)}) async-start(f32[16,192,128]{2,1,0:T(8,128)} %time_term.1), calls=%async_computation.1 | async-start | bytes 3145728 | tf_op jit(solution)/shard_map/all_to_all | solution.py:315
  59.2 2.4 %halves.1 = (f32[4,384,128]{2,1,0:T(8,128)}, f32[4,384,128]{2,1,0:T(8,128)}) custom-call(f32[8,384,128]{2,1,0:T(8,128)} %collective-permute-done.2.before_ref.refs_0_, f32[8,384,128]{2,1,0:T(8,128)} %collective-permute-done.3.after_ref.refs_2_), custom_call_target="tpu_custom_call" | custom-call | bytes 3145728 | tf_op jit(solution)/shard_map/halves/pallas_call | solution.py:290
  61.9 1.8 %collective-permute-start.5 = (f32[4,384,128]{2,1,0:T(8,128)}, f32[4,384,128]{2,1,0:T(8,128)S(1)}, u32[]{:S(2)}, u32[]{:S(2)}) collective-permute-start(f32[4,384,128]{2,1,0:T(8,128)} %get-tuple-element.18), channel_id=1, source_target_pairs={{2,0},{3,1},{4,2},{5,3},{6,4},{7,5},{0,6},{1,7},{10,8},{11,9},{12,... | collective-permute-start | bytes 2359304 | tf_op jit(solution)/shard_map/ppermute | solution.py:301
  63.7 1.0 collective-permute-done.7.refs_3_
  64.7 7.1 %early_terms.1 = (f32[8,384,128]{2,1,0:T(8,128)}, f32[8,128]{1,0:T(8,128)}) custom-call(s32[1]{0:T(128)} %bitcast.1.core_ref, bf16[2,1536,256]{2,1,0:T(8,128)(2,1)} %constant.28.clone.table_ref, f32[8,384,128]{2,1,0:T(8,128)} %collective-permute-done.2.before_ref.refs_0_, f32[8,384,128]{2,1,0:T(8,128)} %collective-permute-done.6.refs_1_, ...), custom_call_target="tpu_custom_call" | custom-call | flops 2415919104 | bytes 11010048 | tf_op jit(solution)/shard_map/early_terms/pallas_call | solution.py:322
  71.8 9.6 %collective-permute-done.4.refs_0_ = f32[4,384,128]{2,1,0:T(8,128)S(1)} collective-permute-done((f32[4,384,128]{2,1,0:T(8,128)}, f32[4,384,128]{2,1,0:T(8,128)S(1)}, u32[]{:S(2)}, u32[]{:S(2)}) %collective-permute-start.4) | collective-permute-done | bytes 786464 | tf_op jit(solution)/shard_map/ppermute | solution.py:300
  81.4 1.3 %collective-permute-done.5.refs_1_ = f32[4,384,128]{2,1,0:T(8,128)S(1)} collective-permute-done((f32[4,384,128]{2,1,0:T(8,128)}, f32[4,384,128]{2,1,0:T(8,128)S(1)}, u32[]{:S(2)}, u32[]{:S(2)}) %collective-permute-start.5) | collective-permute-done | bytes 786464 | tf_op jit(solution)/shard_map/ppermute | solution.py:301
  82.7 0.7 copy-done.13
  83.4 0.5 collective-permute-start.9
  83.9 1.8 %collective-permute-done.8.refs_1_ = f32[4,384,128]{2,1,0:T(8,128)S(1)} collective-permute-done((f32[4,384,128]{2,1,0:T(8,128)S(1)}, f32[4,384,128]{2,1,0:T(8,128)S(1)}, u32[]{:S(2)}, u32[]{:S(2)}) %collective-permute-start.8) | collective-permute-done | bytes 786464 | tf_op jit(solution)/shard_map/ppermute | solution.py:317
  85.7 1.1 %collective-permute-done.9.refs_3_ = f32[4,384,128]{2,1,0:T(8,128)S(1)} collective-permute-done((f32[4,384,128]{2,1,0:T(8,128)S(1)}, f32[4,384,128]{2,1,0:T(8,128)S(1)}, u32[]{:S(2)}, u32[]{:S(2)}) %collective-permute-start.9) | collective-permute-done | bytes 786464 | tf_op jit(solution)/shard_map/ppermute | solution.py:317
  86.8 0.9 copy-done.16
  87.7 5.6 %late_terms.1 = (f32[8,384,128]{2,1,0:T(8,128)}, f32[8,128]{1,0:T(8,128)}) custom-call(s32[1]{0:T(128)} %bitcast.1.core_ref, bf16[2,768,256]{2,1,0:T(8,128)(2,1)} %constant.29.clone.table_ref, f32[4,384,128]{2,1,0:T(8,128)} %copy-done.2, f32[4,384,128]{2,1,0:T(8,128)} %copy-done.15, f32[4,384,128]{2,1,0:T(8,128)} %copy-done.3, f32[4,384,128]{2,1,0:T(8,128)} %copy-done.16, ...), custom_call_target="tpu_custom_call" | custom-call | flops 1207959552 | bytes 7864320 | tf_op jit(solution)/shard_map/late_terms/pallas_call | solution.py:322
  93.4 4.7 %all-to-all-done.1 = f32[16,192,128]{2,1,0:T(8,128)S(1)} async-done(((f32[16,192,128]{2,1,0:T(8,128)}), f32[16,192,128]{2,1,0:T(8,128)S(1)}, u32[]{:S(2)}, u32[]{:S(2)}) %all-to-all-start.1) | async-done | bytes 1572896 | tf_op jit(solution)/shard_map/all_to_all | solution.py:315
  98.1 1.4 %copy-done.7 = f32[8,384,128]{2,1,0:T(8,128)S(1)} copy-done((f32[8,384,128]{2,1,0:T(8,128)S(1)}, f32[8,384,128]{2,1,0:T(8,128)}, u32[]{:S(2)}) %copy-start.7) | copy-done | bytes 1572888
  99.5 1.4 %copy-done.8 = f32[8,384,128]{2,1,0:T(8,128)S(1)} copy-done((f32[8,384,128]{2,1,0:T(8,128)S(1)}, f32[8,384,128]{2,1,0:T(8,128)}, u32[]{:S(2)}) %copy-start.8) | copy-done | bytes 1572888
  100.9 1.3 %last.1 = f32[8,384,128]{2,1,0:T(8,128)} custom-call(f32[8,384,128]{2,1,0:T(8,128)S(1)} %bitcast.21, f32[8,384,128]{2,1,0:T(8,128)S(1)} %copy-done.7, f32[8,384,128]{2,1,0:T(8,128)S(1)} %copy-done.8), custom_call_target="tpu_custom_call" | custom-call | flops 786432 | bytes 6291456 | tf_op jit(solution)/shard_map/last/pallas_call | solution.py:342
  (38 shorter events, 1.5 us)
Async XLA Ops:
  0.0 11.2 %copy-start = (f32[1,8,384,128]{3,2,1,0:T(8,128)S(1)}, f32[1,8,384,128]{3,2,1,0:T(8,128)}, u32[]{:S(2)}) copy-start(f32[1,8,384,128]{3,2,1,0:T(8,128)} %param.13) | copy-start | bytes 4718596
  0.0 51.5 %all-to-all-start = ((f32[16,192,128]{2,1,0:T(8,128)}), f32[16,192,128]{2,1,0:T(8,128)}, u32[]{:S(2)}, u32[]{:S(2)}) async-start(f32[16,192,128]{2,1,0:T(8,128)} %bitcast.13), calls=%async_computation | async-start | bytes 3145728 | tf_op jit(solution)/shard_map/all_to_all | solution.py:241
  11.2 17.6 %copy-start.17 = (f32[2,384]{1,0:T(2,128)S(1)}, f32[2,384]{1,0:T(2,128)}, u32[]{:S(2)}) copy-start(f32[2,384]{1,0:T(2,128)} %constant.31.clone) | copy-start | bytes 9220
  11.2 17.8 %copy-start.1 = (bf16[1,8,384,128]{3,2,1,0:T(8,128)(2,1)S(1)}, bf16[1,8,384,128]{3,2,1,0:T(8,128)(2,1)}, u32[]{:S(2)}) copy-start(bf16[1,8,384,128]{3,2,1,0:T(8,128)(2,1)} %param.10) | copy-start | bytes 2359300
  11.2 17.8 %copy-start.10 = (bf16[1,8,384,128]{3,2,1,0:T(8,128)(2,1)S(1)}, bf16[1,8,384,128]{3,2,1,0:T(8,128)(2,1)}, u32[]{:S(2)}) copy-start(bf16[1,8,384,128]{3,2,1,0:T(8,128)(2,1)} %param.11) | copy-start | bytes 2359300
  11.2 17.6 %collective-permute-start.1 = (f32[8,384,128]{2,1,0:T(8,128)S(1)}, f32[8,384,128]{2,1,0:T(8,128)}, u32[]{:S(2)}, u32[]{:S(2)}) collective-permute-start(f32[8,384,128]{2,1,0:T(8,128)S(1)} %bitcast.14), channel_id=1, source_target_pairs={{0,1},{1,0},{2,3},{3,2},{4,5},{5,4},{6,7},{7,6},{8,9},{9,8},{10,11... | collective-permute-start | bytes 4718600 | tf_op jit(solution)/shard_map/ppermute | solution.py:250
  11.3 47.3 %collective-permute-start.2 = (f32[8,384,128]{2,1,0:T(8,128)S(1)}, f32[8,384,128]{2,1,0:T(8,128)}, u32[]{:S(2)}, u32[]{:S(2)}) collective-permute-start(f32[8,384,128]{2,1,0:T(8,128)S(1)} %bitcast.15), channel_id=1, source_target_pairs={{0,2},{1,3},{2,4},{3,5},{4,6},{5,7},{6,0},{7,1},{8,10},{9,11},{10,... | collective-permute-start | bytes 4718600 | tf_op jit(solution)/shard_map/ppermute | solution.py:248
  11.6 47.1 %collective-permute-start.3 = (f32[8,384,128]{2,1,0:T(8,128)S(1)}, f32[8,384,128]{2,1,0:T(8,128)}, u32[]{:S(2)}, u32[]{:S(2)}) collective-permute-start(f32[8,384,128]{2,1,0:T(8,128)S(1)} %bitcast.16), channel_id=1, source_target_pairs={{2,0},{3,1},{4,2},{5,3},{6,4},{7,5},{0,6},{1,7},{10,8},{11,9},{12,... | collective-permute-start | bytes 4718600 | tf_op jit(solution)/shard_map/ppermute | solution.py:249
  14.2 14.6 %collective-permute-start = (f32[2,384,128]{2,1,0:T(8,128)}, f32[2,384,128]{2,1,0:T(8,128)S(1)}, u32[]{:S(2)}, u32[]{:S(2)}) collective-permute-start(f32[2,384,128]{2,1,0:T(8,128)} %pad_maximum_fusion), channel_id=1, source_target_pairs={{0,8},{8,0},{1,9},{9,1},{2,10},{10,2},{3,11},{11,3},{4,12},{12,4},... | collective-permute-start | bytes 1179656 | tf_op jit(solution)/shard_map/ppermute | solution.py:254
  29.0 1.5 %copy-start.4 = (bf16[768,1152]{1,0:T(8,128)(2,1)S(1)}, bf16[768,1152]{1,0:T(8,128)(2,1)}, u32[]{:S(2)}) copy-start(bf16[768,1152]{1,0:T(8,128)(2,1)} %constant.30.clone.wall_ref) | copy-start | bytes 5308420
  30.5 1.4 %copy-start.9 = (f32[1,8,384,128]{3,2,1,0:T(8,128)S(1)}, f32[1,8,384,128]{3,2,1,0:T(8,128)}, u32[]{:S(2)}) copy-start(f32[1,8,384,128]{3,2,1,0:T(8,128)} %param.14) | copy-start | bytes 4718596
  31.9 1.1 %copy-start.11 = (bf16[1,8,384,128]{3,2,1,0:T(8,128)(2,1)S(1)}, bf16[1,8,384,128]{3,2,1,0:T(8,128)(2,1)}, u32[]{:S(2)}) copy-start(bf16[1,8,384,128]{3,2,1,0:T(8,128)(2,1)} %param.12) | copy-start | bytes 2359300
  33.0 1.1 %copy-start.12 = (bf16[2,768,256]{2,1,0:T(8,128)(2,1)S(1)}, bf16[2,768,256]{2,1,0:T(8,128)(2,1)}, u32[]{:S(2)}) copy-start(bf16[2,768,256]{2,1,0:T(8,128)(2,1)} %constant.27.clone.line_ref) | copy-start | bytes 2359300
  39.9 1.2 %copy-start.5 = (f32[8,384,128]{2,1,0:T(8,128)}, f32[8,384,128]{2,1,0:T(8,128)S(1)}, u32[]{:S(2)}) copy-start(f32[8,384,128]{2,1,0:T(8,128)S(1)} %get-tuple-element.19.refs_5_) | copy-start | bytes 4718596
  41.1 1.2 %copy-start.6 = (f32[8,384,128]{2,1,0:T(8,128)}, f32[8,384,128]{2,1,0:T(8,128)S(1)}, u32[]{:S(2)}) copy-start(f32[8,384,128]{2,1,0:T(8,128)S(1)} %get-tuple-element.16.inv_ref) | copy-start | bytes 4718596
  42.3 0.6 copy-start.14
  54.4 43.7 %all-to-all-start.1 = ((f32[16,192,128]{2,1,0:T(8,128)}), f32[16,192,128]{2,1,0:T(8,128)S(1)}, u32[]{:S(2)}, u32[]{:S(2)}) async-start(f32[16,192,128]{2,1,0:T(8,128)} %time_term.1), calls=%async_computation.1 | async-start | bytes 3145728 | tf_op jit(solution)/shard_map/all_to_all | solution.py:315
  58.6 5.1 %collective-permute-start.6 = (f32[8,384,128]{2,1,0:T(8,128)}, f32[8,384,128]{2,1,0:T(8,128)}, u32[]{:S(2)}, u32[]{:S(2)}) collective-permute-start(f32[8,384,128]{2,1,0:T(8,128)} %collective-permute-done.2.before_ref.refs_0_), channel_id=1, source_target_pairs={{0,1},{1,0},{2,3},{3,2},{4,5},{5,4},{6,7},{7,6},{8,9},{9,8},{10,11... | collective-permute-start | bytes 4718600 | tf_op jit(solution)/shard_map/ppermute | solution.py:317
  58.7 6.0 %collective-permute-start.7 = (f32[8,384,128]{2,1,0:T(8,128)}, f32[8,384,128]{2,1,0:T(8,128)}, u32[]{:S(2)}, u32[]{:S(2)}) collective-permute-start(f32[8,384,128]{2,1,0:T(8,128)} %collective-permute-done.3.after_ref.refs_2_), channel_id=1, source_target_pairs={{0,1},{1,0},{2,3},{3,2},{4,5},{5,4},{6,7},{7,6},{8,9},{9,8},{10,11... | collective-permute-start | bytes 4718600 | tf_op jit(solution)/shard_map/ppermute | solution.py:317
  61.6 19.8 %collective-permute-start.4 = (f32[4,384,128]{2,1,0:T(8,128)}, f32[4,384,128]{2,1,0:T(8,128)S(1)}, u32[]{:S(2)}, u32[]{:S(2)}) collective-permute-start(f32[4,384,128]{2,1,0:T(8,128)} %get-tuple-element.17), channel_id=1, source_target_pairs={{0,2},{1,3},{2,4},{3,5},{4,6},{5,7},{6,0},{7,1},{8,10},{9,11},{10,... | collective-permute-start | bytes 2359304 | tf_op jit(solution)/shard_map/ppermute | solution.py:300
  61.9 20.8 %collective-permute-start.5 = (f32[4,384,128]{2,1,0:T(8,128)}, f32[4,384,128]{2,1,0:T(8,128)S(1)}, u32[]{:S(2)}, u32[]{:S(2)}) collective-permute-start(f32[4,384,128]{2,1,0:T(8,128)} %get-tuple-element.18), channel_id=1, source_target_pairs={{2,0},{3,1},{4,2},{5,3},{6,4},{7,5},{0,6},{1,7},{10,8},{11,9},{12,... | collective-permute-start | bytes 2359304 | tf_op jit(solution)/shard_map/ppermute | solution.py:301
  82.7 0.7 copy-start.13
  83.4 4.4 %copy-start.2 = (f32[4,384,128]{2,1,0:T(8,128)}, f32[4,384,128]{2,1,0:T(8,128)S(1)}, u32[]{:S(2)}) copy-start(f32[4,384,128]{2,1,0:T(8,128)S(1)} %get-tuple-element.21.refs_0_) | copy-start | bytes 2359300
  83.4 4.4 %copy-start.3 = (f32[4,384,128]{2,1,0:T(8,128)}, f32[4,384,128]{2,1,0:T(8,128)S(1)}, u32[]{:S(2)}) copy-start(f32[4,384,128]{2,1,0:T(8,128)S(1)} %get-tuple-element.22.refs_2_) | copy-start | bytes 2359300
  83.4 2.3 %collective-permute-start.8 = (f32[4,384,128]{2,1,0:T(8,128)S(1)}, f32[4,384,128]{2,1,0:T(8,128)S(1)}, u32[]{:S(2)}, u32[]{:S(2)}) collective-permute-start(f32[4,384,128]{2,1,0:T(8,128)S(1)} %get-tuple-element.21.refs_0_), channel_id=1, source_target_pairs={{0,1},{1,0},{2,3},{3,2},{4,5},{5,4},{6,7},{7,6},{8,9},{9,8},{10,11... | collective-permute-start | bytes 2359304 | tf_op jit(solution)/shard_map/ppermute | solution.py:317
  83.4 3.4 %collective-permute-start.9 = (f32[4,384,128]{2,1,0:T(8,128)S(1)}, f32[4,384,128]{2,1,0:T(8,128)S(1)}, u32[]{:S(2)}, u32[]{:S(2)}) collective-permute-start(f32[4,384,128]{2,1,0:T(8,128)S(1)} %get-tuple-element.22.refs_2_), channel_id=1, source_target_pairs={{0,1},{1,0},{2,3},{3,2},{4,5},{5,4},{6,7},{7,6},{8,9},{9,8},{10,11... | collective-permute-start | bytes 2359304 | tf_op jit(solution)/shard_map/ppermute | solution.py:317
  85.7 1.1 %copy-start.15 = (f32[4,384,128]{2,1,0:T(8,128)}, f32[4,384,128]{2,1,0:T(8,128)S(1)}, u32[]{:S(2)}) copy-start(f32[4,384,128]{2,1,0:T(8,128)S(1)} %collective-permute-done.8.refs_1_) | copy-start | bytes 2359300
  86.8 0.9 copy-start.16
  98.1 1.4 %copy-start.7 = (f32[8,384,128]{2,1,0:T(8,128)S(1)}, f32[8,384,128]{2,1,0:T(8,128)}, u32[]{:S(2)}) copy-start(f32[8,384,128]{2,1,0:T(8,128)} %copy-done.6) | copy-start | bytes 4718596
  99.5 1.4 %copy-start.8 = (f32[8,384,128]{2,1,0:T(8,128)S(1)}, f32[8,384,128]{2,1,0:T(8,128)}, u32[]{:S(2)}) copy-start(f32[8,384,128]{2,1,0:T(8,128)} %get-tuple-element.24.steps_ref) | copy-start | bytes 4718596

commit v3 on v1

--- a/solution.py
+++ b/solution.py
@@ -329,11 +329,11 @@
         )(core, *operands)
 
     operands = (early, *with_other(before), *with_other(after), u, part)
-    steps, token = line_terms(early_kernel, "early_terms", 2, 60, [table(early)] + [two] * 6, operands)
+    steps, token = line_terms(early_kernel, "early_terms", 2, 40, [table(early)] + [two] * 6, operands)
     far_0, far_1 = follow("follow_early", far_0, far_1, after=token)
     operands = (late, *with_other(far_0), *with_other(far_1), u, steps)
     specs = [table(late)] + [in_lower] * 2 + [in_upper] * 2 + [two] * 2
-    steps, _ = line_terms(functools.partial(late_kernel, half // pair), "late_terms", 1, 60, specs, operands)
+    steps, _ = line_terms(functools.partial(late_kernel, half // pair), "late_terms", 1, 40, specs, operands)
 
     out = pl.pallas_call(
         functools.partial(last_kernel, planes),

time: 103 us -> 103 us (level)
  waiting for transfers between devices: 40.6 us -> 45.7 us
  Pallas kernels: 25.1 us -> 22 us
  local copies, waits for them, and re-layouts: 12.7 us -> 10.8 us
    pallas_call x2, Pallas kernels: 12.7 us -> 7.19 us  [line_terms(): pl.pallas_call(kernel, out_shape=[jax.ShapeDtypeStruct(b.shape, f32), jax...]
    all_to_all x1, waiting for transfers between devices: 4.28 us -> 7.48 us  [on_device(): time_term = exchange(applied).reshape(planes, rows, width)]
    ppermute x1, waiting for transfers between devices: 9.63 us -> 12.5 us  [on_device(): far_0 = lax.ppermute(onward_half, 'pz', onward)]
    unnamed x36 -> x34, local copies, waits for them, and re-layouts: 12.5 us -> 10.6 us
    pallas_call x1, Pallas kernels: 1.3 us -> 2.7 us  [on_device(): pl.pallas_call(functools.partial(last_kernel, planes), out_shape=jax.Shap...]
  transfers between devices with their start and end apart: 12 -> 12, of which waited for: 8 -> 7; matrix products, arithmetic and copies ran while one was open for 1% -> 1% of each run, Pallas kernels for 23% -> 19%
where the time goes in v3:
time: 103 us; the launch traced here: 102 us
  waiting for transfers between devices  45.7 us (44%)
  starting transfers between devices  22.5 us (22%)
  Pallas kernels  22 us (21%)
  local copies, waits for them, and re-layouts  10.8 us (10%)
    ppermute x1, waiting for transfers between devices, on_device(): edge = lax.ppermute(jnp.stack([b[0], b[planes - 1]]), 'px', swap)  15.2 us
    ppermute x1, waiting for transfers between devices, on_device(): far_0 = lax.ppermute(onward_half, 'pz', onward)  12.5 us
    all_to_all x1, starting transfers between devices, on_device(): sent = exchange(b.reshape(count_i, share, width))  11.2 us
    unnamed x34, local copies, waits for them, and re-layouts  10.6 us
    all_to_all x1, waiting for transfers between devices, on_device(): time_term = exchange(applied).reshape(planes, rows, width)  7.48 us
    pallas_call x2, Pallas kernels, line_terms(): pl.pallas_call(kernel, out_shape=[jax.ShapeDtypeStruct(b.shape, f32), jax...  7.19 us
    all_to_all x1, waiting for transfers between devices, on_device(): sent = exchange(b.reshape(count_i, share, width))  6.32 us
    pallas_call x1, Pallas kernels, on_device(): pl.pallas_call(functools.partial(wall_kernel, dx), out_shape=[jax.ShapeDt...  5.79 us
  transfers between devices with their start and end apart: 12, of which 7 were waited for; matrix products, arithmetic and copies ran while one was open for 1% of the time, Pallas kernels for 19%

profile of v3, /device:TPU:56, one launch (start us, length us, event | category | flops | bytes accessed | tf_op | source)
XLA Modules:
  0.0 102.0 jit_solution(12584750654585541058)
XLA Ops:
  0.0 11.2 %all-to-all-start = ((f32[16,192,128]{2,1,0:T(8,128)}), f32[16,192,128]{2,1,0:T(8,128)}, u32[]{:S(2)}, u32[]{:S(2)}) async-start(f32[16,192,128]{2,1,0:T(8,128)} %bitcast.13), calls=%async_computation | async-start | bytes 3145728 | tf_op jit(solution)/shard_map/all_to_all | solution.py:237
  11.3 0.3 collective-permute-start.2
  11.6 1.8 %collective-permute-start.3 = (f32[8,384,128]{2,1,0:T(8,128)S(1)}, f32[8,384,128]{2,1,0:T(8,128)}, u32[]{:S(2)}, u32[]{:S(2)}) collective-permute-start(f32[8,384,128]{2,1,0:T(8,128)S(1)} %bitcast.16), channel_id=1, source_target_pairs={{2,0},{3,1},{4,2},{5,3},{6,4},{7,5},{0,6},{1,7},{10,8},{11,9},{12,... | collective-permute-start | bytes 4718600 | tf_op jit(solution)/shard_map/ppermute | solution.py:245
  13.5 0.8 pad_maximum_fusion
  14.2 0.6 collective-permute-start
  14.8 15.2 %collective-permute-done.edge_ref = f32[2,384,128]{2,1,0:T(8,128)S(1)} collective-permute-done((f32[2,384,128]{2,1,0:T(8,128)}, f32[2,384,128]{2,1,0:T(8,128)S(1)}, u32[]{:S(2)}, u32[]{:S(2)}) %collective-permute-start) | collective-permute-done | bytes 393248 | tf_op jit(solution)/shard_map/ppermute | solution.py:250
  30.2 1.5 %copy-done.2 = bf16[768,1152]{1,0:T(8,128)(2,1)S(1)} copy-done((bf16[768,1152]{1,0:T(8,128)(2,1)S(1)}, bf16[768,1152]{1,0:T(8,128)(2,1)}, u32[]{:S(2)}) %copy-start.2) | copy-done | bytes 1769496
  31.7 1.4 %copy-done.10 = f32[1,8,384,128]{3,2,1,0:T(8,128)S(1)} copy-done((f32[1,8,384,128]{3,2,1,0:T(8,128)S(1)}, f32[1,8,384,128]{3,2,1,0:T(8,128)}, u32[]{:S(2)}) %copy-start.10) | copy-done | bytes 1572888
  33.1 1.1 %copy-done.13 = bf16[1,8,384,128]{3,2,1,0:T(8,128)(2,1)S(1)} copy-done((bf16[1,8,384,128]{3,2,1,0:T(8,128)(2,1)S(1)}, bf16[1,8,384,128]{3,2,1,0:T(8,128)(2,1)}, u32[]{:S(2)}) %copy-start.13) | copy-done | bytes 786456
  34.2 1.1 %copy-done.14 = bf16[2,768,256]{2,1,0:T(8,128)(2,1)S(1)} copy-done((bf16[2,768,256]{2,1,0:T(8,128)(2,1)S(1)}, bf16[2,768,256]{2,1,0:T(8,128)(2,1)}, u32[]{:S(2)}) %copy-start.14) | copy-done | bytes 786456
  35.4 5.8 %wall_terms.1 = (f32[8,384,128]{2,1,0:T(8,128)S(1)}, f32[8,384,128]{2,1,0:T(8,128)S(1)}, f32[8,128]{1,0:T(8,128)S(1)}) custom-call(s32[1]{0:T(128)} %bitcast.1.core_ref, bf16[768,1152]{1,0:T(8,128)(2,1)S(1)} %copy-done.2, bf16[2,768,256]{2,1,0:T(8,128)(2,1)S(1)} %copy-done.14, f32[2,384,128]{2,1,0:T(8,128)S(1)} %jit_solution_.3.scale_ref, ...), custom_call_target="tpu_custom_call" | custom-call | flops 2415919104 | bytes 11010048 | tf_op jit(solution)/shard_map/wall_terms/pallas_call | solution.py:261
  41.2 1.1 %copy-done.4 = f32[8,384,128]{2,1,0:T(8,128)} copy-done((f32[8,384,128]{2,1,0:T(8,128)}, f32[8,384,128]{2,1,0:T(8,128)S(1)}, u32[]{:S(2)}) %copy-start.4) | copy-done | bytes 1572888
  42.3 1.2 %copy-done.6 = f32[8,384,128]{2,1,0:T(8,128)} copy-done((f32[8,384,128]{2,1,0:T(8,128)}, f32[8,384,128]{2,1,0:T(8,128)S(1)}, u32[]{:S(2)}) %copy-start.6) | copy-done | bytes 1572888
  43.5 0.6 copy-done.15
  44.1 6.3 %all-to-all-done.in_ref = f32[16,192,128]{2,1,0:T(8,128)} async-done(((f32[16,192,128]{2,1,0:T(8,128)}), f32[16,192,128]{2,1,0:T(8,128)}, u32[]{:S(2)}, u32[]{:S(2)}) %all-to-all-start) | async-done | bytes 1572896 | tf_op jit(solution)/shard_map/all_to_all | solution.py:237
  50.4 2.9 %time_term.1 = f32[16,192,128]{2,1,0:T(8,128)} custom-call(f32[16,192,128]{2,1,0:T(8,128)} %all-to-all-done.in_ref, f32[8,128]{1,0:T(8,128)} %copy-done.15), custom_call_target="tpu_custom_call" | custom-call | flops 6291456 | bytes 3145728 | tf_op jit(solution)/shard_map/time_term/pallas_call | solution.py:300
  53.4 5.3 %all-to-all-start.1 = ((f32[16,192,128]{2,1,0:T(8,128)}), f32[16,192,128]{2,1,0:T(8,128)}, u32[]{:S(2)}, u32[]{:S(2)}) async-start(f32[16,192,128]{2,1,0:T(8,128)} %time_term.1), calls=%async_computation.1 | async-start | bytes 3145728 | tf_op jit(solution)/shard_map/all_to_all | solution.py:311
  58.8 0.5 collective-permute-start.7
  59.3 3.4 %halves.1 = (f32[4,384,128]{2,1,0:T(8,128)S(1)}, f32[4,384,128]{2,1,0:T(8,128)S(1)}) custom-call(f32[8,384,128]{2,1,0:T(8,128)} %collective-permute-done.2.before_ref.refs_0_, f32[8,384,128]{2,1,0:T(8,128)} %collective-permute-done.3.after_ref.refs_2_), custom_call_target="tpu_custom_call" | custom-call | bytes 3145728 | tf_op jit(solution)/shard_map/halves/pallas_call | solution.py:286
  62.7 0.3 collective-permute-start.4
  63.0 1.8 %collective-permute-start.5 = (f32[4,384,128]{2,1,0:T(8,128)S(1)}, f32[4,384,128]{2,1,0:T(8,128)S(1)}, u32[]{:S(2)}, u32[]{:S(2)}) collective-permute-start(f32[4,384,128]{2,1,0:T(8,128)S(1)} %get-tuple-element.18), channel_id=1, source_target_pairs={{2,0},{3,1},{4,2},{5,3},{6,4},{7,5},{0,6},{1,7},{10,8},{11,9},{12,... | collective-permute-start | bytes 2359304 | tf_op jit(solution)/shard_map/ppermute | solution.py:297
  64.8 4.7 %early_terms.1 = (f32[8,384,128]{2,1,0:T(8,128)S(1)}, f32[8,128]{1,0:T(8,128)S(1)}) custom-call(s32[1]{0:T(128)} %bitcast.1.core_ref, bf16[2,1536,256]{2,1,0:T(8,128)(2,1)S(1)} %copy-done.3, f32[8,384,128]{2,1,0:T(8,128)} %collective-permute-done.2.before_ref.refs_0_, f32[8,384,128]{2,1,0:T(8,128)S(1)} %collective-permute-done.6.refs_1_, ...), custom_call_target="tpu_custom_call" | custom-call | flops 2415919104 | bytes 11010048 | tf_op jit(solution)/shard_map/early_terms/pallas_call | solution.py:318
  69.6 12.5 %collective-permute-done.4.refs_0_ = f32[4,384,128]{2,1,0:T(8,128)S(1)} collective-permute-done((f32[4,384,128]{2,1,0:T(8,128)S(1)}, f32[4,384,128]{2,1,0:T(8,128)S(1)}, u32[]{:S(2)}, u32[]{:S(2)}) %collective-permute-start.4) | collective-permute-done | bytes 786464 | tf_op jit(solution)/shard_map/ppermute | solution.py:296
  82.0 1.3 %collective-permute-done.5.refs_1_ = f32[4,384,128]{2,1,0:T(8,128)S(1)} collective-permute-done((f32[4,384,128]{2,1,0:T(8,128)S(1)}, f32[4,384,128]{2,1,0:T(8,128)S(1)}, u32[]{:S(2)}, u32[]{:S(2)}) %collective-permute-start.5) | collective-permute-done | bytes 786464 | tf_op jit(solution)/shard_map/ppermute | solution.py:297
  83.4 0.5 collective-permute-start.9
  83.9 1.8 %collective-permute-done.8.refs_1_ = f32[4,384,128]{2,1,0:T(8,128)S(1)} collective-permute-done((f32[4,384,128]{2,1,0:T(8,128)S(1)}, f32[4,384,128]{2,1,0:T(8,128)S(1)}, u32[]{:S(2)}, u32[]{:S(2)}) %collective-permute-start.8) | collective-permute-done | bytes 786464 | tf_op jit(solution)/shard_map/ppermute | solution.py:313
  85.6 1.1 %collective-permute-done.9.refs_3_ = f32[4,384,128]{2,1,0:T(8,128)S(1)} collective-permute-done((f32[4,384,128]{2,1,0:T(8,128)S(1)}, f32[4,384,128]{2,1,0:T(8,128)S(1)}, u32[]{:S(2)}, u32[]{:S(2)}) %collective-permute-start.9) | collective-permute-done | bytes 786464 | tf_op jit(solution)/shard_map/ppermute | solution.py:313
  86.8 2.5 %late_terms.1 = (f32[8,384,128]{2,1,0:T(8,128)S(1)}, f32[8,128]{1,0:T(8,128)}) custom-call(s32[1]{0:T(128)} %bitcast.1.core_ref, bf16[2,768,256]{2,1,0:T(8,128)(2,1)S(1)} %copy-done.11, f32[4,384,128]{2,1,0:T(8,128)S(1)} %get-tuple-element.21.refs_0_, f32[4,384,128]{2,1,0:T(8,128)S(1)} %collective-permute-done.8.refs_1_, ...), custom_call_target="tpu_custom_call" | custom-call | flops 1207959552 | bytes 7864320 | tf_op jit(solution)/shard_map/late_terms/pallas_call | solution.py:318
  89.2 1.1 %copy-done.8 = f32[8,384,128]{2,1,0:T(8,128)} copy-done((f32[8,384,128]{2,1,0:T(8,128)}, f32[8,384,128]{2,1,0:T(8,128)S(1)}, u32[]{:S(2)}) %copy-start.8) | copy-done | bytes 1572888
  90.4 7.5 %all-to-all-done.1 = f32[16,192,128]{2,1,0:T(8,128)} async-done(((f32[16,192,128]{2,1,0:T(8,128)}), f32[16,192,128]{2,1,0:T(8,128)}, u32[]{:S(2)}, u32[]{:S(2)}) %all-to-all-start.1) | async-done | bytes 1572896 | tf_op jit(solution)/shard_map/all_to_all | solution.py:311
  97.9 1.4 %copy-done.9 = f32[8,384,128]{2,1,0:T(8,128)S(1)} copy-done((f32[8,384,128]{2,1,0:T(8,128)S(1)}, f32[8,384,128]{2,1,0:T(8,128)}, u32[]{:S(2)}) %copy-start.9) | copy-done | bytes 1572888
  99.3 2.7 %last.1 = f32[8,384,128]{2,1,0:T(8,128)} custom-call(f32[8,384,128]{2,1,0:T(8,128)} %bitcast.9.time_ref, f32[8,384,128]{2,1,0:T(8,128)S(1)} %copy-done.7, f32[8,384,128]{2,1,0:T(8,128)S(1)} %copy-done.9), custom_call_target="tpu_custom_call" | custom-call | flops 786432 | bytes 6291456 | tf_op jit(solution)/shard_map/last/pallas_call | solution.py:338
  (36 shorter events, 0.4 us)
Async XLA Ops:
  0.0 11.2 %copy-start = (f32[1,8,384,128]{3,2,1,0:T(8,128)S(1)}, f32[1,8,384,128]{3,2,1,0:T(8,128)}, u32[]{:S(2)}) copy-start(f32[1,8,384,128]{3,2,1,0:T(8,128)} %param.13) | copy-start | bytes 4718596
  0.0 50.4 %all-to-all-start = ((f32[16,192,128]{2,1,0:T(8,128)}), f32[16,192,128]{2,1,0:T(8,128)}, u32[]{:S(2)}, u32[]{:S(2)}) async-start(f32[16,192,128]{2,1,0:T(8,128)} %bitcast.13), calls=%async_computation | async-start | bytes 3145728 | tf_op jit(solution)/shard_map/all_to_all | solution.py:237
  11.2 18.8 %copy-start.16 = (f32[2,384]{1,0:T(2,128)S(1)}, f32[2,384]{1,0:T(2,128)}, u32[]{:S(2)}) copy-start(f32[2,384]{1,0:T(2,128)} %constant.31.clone) | copy-start | bytes 9220
  11.2 19.0 %copy-start.1 = (bf16[1,8,384,128]{3,2,1,0:T(8,128)(2,1)S(1)}, bf16[1,8,384,128]{3,2,1,0:T(8,128)(2,1)}, u32[]{:S(2)}) copy-start(bf16[1,8,384,128]{3,2,1,0:T(8,128)(2,1)} %param.10) | copy-start | bytes 2359300
  11.2 19.0 %copy-start.12 = (bf16[1,8,384,128]{3,2,1,0:T(8,128)(2,1)S(1)}, bf16[1,8,384,128]{3,2,1,0:T(8,128)(2,1)}, u32[]{:S(2)}) copy-start(bf16[1,8,384,128]{3,2,1,0:T(8,128)(2,1)} %param.11) | copy-start | bytes 2359300
  11.2 18.8 %collective-permute-start.1 = (f32[8,384,128]{2,1,0:T(8,128)S(1)}, f32[8,384,128]{2,1,0:T(8,128)}, u32[]{:S(2)}, u32[]{:S(2)}) collective-permute-start(f32[8,384,128]{2,1,0:T(8,128)S(1)} %bitcast.14), channel_id=1, source_target_pairs={{0,1},{1,0},{2,3},{3,2},{4,5},{5,4},{6,7},{7,6},{8,9},{9,8},{10,11... | collective-permute-start | bytes 4718600 | tf_op jit(solution)/shard_map/ppermute | solution.py:246
  11.3 47.4 %collective-permute-start.2 = (f32[8,384,128]{2,1,0:T(8,128)S(1)}, f32[8,384,128]{2,1,0:T(8,128)}, u32[]{:S(2)}, u32[]{:S(2)}) collective-permute-start(f32[8,384,128]{2,1,0:T(8,128)S(1)} %bitcast.15), channel_id=1, source_target_pairs={{0,2},{1,3},{2,4},{3,5},{4,6},{5,7},{6,0},{7,1},{8,10},{9,11},{10,... | collective-permute-start | bytes 4718600 | tf_op jit(solution)/shard_map/ppermute | solution.py:244
  11.6 47.2 %collective-permute-start.3 = (f32[8,384,128]{2,1,0:T(8,128)S(1)}, f32[8,384,128]{2,1,0:T(8,128)}, u32[]{:S(2)}, u32[]{:S(2)}) collective-permute-start(f32[8,384,128]{2,1,0:T(8,128)S(1)} %bitcast.16), channel_id=1, source_target_pairs={{2,0},{3,1},{4,2},{5,3},{6,4},{7,5},{0,6},{1,7},{10,8},{11,9},{12,... | collective-permute-start | bytes 4718600 | tf_op jit(solution)/shard_map/ppermute | solution.py:245
  14.2 15.8 %collective-permute-start = (f32[2,384,128]{2,1,0:T(8,128)}, f32[2,384,128]{2,1,0:T(8,128)S(1)}, u32[]{:S(2)}, u32[]{:S(2)}) collective-permute-start(f32[2,384,128]{2,1,0:T(8,128)} %pad_maximum_fusion), channel_id=1, source_target_pairs={{0,8},{8,0},{1,9},{9,1},{2,10},{10,2},{3,11},{11,3},{4,12},{12,4},... | collective-permute-start | bytes 1179656 | tf_op jit(solution)/shard_map/ppermute | solution.py:250
  30.2 1.5 %copy-start.2 = (bf16[768,1152]{1,0:T(8,128)(2,1)S(1)}, bf16[768,1152]{1,0:T(8,128)(2,1)}, u32[]{:S(2)}) copy-start(bf16[768,1152]{1,0:T(8,128)(2,1)} %constant.30.clone.wall_ref) | copy-start | bytes 5308420
  31.7 1.4 %copy-start.10 = (f32[1,8,384,128]{3,2,1,0:T(8,128)S(1)}, f32[1,8,384,128]{3,2,1,0:T(8,128)}, u32[]{:S(2)}) copy-start(f32[1,8,384,128]{3,2,1,0:T(8,128)} %param.14) | copy-start | bytes 4718596
  33.1 1.1 %copy-start.13 = (bf16[1,8,384,128]{3,2,1,0:T(8,128)(2,1)S(1)}, bf16[1,8,384,128]{3,2,1,0:T(8,128)(2,1)}, u32[]{:S(2)}) copy-start(bf16[1,8,384,128]{3,2,1,0:T(8,128)(2,1)} %param.12) | copy-start | bytes 2359300
  34.2 1.1 %copy-start.14 = (bf16[2,768,256]{2,1,0:T(8,128)(2,1)S(1)}, bf16[2,768,256]{2,1,0:T(8,128)(2,1)}, u32[]{:S(2)}) copy-start(bf16[2,768,256]{2,1,0:T(8,128)(2,1)} %constant.27.clone.line_ref) | copy-start | bytes 2359300
  41.2 1.2 %copy-start.4 = (f32[8,384,128]{2,1,0:T(8,128)}, f32[8,384,128]{2,1,0:T(8,128)S(1)}, u32[]{:S(2)}) copy-start(f32[8,384,128]{2,1,0:T(8,128)S(1)} %get-tuple-element.19.refs_5_) | copy-start | bytes 4718596
  42.3 1.2 %copy-start.6 = (f32[8,384,128]{2,1,0:T(8,128)}, f32[8,384,128]{2,1,0:T(8,128)S(1)}, u32[]{:S(2)}) copy-start(f32[8,384,128]{2,1,0:T(8,128)S(1)} %get-tuple-element.16.inv_ref) | copy-start | bytes 4718596
  43.5 0.6 copy-start.15
  53.4 44.5 %all-to-all-start.1 = ((f32[16,192,128]{2,1,0:T(8,128)}), f32[16,192,128]{2,1,0:T(8,128)}, u32[]{:S(2)}, u32[]{:S(2)}) async-start(f32[16,192,128]{2,1,0:T(8,128)} %time_term.1), calls=%async_computation.1 | async-start | bytes 3145728 | tf_op jit(solution)/shard_map/all_to_all | solution.py:311
  58.7 6.1 %copy-start.3 = (bf16[2,1536,256]{2,1,0:T(8,128)(2,1)S(1)}, bf16[2,1536,256]{2,1,0:T(8,128)(2,1)}, u32[]{:S(2)}) copy-start(bf16[2,1536,256]{2,1,0:T(8,128)(2,1)} %constant.28.clone.table_ref) | copy-start | bytes 4718596
  58.7 6.1 %copy-start.5 = (f32[8,384,128]{2,1,0:T(8,128)S(1)}, f32[8,384,128]{2,1,0:T(8,128)}, u32[]{:S(2)}) copy-start(f32[8,384,128]{2,1,0:T(8,128)} %copy-done.4) | copy-start | bytes 4718596
  58.7 6.1 %collective-permute-start.6 = (f32[8,384,128]{2,1,0:T(8,128)}, f32[8,384,128]{2,1,0:T(8,128)S(1)}, u32[]{:S(2)}, u32[]{:S(2)}) collective-permute-start(f32[8,384,128]{2,1,0:T(8,128)} %collective-permute-done.2.before_ref.refs_0_), channel_id=1, source_target_pairs={{0,1},{1,0},{2,3},{3,2},{4,5},{5,4},{6,7},{7,6},{8,9},{9,8},{10,11... | collective-permute-start | bytes 4718600 | tf_op jit(solution)/shard_map/ppermute | solution.py:313
  58.8 6.0 %collective-permute-start.7 = (f32[8,384,128]{2,1,0:T(8,128)}, f32[8,384,128]{2,1,0:T(8,128)S(1)}, u32[]{:S(2)}, u32[]{:S(2)}) collective-permute-start(f32[8,384,128]{2,1,0:T(8,128)} %collective-permute-done.3.after_ref.refs_2_), channel_id=1, source_target_pairs={{0,1},{1,0},{2,3},{3,2},{4,5},{5,4},{6,7},{7,6},{8,9},{9,8},{10,11... | collective-permute-start | bytes 4718600 | tf_op jit(solution)/shard_map/ppermute | solution.py:313
  62.7 19.3 %collective-permute-start.4 = (f32[4,384,128]{2,1,0:T(8,128)S(1)}, f32[4,384,128]{2,1,0:T(8,128)S(1)}, u32[]{:S(2)}, u32[]{:S(2)}) collective-permute-start(f32[4,384,128]{2,1,0:T(8,128)S(1)} %get-tuple-element.17), channel_id=1, source_target_pairs={{0,2},{1,3},{2,4},{3,5},{4,6},{5,7},{6,0},{7,1},{8,10},{9,11},{10,... | collective-permute-start | bytes 2359304 | tf_op jit(solution)/shard_map/ppermute | solution.py:296
  63.0 20.3 %collective-permute-start.5 = (f32[4,384,128]{2,1,0:T(8,128)S(1)}, f32[4,384,128]{2,1,0:T(8,128)S(1)}, u32[]{:S(2)}, u32[]{:S(2)}) collective-permute-start(f32[4,384,128]{2,1,0:T(8,128)S(1)} %get-tuple-element.18), channel_id=1, source_target_pairs={{2,0},{3,1},{4,2},{5,3},{6,4},{7,5},{0,6},{1,7},{10,8},{11,9},{12,... | collective-permute-start | bytes 2359304 | tf_op jit(solution)/shard_map/ppermute | solution.py:297
  69.6 17.2 %copy-start.11 = (bf16[2,768,256]{2,1,0:T(8,128)(2,1)S(1)}, bf16[2,768,256]{2,1,0:T(8,128)(2,1)}, u32[]{:S(2)}) copy-start(bf16[2,768,256]{2,1,0:T(8,128)(2,1)} %constant.29.clone.table_ref) | copy-start | bytes 2359300
  83.3 2.3 %collective-permute-start.8 = (f32[4,384,128]{2,1,0:T(8,128)S(1)}, f32[4,384,128]{2,1,0:T(8,128)S(1)}, u32[]{:S(2)}, u32[]{:S(2)}) collective-permute-start(f32[4,384,128]{2,1,0:T(8,128)S(1)} %get-tuple-element.21.refs_0_), channel_id=1, source_target_pairs={{0,1},{1,0},{2,3},{3,2},{4,5},{5,4},{6,7},{7,6},{8,9},{9,8},{10,11... | collective-permute-start | bytes 2359304 | tf_op jit(solution)/shard_map/ppermute | solution.py:313
  83.4 3.4 %collective-permute-start.9 = (f32[4,384,128]{2,1,0:T(8,128)S(1)}, f32[4,384,128]{2,1,0:T(8,128)S(1)}, u32[]{:S(2)}, u32[]{:S(2)}) collective-permute-start(f32[4,384,128]{2,1,0:T(8,128)S(1)} %get-tuple-element.22.refs_2_), channel_id=1, source_target_pairs={{0,1},{1,0},{2,3},{3,2},{4,5},{5,4},{6,7},{7,6},{8,9},{9,8},{10,11... | collective-permute-start | bytes 2359304 | tf_op jit(solution)/shard_map/ppermute | solution.py:313
  86.8 11.1 %copy-start.7 = (f32[8,384,128]{2,1,0:T(8,128)S(1)}, f32[8,384,128]{2,1,0:T(8,128)}, u32[]{:S(2)}) copy-start(f32[8,384,128]{2,1,0:T(8,128)} %copy-done.6) | copy-start | bytes 4718596
  89.2 1.1 %copy-start.8 = (f32[8,384,128]{2,1,0:T(8,128)}, f32[8,384,128]{2,1,0:T(8,128)S(1)}, u32[]{:S(2)}) copy-start(f32[8,384,128]{2,1,0:T(8,128)S(1)} %get-tuple-element.24.steps_ref) | copy-start | bytes 4718596
  97.9 1.4 %copy-start.9 = (f32[8,384,128]{2,1,0:T(8,128)S(1)}, f32[8,384,128]{2,1,0:T(8,128)}, u32[]{:S(2)}) copy-start(f32[8,384,128]{2,1,0:T(8,128)} %copy-done.8) | copy-start | bytes 4718596

commit v4 on v3

--- a/solution.py
+++ b/solution.py
@@ -197,9 +197,9 @@
     in_parts(parts, [in_ref], [source], result, out_ref, in_sems, out_sems, work)
 
 
-def last_kernel(parts, time_ref, inv_ref, steps_ref, out_ref, result, in_sems, out_sems):
-    work = LastPart(steps_ref.shape[0] // parts, steps_ref, time_ref, inv_ref, result)
-    in_parts(parts, [], [], result, out_ref, in_sems, out_sems, work)
+def last_kernel(parts, inv_ref, time_ref, steps_ref, out_ref, time, steps, result, in_sems, out_sems):
+    work = LastPart(steps_ref.shape[0] // parts, steps, time, inv_ref, result)
+    in_parts(parts, [time_ref, steps_ref], [time, steps], result, out_ref, in_sems, out_sems, work)
 
 
 def on_device(stream_vel, normal_vel, span_vel, adjoint_buoy, adjoint_normal):
@@ -338,14 +338,15 @@
     out = pl.pallas_call(
         functools.partial(last_kernel, planes),
         out_shape=jax.ShapeDtypeStruct(b.shape, f32),
-        in_specs=[pl.BlockSpec(memory_space=pltpu.VMEM)] * 3,
+        in_specs=[pl.BlockSpec(memory_space=pltpu.VMEM)] + [in_memory] * 2,
         out_specs=in_memory,
-        scratch_shapes=[pltpu.VMEM(b.shape, f32)]
-        + [pltpu.SemaphoreType.DMA((1, planes)), pltpu.SemaphoreType.DMA((planes,))],
-        compiler_params=params(8),
+        input_output_aliases={2: 0},
+        scratch_shapes=[pltpu.VMEM(b.shape, f32)] * 3
+        + [pltpu.SemaphoreType.DMA((2, planes)), pltpu.SemaphoreType.DMA((planes,))],
+        compiler_params=params(60),
         cost_estimate=pl.CostEstimate(flops=2 * b.size, bytes_accessed=b.size * 16, transcendentals=0),
         name="last",
-    )(time_term, inv, steps)
+    )(inv, time_term, steps)
     return out[None]
 
 

time: 103 us -> 103 us (level)
  local copies, waits for them, and re-layouts: 10.8 us -> 8.28 us
  Pallas kernels: 22 us -> 24.1 us
    unnamed x34 -> x28, local copies, waits for them, and re-layouts: 10.6 us -> 8.1 us
    pallas_call x1, Pallas kernels: 2.7 us -> 4.25 us  [on_device(): pl.pallas_call(functools.partial(last_kernel, planes), out_shape=jax.Shap...]
where the time goes in v4:
time: 103 us; the launch traced here: 102 us
  waiting for transfers between devices  46.3 us (45%)
  Pallas kernels  24.1 us (23%)
  starting transfers between devices  22.5 us (22%)
  local copies, waits for them, and re-layouts  8.28 us (8%)
    ppermute x1, waiting for transfers between devices, on_device(): edge = lax.ppermute(jnp.stack([b[0], b[planes - 1]]), 'px', swap)  15.2 us
    ppermute x1, waiting for transfers between devices, on_device(): far_0 = lax.ppermute(onward_half, 'pz', onward)  12.5 us
    all_to_all x1, starting transfers between devices, on_device(): sent = exchange(b.reshape(count_i, share, width))  11.2 us
    all_to_all x1, waiting for transfers between devices, on_device(): time_term = exchange(applied).reshape(planes, rows, width)  8.14 us
    unnamed x28, local copies, waits for them, and re-layouts  8.1 us
    pallas_call x2, Pallas kernels, line_terms(): pl.pallas_call(kernel, out_shape=[jax.ShapeDtypeStruct(b.shape, f32), jax...  7.68 us
    all_to_all x1, waiting for transfers between devices, on_device(): sent = exchange(b.reshape(count_i, share, width))  6.32 us
    pallas_call x1, Pallas kernels, on_device(): pl.pallas_call(functools.partial(wall_kernel, dx), out_shape=[jax.ShapeDt...  5.79 us
  transfers between devices with their start and end apart: 12, of which 7 were waited for; matrix products, arithmetic and copies ran while one was open for 1% of the time, Pallas kernels for 19%

profile of v4, /device:TPU:56, one launch (start us, length us, event | category | flops | bytes accessed | tf_op | source)
XLA Modules:
  0.0 102.2 jit_solution(3860592794145990525)
XLA Ops:
  0.0 11.2 %all-to-all-start = ((f32[16,192,128]{2,1,0:T(8,128)}), f32[16,192,128]{2,1,0:T(8,128)}, u32[]{:S(2)}, u32[]{:S(2)}) async-start(f32[16,192,128]{2,1,0:T(8,128)} %bitcast.13), calls=%async_computation | async-start | bytes 3145728 | tf_op jit(solution)/shard_map/all_to_all | solution.py:237
  11.2 0.1 collective-permute-start.1
  11.3 0.3 collective-permute-start.2
  11.6 1.8 %collective-permute-start.3 = (f32[8,384,128]{2,1,0:T(8,128)S(1)}, f32[8,384,128]{2,1,0:T(8,128)}, u32[]{:S(2)}, u32[]{:S(2)}) collective-permute-start(f32[8,384,128]{2,1,0:T(8,128)S(1)} %bitcast.16), channel_id=1, source_target_pairs={{2,0},{3,1},{4,2},{5,3},{6,4},{7,5},{0,6},{1,7},{10,8},{11,9},{12,... | collective-permute-start | bytes 4718600 | tf_op jit(solution)/shard_map/ppermute | solution.py:245
  13.5 0.8 pad_maximum_fusion
  14.2 0.6 collective-permute-start
  14.8 15.2 %collective-permute-done.edge_ref = f32[2,384,128]{2,1,0:T(8,128)S(1)} collective-permute-done((f32[2,384,128]{2,1,0:T(8,128)}, f32[2,384,128]{2,1,0:T(8,128)S(1)}, u32[]{:S(2)}, u32[]{:S(2)}) %collective-permute-start) | collective-permute-done | bytes 393248 | tf_op jit(solution)/shard_map/ppermute | solution.py:250
  30.0 0.2 jit_solution_.3.scale_ref
  30.2 1.5 %copy-done.2 = bf16[768,1152]{1,0:T(8,128)(2,1)S(1)} copy-done((bf16[768,1152]{1,0:T(8,128)(2,1)S(1)}, bf16[768,1152]{1,0:T(8,128)(2,1)}, u32[]{:S(2)}) %copy-start.2) | copy-done | bytes 1769496
  31.7 1.4 %copy-done.7 = f32[1,8,384,128]{3,2,1,0:T(8,128)S(1)} copy-done((f32[1,8,384,128]{3,2,1,0:T(8,128)S(1)}, f32[1,8,384,128]{3,2,1,0:T(8,128)}, u32[]{:S(2)}) %copy-start.7) | copy-done | bytes 1572888
  33.1 1.1 %copy-done.10 = bf16[1,8,384,128]{3,2,1,0:T(8,128)(2,1)S(1)} copy-done((bf16[1,8,384,128]{3,2,1,0:T(8,128)(2,1)S(1)}, bf16[1,8,384,128]{3,2,1,0:T(8,128)(2,1)}, u32[]{:S(2)}) %copy-start.10) | copy-done | bytes 786456
  34.2 1.1 %copy-done.11 = bf16[2,768,256]{2,1,0:T(8,128)(2,1)S(1)} copy-done((bf16[2,768,256]{2,1,0:T(8,128)(2,1)S(1)}, bf16[2,768,256]{2,1,0:T(8,128)(2,1)}, u32[]{:S(2)}) %copy-start.11) | copy-done | bytes 786456
  35.4 5.8 %wall_terms.1 = (f32[8,384,128]{2,1,0:T(8,128)S(1)}, f32[8,384,128]{2,1,0:T(8,128)S(1)}, f32[8,128]{1,0:T(8,128)S(1)}) custom-call(s32[1]{0:T(128)} %bitcast.core_ref, bf16[768,1152]{1,0:T(8,128)(2,1)S(1)} %copy-done.2, bf16[2,768,256]{2,1,0:T(8,128)(2,1)S(1)} %copy-done.11, f32[2,384,128]{2,1,0:T(8,128)S(1)} %jit_solution_.3.scale_ref, ...), custom_call_target="tpu_custom_call" | custom-call | flops 2415919104 | bytes 11010048 | tf_op jit(solution)/shard_map/wall_terms/pallas_call | solution.py:261
  41.2 1.1 %copy-done.4 = f32[8,384,128]{2,1,0:T(8,128)} copy-done((f32[8,384,128]{2,1,0:T(8,128)}, f32[8,384,128]{2,1,0:T(8,128)S(1)}, u32[]{:S(2)}) %copy-start.4) | copy-done | bytes 1572888
  42.3 1.2 %copy-done.6 = f32[8,384,128]{2,1,0:T(8,128)} copy-done((f32[8,384,128]{2,1,0:T(8,128)}, f32[8,384,128]{2,1,0:T(8,128)S(1)}, u32[]{:S(2)}) %copy-start.6) | copy-done | bytes 1572888
  43.5 0.6 copy-done.12
  44.1 6.3 %all-to-all-done.in_ref = f32[16,192,128]{2,1,0:T(8,128)} async-done(((f32[16,192,128]{2,1,0:T(8,128)}), f32[16,192,128]{2,1,0:T(8,128)}, u32[]{:S(2)}, u32[]{:S(2)}) %all-to-all-start) | async-done | bytes 1572896 | tf_op jit(solution)/shard_map/all_to_all | solution.py:237
  50.4 3.0 %time_term.1 = f32[16,192,128]{2,1,0:T(8,128)} custom-call(f32[16,192,128]{2,1,0:T(8,128)} %all-to-all-done.in_ref, f32[8,128]{1,0:T(8,128)} %copy-done.12), custom_call_target="tpu_custom_call" | custom-call | flops 6291456 | bytes 3145728 | tf_op jit(solution)/shard_map/time_term/pallas_call | solution.py:300
  53.4 5.3 %all-to-all-start.1 = ((f32[16,192,128]{2,1,0:T(8,128)}), f32[16,192,128]{2,1,0:T(8,128)}, u32[]{:S(2)}, u32[]{:S(2)}) async-start(f32[16,192,128]{2,1,0:T(8,128)} %time_term.1), calls=%async_computation.1 | async-start | bytes 3145728 | tf_op jit(solution)/shard_map/all_to_all | solution.py:311
  58.9 0.5 collective-permute-start.7
  59.4 3.4 %halves.1 = (f32[4,384,128]{2,1,0:T(8,128)S(1)}, f32[4,384,128]{2,1,0:T(8,128)S(1)}) custom-call(f32[8,384,128]{2,1,0:T(8,128)} %collective-permute-done.2.before_ref.refs_0_, f32[8,384,128]{2,1,0:T(8,128)} %collective-permute-done.3.after_ref.refs_2_), custom_call_target="tpu_custom_call" | custom-call | bytes 3145728 | tf_op jit(solution)/shard_map/halves/pallas_call | solution.py:286
  62.8 0.3 collective-permute-start.4
  63.1 1.8 %collective-permute-start.5 = (f32[4,384,128]{2,1,0:T(8,128)S(1)}, f32[4,384,128]{2,1,0:T(8,128)S(1)}, u32[]{:S(2)}, u32[]{:S(2)}) collective-permute-start(f32[4,384,128]{2,1,0:T(8,128)S(1)} %get-tuple-element.18), channel_id=1, source_target_pairs={{2,0},{3,1},{4,2},{5,3},{6,4},{7,5},{0,6},{1,7},{10,8},{11,9},{12,... | collective-permute-start | bytes 2359304 | tf_op jit(solution)/shard_map/ppermute | solution.py:297
  64.9 4.7 %early_terms.1 = (f32[8,384,128]{2,1,0:T(8,128)S(1)}, f32[8,128]{1,0:T(8,128)S(1)}) custom-call(s32[1]{0:T(128)} %bitcast.core_ref, bf16[2,1536,256]{2,1,0:T(8,128)(2,1)S(1)} %copy-done.3, f32[8,384,128]{2,1,0:T(8,128)} %collective-permute-done.2.before_ref.refs_0_, f32[8,384,128]{2,1,0:T(8,128)S(1)} %collective-permute-done.6.refs_1_, ...), custom_call_target="tpu_custom_call" | custom-call | flops 2415919104 | bytes 11010048 | tf_op jit(solution)/shard_map/early_terms/pallas_call | solution.py:318
  69.6 12.5 %collective-permute-done.4.refs_0_ = f32[4,384,128]{2,1,0:T(8,128)S(1)} collective-permute-done((f32[4,384,128]{2,1,0:T(8,128)S(1)}, f32[4,384,128]{2,1,0:T(8,128)S(1)}, u32[]{:S(2)}, u32[]{:S(2)}) %collective-permute-start.4) | collective-permute-done | bytes 786464 | tf_op jit(solution)/shard_map/ppermute | solution.py:296
  82.1 1.3 %collective-permute-done.5.refs_1_ = f32[4,384,128]{2,1,0:T(8,128)S(1)} collective-permute-done((f32[4,384,128]{2,1,0:T(8,128)S(1)}, f32[4,384,128]{2,1,0:T(8,128)S(1)}, u32[]{:S(2)}, u32[]{:S(2)}) %collective-permute-start.5) | collective-permute-done | bytes 786464 | tf_op jit(solution)/shard_map/ppermute | solution.py:297
  83.4 0.5 collective-permute-start.9
  83.9 1.8 %collective-permute-done.8.refs_1_ = f32[4,384,128]{2,1,0:T(8,128)S(1)} collective-permute-done((f32[4,384,128]{2,1,0:T(8,128)S(1)}, f32[4,384,128]{2,1,0:T(8,128)S(1)}, u32[]{:S(2)}, u32[]{:S(2)}) %collective-permute-start.8) | collective-permute-done | bytes 786464 | tf_op jit(solution)/shard_map/ppermute | solution.py:313
  85.7 1.1 %collective-permute-done.9.refs_3_ = f32[4,384,128]{2,1,0:T(8,128)S(1)} collective-permute-done((f32[4,384,128]{2,1,0:T(8,128)S(1)}, f32[4,384,128]{2,1,0:T(8,128)S(1)}, u32[]{:S(2)}, u32[]{:S(2)}) %collective-permute-start.9) | collective-permute-done | bytes 786464 | tf_op jit(solution)/shard_map/ppermute | solution.py:313
  86.8 3.0 %late_terms.1 = (f32[8,384,128]{2,1,0:T(8,128)}, f32[8,128]{1,0:T(8,128)}) custom-call(s32[1]{0:T(128)} %bitcast.core_ref, bf16[2,768,256]{2,1,0:T(8,128)(2,1)S(1)} %copy-done.8, f32[4,384,128]{2,1,0:T(8,128)S(1)} %get-tuple-element.21.refs_0_, f32[4,384,128]{2,1,0:T(8,128)S(1)} %collective-permute-done.8.refs_1_, ...), custom_call_target="tpu_custom_call" | custom-call | flops 1207959552 | bytes 7864320 | tf_op jit(solution)/shard_map/late_terms/pallas_call | solution.py:318
  89.8 8.1 %all-to-all-done.1 = f32[16,192,128]{2,1,0:T(8,128)} async-done(((f32[16,192,128]{2,1,0:T(8,128)}), f32[16,192,128]{2,1,0:T(8,128)}, u32[]{:S(2)}, u32[]{:S(2)}) %all-to-all-start.1) | async-done | bytes 1572896 | tf_op jit(solution)/shard_map/all_to_all | solution.py:311
  97.9 4.3 %last.1 = f32[8,384,128]{2,1,0:T(8,128)} custom-call(f32[8,384,128]{2,1,0:T(8,128)} %copy-done.6, f32[8,384,128]{2,1,0:T(8,128)} %bitcast.9.time_ref, f32[8,384,128]{2,1,0:T(8,128)} %get-tuple-element.24.steps_ref), custom_call_target="tpu_custom_call", output_to_operand_aliasing={{}: (2, {})} | custom-call | flops 786432 | bytes 6291456 | tf_op jit(solution)/shard_map/last/pallas_call | solution.py:338
  (30 shorter events, 0.2 us)
Async XLA Ops:
  0.0 11.2 %copy-start = (f32[1,8,384,128]{3,2,1,0:T(8,128)S(1)}, f32[1,8,384,128]{3,2,1,0:T(8,128)}, u32[]{:S(2)}) copy-start(f32[1,8,384,128]{3,2,1,0:T(8,128)} %param.13) | copy-start | bytes 4718596
  0.0 50.4 %all-to-all-start = ((f32[16,192,128]{2,1,0:T(8,128)}), f32[16,192,128]{2,1,0:T(8,128)}, u32[]{:S(2)}, u32[]{:S(2)}) async-start(f32[16,192,128]{2,1,0:T(8,128)} %bitcast.13), calls=%async_computation | async-start | bytes 3145728 | tf_op jit(solution)/shard_map/all_to_all | solution.py:237
  11.2 18.8 %copy-start.13 = (f32[2,384]{1,0:T(2,128)S(1)}, f32[2,384]{1,0:T(2,128)}, u32[]{:S(2)}) copy-start(f32[2,384]{1,0:T(2,128)} %constant.31.clone) | copy-start | bytes 9220
  11.2 19.0 %copy-start.1 = (bf16[1,8,384,128]{3,2,1,0:T(8,128)(2,1)S(1)}, bf16[1,8,384,128]{3,2,1,0:T(8,128)(2,1)}, u32[]{:S(2)}) copy-start(bf16[1,8,384,128]{3,2,1,0:T(8,128)(2,1)} %param.10) | copy-start | bytes 2359300
  11.2 19.0 %copy-start.9 = (bf16[1,8,384,128]{3,2,1,0:T(8,128)(2,1)S(1)}, bf16[1,8,384,128]{3,2,1,0:T(8,128)(2,1)}, u32[]{:S(2)}) copy-start(bf16[1,8,384,128]{3,2,1,0:T(8,128)(2,1)} %param.11) | copy-start | bytes 2359300
  11.2 18.8 %collective-permute-start.1 = (f32[8,384,128]{2,1,0:T(8,128)S(1)}, f32[8,384,128]{2,1,0:T(8,128)}, u32[]{:S(2)}, u32[]{:S(2)}) collective-permute-start(f32[8,384,128]{2,1,0:T(8,128)S(1)} %bitcast.14), channel_id=1, source_target_pairs={{0,1},{1,0},{2,3},{3,2},{4,5},{5,4},{6,7},{7,6},{8,9},{9,8},{10,11... | collective-permute-start | bytes 4718600 | tf_op jit(solution)/shard_map/ppermute | solution.py:246
  11.3 47.5 %collective-permute-start.2 = (f32[8,384,128]{2,1,0:T(8,128)S(1)}, f32[8,384,128]{2,1,0:T(8,128)}, u32[]{:S(2)}, u32[]{:S(2)}) collective-permute-start(f32[8,384,128]{2,1,0:T(8,128)S(1)} %bitcast.15), channel_id=1, source_target_pairs={{0,2},{1,3},{2,4},{3,5},{4,6},{5,7},{6,0},{7,1},{8,10},{9,11},{10,... | collective-permute-start | bytes 4718600 | tf_op jit(solution)/shard_map/ppermute | solution.py:244
  11.6 47.3 %collective-permute-start.3 = (f32[8,384,128]{2,1,0:T(8,128)S(1)}, f32[8,384,128]{2,1,0:T(8,128)}, u32[]{:S(2)}, u32[]{:S(2)}) collective-permute-start(f32[8,384,128]{2,1,0:T(8,128)S(1)} %bitcast.16), channel_id=1, source_target_pairs={{2,0},{3,1},{4,2},{5,3},{6,4},{7,5},{0,6},{1,7},{10,8},{11,9},{12,... | collective-permute-start | bytes 4718600 | tf_op jit(solution)/shard_map/ppermute | solution.py:245
  14.2 15.8 %collective-permute-start = (f32[2,384,128]{2,1,0:T(8,128)}, f32[2,384,128]{2,1,0:T(8,128)S(1)}, u32[]{:S(2)}, u32[]{:S(2)}) collective-permute-start(f32[2,384,128]{2,1,0:T(8,128)} %pad_maximum_fusion), channel_id=1, source_target_pairs={{0,8},{8,0},{1,9},{9,1},{2,10},{10,2},{3,11},{11,3},{4,12},{12,4},... | collective-permute-start | bytes 1179656 | tf_op jit(solution)/shard_map/ppermute | solution.py:250
  30.2 1.5 %copy-start.2 = (bf16[768,1152]{1,0:T(8,128)(2,1)S(1)}, bf16[768,1152]{1,0:T(8,128)(2,1)}, u32[]{:S(2)}) copy-start(bf16[768,1152]{1,0:T(8,128)(2,1)} %constant.30.clone.wall_ref) | copy-start | bytes 5308420
  31.7 1.4 %copy-start.7 = (f32[1,8,384,128]{3,2,1,0:T(8,128)S(1)}, f32[1,8,384,128]{3,2,1,0:T(8,128)}, u32[]{:S(2)}) copy-start(f32[1,8,384,128]{3,2,1,0:T(8,128)} %param.14) | copy-start | bytes 4718596
  33.1 1.1 %copy-start.10 = (bf16[1,8,384,128]{3,2,1,0:T(8,128)(2,1)S(1)}, bf16[1,8,384,128]{3,2,1,0:T(8,128)(2,1)}, u32[]{:S(2)}) copy-start(bf16[1,8,384,128]{3,2,1,0:T(8,128)(2,1)} %param.12) | copy-start | bytes 2359300
  34.2 1.1 %copy-start.11 = (bf16[2,768,256]{2,1,0:T(8,128)(2,1)S(1)}, bf16[2,768,256]{2,1,0:T(8,128)(2,1)}, u32[]{:S(2)}) copy-start(bf16[2,768,256]{2,1,0:T(8,128)(2,1)} %constant.27.clone.line_ref) | copy-start | bytes 2359300
  41.2 1.1 %copy-start.4 = (f32[8,384,128]{2,1,0:T(8,128)}, f32[8,384,128]{2,1,0:T(8,128)S(1)}, u32[]{:S(2)}) copy-start(f32[8,384,128]{2,1,0:T(8,128)S(1)} %get-tuple-element.19.refs_5_) | copy-start | bytes 4718596
  42.3 1.2 %copy-start.6 = (f32[8,384,128]{2,1,0:T(8,128)}, f32[8,384,128]{2,1,0:T(8,128)S(1)}, u32[]{:S(2)}) copy-start(f32[8,384,128]{2,1,0:T(8,128)S(1)} %get-tuple-element.15.inv_ref) | copy-start | bytes 4718596
  43.5 0.6 copy-start.12
  53.4 44.5 %all-to-all-start.1 = ((f32[16,192,128]{2,1,0:T(8,128)}), f32[16,192,128]{2,1,0:T(8,128)}, u32[]{:S(2)}, u32[]{:S(2)}) async-start(f32[16,192,128]{2,1,0:T(8,128)} %time_term.1), calls=%async_computation.1 | async-start | bytes 3145728 | tf_op jit(solution)/shard_map/all_to_all | solution.py:311
  58.8 6.1 %copy-start.3 = (bf16[2,1536,256]{2,1,0:T(8,128)(2,1)S(1)}, bf16[2,1536,256]{2,1,0:T(8,128)(2,1)}, u32[]{:S(2)}) copy-start(bf16[2,1536,256]{2,1,0:T(8,128)(2,1)} %constant.28.clone.table_ref) | copy-start | bytes 4718596
  58.8 6.1 %copy-start.5 = (f32[8,384,128]{2,1,0:T(8,128)S(1)}, f32[8,384,128]{2,1,0:T(8,128)}, u32[]{:S(2)}) copy-start(f32[8,384,128]{2,1,0:T(8,128)} %copy-done.4) | copy-start | bytes 4718596
  58.8 6.1 %collective-permute-start.6 = (f32[8,384,128]{2,1,0:T(8,128)}, f32[8,384,128]{2,1,0:T(8,128)S(1)}, u32[]{:S(2)}, u32[]{:S(2)}) collective-permute-start(f32[8,384,128]{2,1,0:T(8,128)} %collective-permute-done.2.before_ref.refs_0_), channel_id=1, source_target_pairs={{0,1},{1,0},{2,3},{3,2},{4,5},{5,4},{6,7},{7,6},{8,9},{9,8},{10,11... | collective-permute-start | bytes 4718600 | tf_op jit(solution)/shard_map/ppermute | solution.py:313
  58.9 6.0 %collective-permute-start.7 = (f32[8,384,128]{2,1,0:T(8,128)}, f32[8,384,128]{2,1,0:T(8,128)S(1)}, u32[]{:S(2)}, u32[]{:S(2)}) collective-permute-start(f32[8,384,128]{2,1,0:T(8,128)} %collective-permute-done.3.after_ref.refs_2_), channel_id=1, source_target_pairs={{0,1},{1,0},{2,3},{3,2},{4,5},{5,4},{6,7},{7,6},{8,9},{9,8},{10,11... | collective-permute-start | bytes 4718600 | tf_op jit(solution)/shard_map/ppermute | solution.py:313
  62.8 19.3 %collective-permute-start.4 = (f32[4,384,128]{2,1,0:T(8,128)S(1)}, f32[4,384,128]{2,1,0:T(8,128)S(1)}, u32[]{:S(2)}, u32[]{:S(2)}) collective-permute-start(f32[4,384,128]{2,1,0:T(8,128)S(1)} %get-tuple-element.17), channel_id=1, source_target_pairs={{0,2},{1,3},{2,4},{3,5},{4,6},{5,7},{6,0},{7,1},{8,10},{9,11},{10,... | collective-permute-start | bytes 2359304 | tf_op jit(solution)/shard_map/ppermute | solution.py:296
  63.1 20.3 %collective-permute-start.5 = (f32[4,384,128]{2,1,0:T(8,128)S(1)}, f32[4,384,128]{2,1,0:T(8,128)S(1)}, u32[]{:S(2)}, u32[]{:S(2)}) collective-permute-start(f32[4,384,128]{2,1,0:T(8,128)S(1)} %get-tuple-element.18), channel_id=1, source_target_pairs={{2,0},{3,1},{4,2},{5,3},{6,4},{7,5},{0,6},{1,7},{10,8},{11,9},{12,... | collective-permute-start | bytes 2359304 | tf_op jit(solution)/shard_map/ppermute | solution.py:297
  69.6 17.2 %copy-start.8 = (bf16[2,768,256]{2,1,0:T(8,128)(2,1)S(1)}, bf16[2,768,256]{2,1,0:T(8,128)(2,1)}, u32[]{:S(2)}) copy-start(bf16[2,768,256]{2,1,0:T(8,128)(2,1)} %constant.29.clone.table_ref) | copy-start | bytes 2359300
  83.4 2.3 %collective-permute-start.8 = (f32[4,384,128]{2,1,0:T(8,128)S(1)}, f32[4,384,128]{2,1,0:T(8,128)S(1)}, u32[]{:S(2)}, u32[]{:S(2)}) collective-permute-start(f32[4,384,128]{2,1,0:T(8,128)S(1)} %get-tuple-element.21.refs_0_), channel_id=1, source_target_pairs={{0,1},{1,0},{2,3},{3,2},{4,5},{5,4},{6,7},{7,6},{8,9},{9,8},{10,11... | collective-permute-start | bytes 2359304 | tf_op jit(solution)/shard_map/ppermute | solution.py:313
  83.4 3.4 %collective-permute-start.9 = (f32[4,384,128]{2,1,0:T(8,128)S(1)}, f32[4,384,128]{2,1,0:T(8,128)S(1)}, u32[]{:S(2)}, u32[]{:S(2)}) collective-permute-start(f32[4,384,128]{2,1,0:T(8,128)S(1)} %get-tuple-element.22.refs_2_), channel_id=1, source_target_pairs={{0,1},{1,0},{2,3},{3,2},{4,5},{5,4},{6,7},{7,6},{8,9},{9,8},{10,11... | collective-permute-start | bytes 2359304 | tf_op jit(solution)/shard_map/ppermute | solution.py:313

commit v5 on v4

--- a/solution.py
+++ b/solution.py
@@ -343,7 +343,7 @@
         input_output_aliases={2: 0},
         scratch_shapes=[pltpu.VMEM(b.shape, f32)] * 3
         + [pltpu.SemaphoreType.DMA((2, planes)), pltpu.SemaphoreType.DMA((planes,))],
-        compiler_params=params(60),
+        compiler_params=params(16),
         cost_estimate=pl.CostEstimate(flops=2 * b.size, bytes_accessed=b.size * 16, transcendentals=0),
         name="last",
     )(inv, time_term, steps)

time: 103 us -> 102 us (level)
  Pallas kernels: 24.1 us -> 22.7 us
    pallas_call x1, Pallas kernels: 4.25 us -> 2.84 us  [on_device(): pl.pallas_call(functools.partial(last_kernel, planes), out_shape=jax.Shap...]
    unnamed x28 -> x30, local copies, waits for them, and re-layouts: 8.1 us -> 8.09 us
  transfers between devices with their start and end apart: 12 -> 12, of which waited for: 7 -> 7; matrix products, arithmetic and copies ran while one was open for 1% -> 1% of each run, Pallas kernels for 19% -> 20%
where the time goes in v5:
time: 102 us; the launch traced here: 101 us
  waiting for transfers between devices  46.3 us (45%)
  Pallas kernels  22.7 us (22%)
  starting transfers between devices  22.5 us (22%)
  local copies, waits for them, and re-layouts  8.27 us (8%)
    ppermute x1, waiting for transfers between devices, on_device(): edge = lax.ppermute(jnp.stack([b[0], b[planes - 1]]), 'px', swap)  15.2 us
    ppermute x1, waiting for transfers between devices, on_device(): far_0 = lax.ppermute(onward_half, 'pz', onward)  12.5 us
    all_to_all x1, starting transfers between devices, on_device(): sent = exchange(b.reshape(count_i, share, width))  11.2 us
    all_to_all x1, waiting for transfers between devices, on_device(): time_term = exchange(applied).reshape(planes, rows, width)  8.14 us
    unnamed x30, local copies, waits for them, and re-layouts  8.09 us
    pallas_call x2, Pallas kernels, line_terms(): pl.pallas_call(kernel, out_shape=[jax.ShapeDtypeStruct(b.shape, f32), jax...  7.68 us
    all_to_all x1, waiting for transfers between devices, on_device(): sent = exchange(b.reshape(count_i, share, width))  6.32 us
    pallas_call x1, Pallas kernels, on_device(): pl.pallas_call(functools.partial(wall_kernel, dx), out_shape=[jax.ShapeDt...  5.79 us
  transfers between devices with their start and end apart: 12, of which 7 were waited for; matrix products, arithmetic and copies ran while one was open for 1% of the time, Pallas kernels for 20%

profile of v5, /device:TPU:56, one launch (start us, length us, event | category | flops | bytes accessed | tf_op | source)
XLA Modules:
  0.0 100.7 jit_solution(14223070908806312808)
XLA Ops:
  0.0 11.2 %all-to-all-start = ((f32[16,192,128]{2,1,0:T(8,128)}), f32[16,192,128]{2,1,0:T(8,128)}, u32[]{:S(2)}, u32[]{:S(2)}) async-start(f32[16,192,128]{2,1,0:T(8,128)} %bitcast.13), calls=%async_computation | async-start | bytes 3145728 | tf_op jit(solution)/shard_map/all_to_all | solution.py:237
  11.2 0.1 collective-permute-start.1
  11.3 0.3 collective-permute-start.2
  11.6 1.8 %collective-permute-start.3 = (f32[8,384,128]{2,1,0:T(8,128)S(1)}, f32[8,384,128]{2,1,0:T(8,128)}, u32[]{:S(2)}, u32[]{:S(2)}) collective-permute-start(f32[8,384,128]{2,1,0:T(8,128)S(1)} %bitcast.16), channel_id=1, source_target_pairs={{2,0},{3,1},{4,2},{5,3},{6,4},{7,5},{0,6},{1,7},{10,8},{11,9},{12,... | collective-permute-start | bytes 4718600 | tf_op jit(solution)/shard_map/ppermute | solution.py:245
  13.5 0.8 pad_maximum_fusion
  14.2 0.6 collective-permute-start
  14.8 15.2 %collective-permute-done.edge_ref = f32[2,384,128]{2,1,0:T(8,128)S(1)} collective-permute-done((f32[2,384,128]{2,1,0:T(8,128)}, f32[2,384,128]{2,1,0:T(8,128)S(1)}, u32[]{:S(2)}, u32[]{:S(2)}) %collective-permute-start) | collective-permute-done | bytes 393248 | tf_op jit(solution)/shard_map/ppermute | solution.py:250
  30.0 0.2 jit_solution_.3.scale_ref
  30.2 1.5 %copy-done.2 = bf16[768,1152]{1,0:T(8,128)(2,1)S(1)} copy-done((bf16[768,1152]{1,0:T(8,128)(2,1)S(1)}, bf16[768,1152]{1,0:T(8,128)(2,1)}, u32[]{:S(2)}) %copy-start.2) | copy-done | bytes 1769496
  31.7 1.4 %copy-done.8 = f32[1,8,384,128]{3,2,1,0:T(8,128)S(1)} copy-done((f32[1,8,384,128]{3,2,1,0:T(8,128)S(1)}, f32[1,8,384,128]{3,2,1,0:T(8,128)}, u32[]{:S(2)}) %copy-start.8) | copy-done | bytes 1572888
  33.1 1.1 %copy-done.11 = bf16[1,8,384,128]{3,2,1,0:T(8,128)(2,1)S(1)} copy-done((bf16[1,8,384,128]{3,2,1,0:T(8,128)(2,1)S(1)}, bf16[1,8,384,128]{3,2,1,0:T(8,128)(2,1)}, u32[]{:S(2)}) %copy-start.11) | copy-done | bytes 786456
  34.2 1.1 %copy-done.12 = bf16[2,768,256]{2,1,0:T(8,128)(2,1)S(1)} copy-done((bf16[2,768,256]{2,1,0:T(8,128)(2,1)S(1)}, bf16[2,768,256]{2,1,0:T(8,128)(2,1)}, u32[]{:S(2)}) %copy-start.12) | copy-done | bytes 786456
  35.4 5.8 %wall_terms.1 = (f32[8,384,128]{2,1,0:T(8,128)S(1)}, f32[8,384,128]{2,1,0:T(8,128)S(1)}, f32[8,128]{1,0:T(8,128)S(1)}) custom-call(s32[1]{0:T(128)} %bitcast.core_ref, bf16[768,1152]{1,0:T(8,128)(2,1)S(1)} %copy-done.2, bf16[2,768,256]{2,1,0:T(8,128)(2,1)S(1)} %copy-done.12, f32[2,384,128]{2,1,0:T(8,128)S(1)} %jit_solution_.3.scale_ref, ...), custom_call_target="tpu_custom_call" | custom-call | flops 2415919104 | bytes 11010048 | tf_op jit(solution)/shard_map/wall_terms/pallas_call | solution.py:261
  41.2 1.1 %copy-done.4 = f32[8,384,128]{2,1,0:T(8,128)} copy-done((f32[8,384,128]{2,1,0:T(8,128)}, f32[8,384,128]{2,1,0:T(8,128)S(1)}, u32[]{:S(2)}) %copy-start.4) | copy-done | bytes 1572888
  42.3 1.2 %copy-done.6 = f32[8,384,128]{2,1,0:T(8,128)} copy-done((f32[8,384,128]{2,1,0:T(8,128)}, f32[8,384,128]{2,1,0:T(8,128)S(1)}, u32[]{:S(2)}) %copy-start.6) | copy-done | bytes 1572888
  43.5 0.6 copy-done.13
  44.1 6.3 %all-to-all-done.in_ref = f32[16,192,128]{2,1,0:T(8,128)} async-done(((f32[16,192,128]{2,1,0:T(8,128)}), f32[16,192,128]{2,1,0:T(8,128)}, u32[]{:S(2)}, u32[]{:S(2)}) %all-to-all-start) | async-done | bytes 1572896 | tf_op jit(solution)/shard_map/all_to_all | solution.py:237
  50.4 3.0 %time_term.1 = f32[16,192,128]{2,1,0:T(8,128)} custom-call(f32[16,192,128]{2,1,0:T(8,128)} %all-to-all-done.in_ref, f32[8,128]{1,0:T(8,128)} %copy-done.13), custom_call_target="tpu_custom_call" | custom-call | flops 6291456 | bytes 3145728 | tf_op jit(solution)/shard_map/time_term/pallas_call | solution.py:300
  53.4 5.3 %all-to-all-start.1 = ((f32[16,192,128]{2,1,0:T(8,128)}), f32[16,192,128]{2,1,0:T(8,128)}, u32[]{:S(2)}, u32[]{:S(2)}) async-start(f32[16,192,128]{2,1,0:T(8,128)} %time_term.1), calls=%async_computation.1 | async-start | bytes 3145728 | tf_op jit(solution)/shard_map/all_to_all | solution.py:311
  58.9 0.5 collective-permute-start.7
  59.3 3.4 %halves.1 = (f32[4,384,128]{2,1,0:T(8,128)S(1)}, f32[4,384,128]{2,1,0:T(8,128)S(1)}) custom-call(f32[8,384,128]{2,1,0:T(8,128)} %collective-permute-done.2.before_ref.refs_0_, f32[8,384,128]{2,1,0:T(8,128)} %collective-permute-done.3.after_ref.refs_2_), custom_call_target="tpu_custom_call" | custom-call | bytes 3145728 | tf_op jit(solution)/shard_map/halves/pallas_call | solution.py:286
  62.7 0.3 collective-permute-start.4
  63.0 1.8 %collective-permute-start.5 = (f32[4,384,128]{2,1,0:T(8,128)S(1)}, f32[4,384,128]{2,1,0:T(8,128)S(1)}, u32[]{:S(2)}, u32[]{:S(2)}) collective-permute-start(f32[4,384,128]{2,1,0:T(8,128)S(1)} %get-tuple-element.18), channel_id=1, source_target_pairs={{2,0},{3,1},{4,2},{5,3},{6,4},{7,5},{0,6},{1,7},{10,8},{11,9},{12,... | collective-permute-start | bytes 2359304 | tf_op jit(solution)/shard_map/ppermute | solution.py:297
  64.9 4.7 %early_terms.1 = (f32[8,384,128]{2,1,0:T(8,128)S(1)}, f32[8,128]{1,0:T(8,128)S(1)}) custom-call(s32[1]{0:T(128)} %bitcast.core_ref, bf16[2,1536,256]{2,1,0:T(8,128)(2,1)S(1)} %copy-done.3, f32[8,384,128]{2,1,0:T(8,128)} %collective-permute-done.2.before_ref.refs_0_, f32[8,384,128]{2,1,0:T(8,128)S(1)} %collective-permute-done.6.refs_1_, ...), custom_call_target="tpu_custom_call" | custom-call | flops 2415919104 | bytes 11010048 | tf_op jit(solution)/shard_map/early_terms/pallas_call | solution.py:318
  69.6 12.5 %collective-permute-done.4.refs_0_ = f32[4,384,128]{2,1,0:T(8,128)S(1)} collective-permute-done((f32[4,384,128]{2,1,0:T(8,128)S(1)}, f32[4,384,128]{2,1,0:T(8,128)S(1)}, u32[]{:S(2)}, u32[]{:S(2)}) %collective-permute-start.4) | collective-permute-done | bytes 786464 | tf_op jit(solution)/shard_map/ppermute | solution.py:296
  82.1 1.3 %collective-permute-done.5.refs_1_ = f32[4,384,128]{2,1,0:T(8,128)S(1)} collective-permute-done((f32[4,384,128]{2,1,0:T(8,128)S(1)}, f32[4,384,128]{2,1,0:T(8,128)S(1)}, u32[]{:S(2)}, u32[]{:S(2)}) %collective-permute-start.5) | collective-permute-done | bytes 786464 | tf_op jit(solution)/shard_map/ppermute | solution.py:297
  83.4 0.5 collective-permute-start.9
  83.9 1.8 %collective-permute-done.8.refs_1_ = f32[4,384,128]{2,1,0:T(8,128)S(1)} collective-permute-done((f32[4,384,128]{2,1,0:T(8,128)S(1)}, f32[4,384,128]{2,1,0:T(8,128)S(1)}, u32[]{:S(2)}, u32[]{:S(2)}) %collective-permute-start.8) | collective-permute-done | bytes 786464 | tf_op jit(solution)/shard_map/ppermute | solution.py:313
  85.6 1.1 %collective-permute-done.9.refs_3_ = f32[4,384,128]{2,1,0:T(8,128)S(1)} collective-permute-done((f32[4,384,128]{2,1,0:T(8,128)S(1)}, f32[4,384,128]{2,1,0:T(8,128)S(1)}, u32[]{:S(2)}, u32[]{:S(2)}) %collective-permute-start.9) | collective-permute-done | bytes 786464 | tf_op jit(solution)/shard_map/ppermute | solution.py:313
  86.8 3.0 %late_terms.1 = (f32[8,384,128]{2,1,0:T(8,128)}, f32[8,128]{1,0:T(8,128)}) custom-call(s32[1]{0:T(128)} %bitcast.core_ref, bf16[2,768,256]{2,1,0:T(8,128)(2,1)S(1)} %copy-done.9, f32[4,384,128]{2,1,0:T(8,128)S(1)} %get-tuple-element.21.refs_0_, f32[4,384,128]{2,1,0:T(8,128)S(1)} %collective-permute-done.8.refs_1_, ...), custom_call_target="tpu_custom_call" | custom-call | flops 1207959552 | bytes 7864320 | tf_op jit(solution)/shard_map/late_terms/pallas_call | solution.py:318
  89.7 8.1 %all-to-all-done.1 = f32[16,192,128]{2,1,0:T(8,128)} async-done(((f32[16,192,128]{2,1,0:T(8,128)}), f32[16,192,128]{2,1,0:T(8,128)}, u32[]{:S(2)}, u32[]{:S(2)}) %all-to-all-start.1) | async-done | bytes 1572896 | tf_op jit(solution)/shard_map/all_to_all | solution.py:311
  97.9 2.8 %last.1 = f32[8,384,128]{2,1,0:T(8,128)} custom-call(f32[8,384,128]{2,1,0:T(8,128)S(1)} %copy-done.7, f32[8,384,128]{2,1,0:T(8,128)} %bitcast.9.time_ref, f32[8,384,128]{2,1,0:T(8,128)} %get-tuple-element.24.steps_ref), custom_call_target="tpu_custom_call", output_to_operand_aliasing={{}: (2, {})} | custom-call | flops 786432 | bytes 6291456 | tf_op jit(solution)/shard_map/last/pallas_call | solution.py:338
  (32 shorter events, 0.2 us)
Async XLA Ops:
  0.0 11.2 %copy-start = (f32[1,8,384,128]{3,2,1,0:T(8,128)S(1)}, f32[1,8,384,128]{3,2,1,0:T(8,128)}, u32[]{:S(2)}) copy-start(f32[1,8,384,128]{3,2,1,0:T(8,128)} %param.13) | copy-start | bytes 4718596
  0.0 50.4 %all-to-all-start = ((f32[16,192,128]{2,1,0:T(8,128)}), f32[16,192,128]{2,1,0:T(8,128)}, u32[]{:S(2)}, u32[]{:S(2)}) async-start(f32[16,192,128]{2,1,0:T(8,128)} %bitcast.13), calls=%async_computation | async-start | bytes 3145728 | tf_op jit(solution)/shard_map/all_to_all | solution.py:237
  11.2 18.8 %copy-start.14 = (f32[2,384]{1,0:T(2,128)S(1)}, f32[2,384]{1,0:T(2,128)}, u32[]{:S(2)}) copy-start(f32[2,384]{1,0:T(2,128)} %constant.31.clone) | copy-start | bytes 9220
  11.2 19.0 %copy-start.1 = (bf16[1,8,384,128]{3,2,1,0:T(8,128)(2,1)S(1)}, bf16[1,8,384,128]{3,2,1,0:T(8,128)(2,1)}, u32[]{:S(2)}) copy-start(bf16[1,8,384,128]{3,2,1,0:T(8,128)(2,1)} %param.10) | copy-start | bytes 2359300
  11.2 19.0 %copy-start.10 = (bf16[1,8,384,128]{3,2,1,0:T(8,128)(2,1)S(1)}, bf16[1,8,384,128]{3,2,1,0:T(8,128)(2,1)}, u32[]{:S(2)}) copy-start(bf16[1,8,384,128]{3,2,1,0:T(8,128)(2,1)} %param.11) | copy-start | bytes 2359300
  11.2 18.8 %collective-permute-start.1 = (f32[8,384,128]{2,1,0:T(8,128)S(1)}, f32[8,384,128]{2,1,0:T(8,128)}, u32[]{:S(2)}, u32[]{:S(2)}) collective-permute-start(f32[8,384,128]{2,1,0:T(8,128)S(1)} %bitcast.14), channel_id=1, source_target_pairs={{0,1},{1,0},{2,3},{3,2},{4,5},{5,4},{6,7},{7,6},{8,9},{9,8},{10,11... | collective-permute-start | bytes 4718600 | tf_op jit(solution)/shard_map/ppermute | solution.py:246
  11.3 47.4 %collective-permute-start.2 = (f32[8,384,128]{2,1,0:T(8,128)S(1)}, f32[8,384,128]{2,1,0:T(8,128)}, u32[]{:S(2)}, u32[]{:S(2)}) collective-permute-start(f32[8,384,128]{2,1,0:T(8,128)S(1)} %bitcast.15), channel_id=1, source_target_pairs={{0,2},{1,3},{2,4},{3,5},{4,6},{5,7},{6,0},{7,1},{8,10},{9,11},{10,... | collective-permute-start | bytes 4718600 | tf_op jit(solution)/shard_map/ppermute | solution.py:244
  11.6 47.2 %collective-permute-start.3 = (f32[8,384,128]{2,1,0:T(8,128)S(1)}, f32[8,384,128]{2,1,0:T(8,128)}, u32[]{:S(2)}, u32[]{:S(2)}) collective-permute-start(f32[8,384,128]{2,1,0:T(8,128)S(1)} %bitcast.16), channel_id=1, source_target_pairs={{2,0},{3,1},{4,2},{5,3},{6,4},{7,5},{0,6},{1,7},{10,8},{11,9},{12,... | collective-permute-start | bytes 4718600 | tf_op jit(solution)/shard_map/ppermute | solution.py:245
  14.2 15.8 %collective-permute-start = (f32[2,384,128]{2,1,0:T(8,128)}, f32[2,384,128]{2,1,0:T(8,128)S(1)}, u32[]{:S(2)}, u32[]{:S(2)}) collective-permute-start(f32[2,384,128]{2,1,0:T(8,128)} %pad_maximum_fusion), channel_id=1, source_target_pairs={{0,8},{8,0},{1,9},{9,1},{2,10},{10,2},{3,11},{11,3},{4,12},{12,4},... | collective-permute-start | bytes 1179656 | tf_op jit(solution)/shard_map/ppermute | solution.py:250
  30.2 1.5 %copy-start.2 = (bf16[768,1152]{1,0:T(8,128)(2,1)S(1)}, bf16[768,1152]{1,0:T(8,128)(2,1)}, u32[]{:S(2)}) copy-start(bf16[768,1152]{1,0:T(8,128)(2,1)} %constant.30.clone.wall_ref) | copy-start | bytes 5308420
  31.7 1.4 %copy-start.8 = (f32[1,8,384,128]{3,2,1,0:T(8,128)S(1)}, f32[1,8,384,128]{3,2,1,0:T(8,128)}, u32[]{:S(2)}) copy-start(f32[1,8,384,128]{3,2,1,0:T(8,128)} %param.14) | copy-start | bytes 4718596
  33.1 1.1 %copy-start.11 = (bf16[1,8,384,128]{3,2,1,0:T(8,128)(2,1)S(1)}, bf16[1,8,384,128]{3,2,1,0:T(8,128)(2,1)}, u32[]{:S(2)}) copy-start(bf16[1,8,384,128]{3,2,1,0:T(8,128)(2,1)} %param.12) | copy-start | bytes 2359300
  34.2 1.1 %copy-start.12 = (bf16[2,768,256]{2,1,0:T(8,128)(2,1)S(1)}, bf16[2,768,256]{2,1,0:T(8,128)(2,1)}, u32[]{:S(2)}) copy-start(bf16[2,768,256]{2,1,0:T(8,128)(2,1)} %constant.27.clone.line_ref) | copy-start | bytes 2359300
  41.2 1.1 %copy-start.4 = (f32[8,384,128]{2,1,0:T(8,128)}, f32[8,384,128]{2,1,0:T(8,128)S(1)}, u32[]{:S(2)}) copy-start(f32[8,384,128]{2,1,0:T(8,128)S(1)} %get-tuple-element.19.refs_5_) | copy-start | bytes 4718596
  42.3 1.2 %copy-start.6 = (f32[8,384,128]{2,1,0:T(8,128)}, f32[8,384,128]{2,1,0:T(8,128)S(1)}, u32[]{:S(2)}) copy-start(f32[8,384,128]{2,1,0:T(8,128)S(1)} %get-tuple-element.15.inv_ref) | copy-start | bytes 4718596
  43.5 0.6 copy-start.13
  53.4 44.5 %all-to-all-start.1 = ((f32[16,192,128]{2,1,0:T(8,128)}), f32[16,192,128]{2,1,0:T(8,128)}, u32[]{:S(2)}, u32[]{:S(2)}) async-start(f32[16,192,128]{2,1,0:T(8,128)} %time_term.1), calls=%async_computation.1 | async-start | bytes 3145728 | tf_op jit(solution)/shard_map/all_to_all | solution.py:311
  58.7 6.1 %copy-start.3 = (bf16[2,1536,256]{2,1,0:T(8,128)(2,1)S(1)}, bf16[2,1536,256]{2,1,0:T(8,128)(2,1)}, u32[]{:S(2)}) copy-start(bf16[2,1536,256]{2,1,0:T(8,128)(2,1)} %constant.28.clone.table_ref) | copy-start | bytes 4718596
  58.7 6.1 %copy-start.5 = (f32[8,384,128]{2,1,0:T(8,128)S(1)}, f32[8,384,128]{2,1,0:T(8,128)}, u32[]{:S(2)}) copy-start(f32[8,384,128]{2,1,0:T(8,128)} %copy-done.4) | copy-start | bytes 4718596
  58.7 6.1 %collective-permute-start.6 = (f32[8,384,128]{2,1,0:T(8,128)}, f32[8,384,128]{2,1,0:T(8,128)S(1)}, u32[]{:S(2)}, u32[]{:S(2)}) collective-permute-start(f32[8,384,128]{2,1,0:T(8,128)} %collective-permute-done.2.before_ref.refs_0_), channel_id=1, source_target_pairs={{0,1},{1,0},{2,3},{3,2},{4,5},{5,4},{6,7},{7,6},{8,9},{9,8},{10,11... | collective-permute-start | bytes 4718600 | tf_op jit(solution)/shard_map/ppermute | solution.py:313
  58.9 6.0 %collective-permute-start.7 = (f32[8,384,128]{2,1,0:T(8,128)}, f32[8,384,128]{2,1,0:T(8,128)S(1)}, u32[]{:S(2)}, u32[]{:S(2)}) collective-permute-start(f32[8,384,128]{2,1,0:T(8,128)} %collective-permute-done.3.after_ref.refs_2_), channel_id=1, source_target_pairs={{0,1},{1,0},{2,3},{3,2},{4,5},{5,4},{6,7},{7,6},{8,9},{9,8},{10,11... | collective-permute-start | bytes 4718600 | tf_op jit(solution)/shard_map/ppermute | solution.py:313
  62.7 19.3 %collective-permute-start.4 = (f32[4,384,128]{2,1,0:T(8,128)S(1)}, f32[4,384,128]{2,1,0:T(8,128)S(1)}, u32[]{:S(2)}, u32[]{:S(2)}) collective-permute-start(f32[4,384,128]{2,1,0:T(8,128)S(1)} %get-tuple-element.17), channel_id=1, source_target_pairs={{0,2},{1,3},{2,4},{3,5},{4,6},{5,7},{6,0},{7,1},{8,10},{9,11},{10,... | collective-permute-start | bytes 2359304 | tf_op jit(solution)/shard_map/ppermute | solution.py:296
  63.0 20.3 %collective-permute-start.5 = (f32[4,384,128]{2,1,0:T(8,128)S(1)}, f32[4,384,128]{2,1,0:T(8,128)S(1)}, u32[]{:S(2)}, u32[]{:S(2)}) collective-permute-start(f32[4,384,128]{2,1,0:T(8,128)S(1)} %get-tuple-element.18), channel_id=1, source_target_pairs={{2,0},{3,1},{4,2},{5,3},{6,4},{7,5},{0,6},{1,7},{10,8},{11,9},{12,... | collective-permute-start | bytes 2359304 | tf_op jit(solution)/shard_map/ppermute | solution.py:297
  69.6 17.2 %copy-start.9 = (bf16[2,768,256]{2,1,0:T(8,128)(2,1)S(1)}, bf16[2,768,256]{2,1,0:T(8,128)(2,1)}, u32[]{:S(2)}) copy-start(bf16[2,768,256]{2,1,0:T(8,128)(2,1)} %constant.29.clone.table_ref) | copy-start | bytes 2359300
  83.4 2.3 %collective-permute-start.8 = (f32[4,384,128]{2,1,0:T(8,128)S(1)}, f32[4,384,128]{2,1,0:T(8,128)S(1)}, u32[]{:S(2)}, u32[]{:S(2)}) collective-permute-start(f32[4,384,128]{2,1,0:T(8,128)S(1)} %get-tuple-element.21.refs_0_), channel_id=1, source_target_pairs={{0,1},{1,0},{2,3},{3,2},{4,5},{5,4},{6,7},{7,6},{8,9},{9,8},{10,11... | collective-permute-start | bytes 2359304 | tf_op jit(solution)/shard_map/ppermute | solution.py:313
  83.4 3.4 %collective-permute-start.9 = (f32[4,384,128]{2,1,0:T(8,128)S(1)}, f32[4,384,128]{2,1,0:T(8,128)S(1)}, u32[]{:S(2)}, u32[]{:S(2)}) collective-permute-start(f32[4,384,128]{2,1,0:T(8,128)S(1)} %get-tuple-element.22.refs_2_), channel_id=1, source_target_pairs={{0,1},{1,0},{2,3},{3,2},{4,5},{5,4},{6,7},{7,6},{8,9},{9,8},{10,11... | collective-permute-start | bytes 2359304 | tf_op jit(solution)/shard_map/ppermute | solution.py:313
  86.8 11.1 %copy-start.7 = (f32[8,384,128]{2,1,0:T(8,128)S(1)}, f32[8,384,128]{2,1,0:T(8,128)}, u32[]{:S(2)}) copy-start(f32[8,384,128]{2,1,0:T(8,128)} %copy-done.6) | copy-start | bytes 4718596

commit v6 on v5

--- a/solution.py
+++ b/solution.py
@@ -304,7 +304,7 @@
         out_specs=in_memory,
         scratch_shapes=[pltpu.VMEM(sent.shape, f32)] * 2
         + [pltpu.SemaphoreType.DMA((1, parts)), pltpu.SemaphoreType.DMA((parts,))],
-        compiler_params=params(60),
+        compiler_params=params(16),
         cost_estimate=pl.CostEstimate(flops=sent.size * 16, bytes_accessed=sent.size * 8, transcendentals=0),
         name="time_term",
     )(sent, token)

time: 102 us -> 102 us (level)
  transfers between devices with their start and end apart: 12 -> 12, of which waited for: 7 -> 7; matrix products, arithmetic and copies ran while one was open for 1% -> 1% of each run, Pallas kernels for 20% -> 19%
where the time goes in v6:
time: 102 us; the launch traced here: 101 us
  waiting for transfers between devices  46.8 us (46%)
  starting transfers between devices  22.5 us (22%)
  Pallas kernels  22.4 us (22%)
  local copies, waits for them, and re-layouts  8.82 us (9%)
    ppermute x1, waiting for transfers between devices, on_device(): edge = lax.ppermute(jnp.stack([b[0], b[planes - 1]]), 'px', swap)  15.2 us
    ppermute x1, waiting for transfers between devices, on_device(): far_0 = lax.ppermute(onward_half, 'pz', onward)  12.4 us
    all_to_all x1, starting transfers between devices, on_device(): sent = exchange(b.reshape(count_i, share, width))  11.2 us
    unnamed x30, local copies, waits for them, and re-layouts  8.64 us
    all_to_all x1, waiting for transfers between devices, on_device(): time_term = exchange(applied).reshape(planes, rows, width)  8.1 us
    pallas_call x2, Pallas kernels, line_terms(): pl.pallas_call(kernel, out_shape=[jax.ShapeDtypeStruct(b.shape, f32), jax...  7.78 us
    all_to_all x1, waiting for transfers between devices, on_device(): sent = exchange(b.reshape(count_i, share, width))  6.91 us
    pallas_call x1, Pallas kernels, on_device(): pl.pallas_call(functools.partial(wall_kernel, dx), out_shape=[jax.ShapeDt...  5.79 us
  transfers between devices with their start and end apart: 12, of which 7 were waited for; matrix products, arithmetic and copies ran while one was open for 1% of the time, Pallas kernels for 19%

profile of v6, /device:TPU:56, one launch (start us, length us, event | category | flops | bytes accessed | tf_op | source)
XLA Modules:
  0.0 101.5 jit_solution(8237041157735254421)
XLA Ops:
  0.0 11.2 %all-to-all-start = ((f32[16,192,128]{2,1,0:T(8,128)}), f32[16,192,128]{2,1,0:T(8,128)}, u32[]{:S(2)}, u32[]{:S(2)}) async-start(f32[16,192,128]{2,1,0:T(8,128)} %bitcast.13), calls=%async_computation | async-start | bytes 3145728 | tf_op jit(solution)/shard_map/all_to_all | solution.py:237
  11.2 0.1 collective-permute-start.1
  11.3 0.3 collective-permute-start.2
  11.6 1.8 %collective-permute-start.3 = (f32[8,384,128]{2,1,0:T(8,128)S(1)}, f32[8,384,128]{2,1,0:T(8,128)}, u32[]{:S(2)}, u32[]{:S(2)}) collective-permute-start(f32[8,384,128]{2,1,0:T(8,128)S(1)} %bitcast.16), channel_id=1, source_target_pairs={{2,0},{3,1},{4,2},{5,3},{6,4},{7,5},{0,6},{1,7},{10,8},{11,9},{12,... | collective-permute-start | bytes 4718600 | tf_op jit(solution)/shard_map/ppermute | solution.py:245
  13.5 0.8 pad_maximum_fusion
  14.2 0.6 collective-permute-start
  14.8 15.2 %collective-permute-done.edge_ref = f32[2,384,128]{2,1,0:T(8,128)S(1)} collective-permute-done((f32[2,384,128]{2,1,0:T(8,128)}, f32[2,384,128]{2,1,0:T(8,128)S(1)}, u32[]{:S(2)}, u32[]{:S(2)}) %collective-permute-start) | collective-permute-done | bytes 393248 | tf_op jit(solution)/shard_map/ppermute | solution.py:250
  30.0 0.2 jit_solution_.3.scale_ref
  30.2 1.5 %copy-done.3 = bf16[768,1152]{1,0:T(8,128)(2,1)S(1)} copy-done((bf16[768,1152]{1,0:T(8,128)(2,1)S(1)}, bf16[768,1152]{1,0:T(8,128)(2,1)}, u32[]{:S(2)}) %copy-start.3) | copy-done | bytes 1769496
  31.7 1.4 %copy-done.9 = f32[1,8,384,128]{3,2,1,0:T(8,128)S(1)} copy-done((f32[1,8,384,128]{3,2,1,0:T(8,128)S(1)}, f32[1,8,384,128]{3,2,1,0:T(8,128)}, u32[]{:S(2)}) %copy-start.9) | copy-done | bytes 1572888
  33.1 1.1 %copy-done.12 = bf16[1,8,384,128]{3,2,1,0:T(8,128)(2,1)S(1)} copy-done((bf16[1,8,384,128]{3,2,1,0:T(8,128)(2,1)S(1)}, bf16[1,8,384,128]{3,2,1,0:T(8,128)(2,1)}, u32[]{:S(2)}) %copy-start.12) | copy-done | bytes 786456
  34.2 1.1 %copy-done.13 = bf16[2,768,256]{2,1,0:T(8,128)(2,1)S(1)} copy-done((bf16[2,768,256]{2,1,0:T(8,128)(2,1)S(1)}, bf16[2,768,256]{2,1,0:T(8,128)(2,1)}, u32[]{:S(2)}) %copy-start.13) | copy-done | bytes 786456
  35.4 5.8 %wall_terms.1 = (f32[8,384,128]{2,1,0:T(8,128)S(1)}, f32[8,384,128]{2,1,0:T(8,128)S(1)}, f32[8,128]{1,0:T(8,128)S(1)}) custom-call(s32[1]{0:T(128)} %bitcast.core_ref, bf16[768,1152]{1,0:T(8,128)(2,1)S(1)} %copy-done.3, bf16[2,768,256]{2,1,0:T(8,128)(2,1)S(1)} %copy-done.13, f32[2,384,128]{2,1,0:T(8,128)S(1)} %jit_solution_.3.scale_ref, ...), custom_call_target="tpu_custom_call" | custom-call | flops 2415919104 | bytes 11010048 | tf_op jit(solution)/shard_map/wall_terms/pallas_call | solution.py:261
  41.2 1.1 %copy-done.5 = f32[8,384,128]{2,1,0:T(8,128)} copy-done((f32[8,384,128]{2,1,0:T(8,128)}, f32[8,384,128]{2,1,0:T(8,128)S(1)}, u32[]{:S(2)}) %copy-start.5) | copy-done | bytes 1572888
  42.3 1.2 %copy-done.7 = f32[8,384,128]{2,1,0:T(8,128)} copy-done((f32[8,384,128]{2,1,0:T(8,128)}, f32[8,384,128]{2,1,0:T(8,128)S(1)}, u32[]{:S(2)}) %copy-start.7) | copy-done | bytes 1572888
  43.5 6.9 %all-to-all-done.in_ref = f32[16,192,128]{2,1,0:T(8,128)} async-done(((f32[16,192,128]{2,1,0:T(8,128)}), f32[16,192,128]{2,1,0:T(8,128)}, u32[]{:S(2)}, u32[]{:S(2)}) %all-to-all-start) | async-done | bytes 1572896 | tf_op jit(solution)/shard_map/all_to_all | solution.py:237
  50.4 2.6 %time_term.1 = f32[16,192,128]{2,1,0:T(8,128)S(1)} custom-call(f32[16,192,128]{2,1,0:T(8,128)} %all-to-all-done.in_ref, f32[8,128]{1,0:T(8,128)S(1)} %get-tuple-element.16.refs_0_), custom_call_target="tpu_custom_call" | custom-call | flops 6291456 | bytes 3145728 | tf_op jit(solution)/shard_map/time_term/pallas_call | solution.py:300
  53.0 1.1 %copy-done.2 = f32[16,192,128]{2,1,0:T(8,128)} copy-done((f32[16,192,128]{2,1,0:T(8,128)}, f32[16,192,128]{2,1,0:T(8,128)S(1)}, u32[]{:S(2)}) %copy-start.2) | copy-done | bytes 1572888
  54.1 5.3 %all-to-all-start.1 = ((f32[16,192,128]{2,1,0:T(8,128)}), f32[16,192,128]{2,1,0:T(8,128)}, u32[]{:S(2)}, u32[]{:S(2)}) async-start(f32[16,192,128]{2,1,0:T(8,128)} %copy-done.2), calls=%async_computation.1 | async-start | bytes 3145728 | tf_op jit(solution)/shard_map/all_to_all | solution.py:311
  59.6 0.5 collective-permute-start.7
  60.1 3.4 %halves.1 = (f32[4,384,128]{2,1,0:T(8,128)S(1)}, f32[4,384,128]{2,1,0:T(8,128)S(1)}) custom-call(f32[8,384,128]{2,1,0:T(8,128)} %collective-permute-done.2.before_ref.refs_0_, f32[8,384,128]{2,1,0:T(8,128)} %collective-permute-done.3.after_ref.refs_2_), custom_call_target="tpu_custom_call" | custom-call | bytes 3145728 | tf_op jit(solution)/shard_map/halves/pallas_call | solution.py:286
  63.5 0.3 collective-permute-start.4
  63.8 1.8 %collective-permute-start.5 = (f32[4,384,128]{2,1,0:T(8,128)S(1)}, f32[4,384,128]{2,1,0:T(8,128)S(1)}, u32[]{:S(2)}, u32[]{:S(2)}) collective-permute-start(f32[4,384,128]{2,1,0:T(8,128)S(1)} %get-tuple-element.18), channel_id=1, source_target_pairs={{2,0},{3,1},{4,2},{5,3},{6,4},{7,5},{0,6},{1,7},{10,8},{11,9},{12,... | collective-permute-start | bytes 2359304 | tf_op jit(solution)/shard_map/ppermute | solution.py:297
  65.6 4.8 %early_terms.1 = (f32[8,384,128]{2,1,0:T(8,128)S(1)}, f32[8,128]{1,0:T(8,128)S(1)}) custom-call(s32[1]{0:T(128)} %bitcast.core_ref, bf16[2,1536,256]{2,1,0:T(8,128)(2,1)S(1)} %copy-done.4, f32[8,384,128]{2,1,0:T(8,128)} %collective-permute-done.2.before_ref.refs_0_, f32[8,384,128]{2,1,0:T(8,128)S(1)} %collective-permute-done.6.refs_1_, ...), custom_call_target="tpu_custom_call" | custom-call | flops 2415919104 | bytes 11010048 | tf_op jit(solution)/shard_map/early_terms/pallas_call | solution.py:318
  70.4 12.4 %collective-permute-done.4.refs_0_ = f32[4,384,128]{2,1,0:T(8,128)S(1)} collective-permute-done((f32[4,384,128]{2,1,0:T(8,128)S(1)}, f32[4,384,128]{2,1,0:T(8,128)S(1)}, u32[]{:S(2)}, u32[]{:S(2)}) %collective-permute-start.4) | collective-permute-done | bytes 786464 | tf_op jit(solution)/shard_map/ppermute | solution.py:296
  82.8 1.3 %collective-permute-done.5.refs_1_ = f32[4,384,128]{2,1,0:T(8,128)S(1)} collective-permute-done((f32[4,384,128]{2,1,0:T(8,128)S(1)}, f32[4,384,128]{2,1,0:T(8,128)S(1)}, u32[]{:S(2)}, u32[]{:S(2)}) %collective-permute-start.5) | collective-permute-done | bytes 786464 | tf_op jit(solution)/shard_map/ppermute | solution.py:297
  84.1 0.5 collective-permute-start.9
  84.6 1.8 %collective-permute-done.8.refs_1_ = f32[4,384,128]{2,1,0:T(8,128)S(1)} collective-permute-done((f32[4,384,128]{2,1,0:T(8,128)S(1)}, f32[4,384,128]{2,1,0:T(8,128)S(1)}, u32[]{:S(2)}, u32[]{:S(2)}) %collective-permute-start.8) | collective-permute-done | bytes 786464 | tf_op jit(solution)/shard_map/ppermute | solution.py:313
  86.4 1.1 %collective-permute-done.9.refs_3_ = f32[4,384,128]{2,1,0:T(8,128)S(1)} collective-permute-done((f32[4,384,128]{2,1,0:T(8,128)S(1)}, f32[4,384,128]{2,1,0:T(8,128)S(1)}, u32[]{:S(2)}, u32[]{:S(2)}) %collective-permute-start.9) | collective-permute-done | bytes 786464 | tf_op jit(solution)/shard_map/ppermute | solution.py:313
  87.5 3.0 %late_terms.1 = (f32[8,384,128]{2,1,0:T(8,128)}, f32[8,128]{1,0:T(8,128)}) custom-call(s32[1]{0:T(128)} %bitcast.core_ref, bf16[2,768,256]{2,1,0:T(8,128)(2,1)S(1)} %copy-done.10, f32[4,384,128]{2,1,0:T(8,128)S(1)} %get-tuple-element.21.refs_0_, f32[4,384,128]{2,1,0:T(8,128)S(1)} %collective-permute-done.8.refs_1_, ...), custom_call_target="tpu_custom_call" | custom-call | flops 1207959552 | bytes 7864320 | tf_op jit(solution)/shard_map/late_terms/pallas_call | solution.py:318
  90.5 8.1 %all-to-all-done.1 = f32[16,192,128]{2,1,0:T(8,128)} async-done(((f32[16,192,128]{2,1,0:T(8,128)}), f32[16,192,128]{2,1,0:T(8,128)}, u32[]{:S(2)}, u32[]{:S(2)}) %all-to-all-start.1) | async-done | bytes 1572896 | tf_op jit(solution)/shard_map/all_to_all | solution.py:311
  98.6 2.8 %last.1 = f32[8,384,128]{2,1,0:T(8,128)} custom-call(f32[8,384,128]{2,1,0:T(8,128)S(1)} %copy-done.8, f32[8,384,128]{2,1,0:T(8,128)} %bitcast.9.time_ref, f32[8,384,128]{2,1,0:T(8,128)} %get-tuple-element.24.steps_ref), custom_call_target="tpu_custom_call", output_to_operand_aliasing={{}: (2, {})} | custom-call | flops 786432 | bytes 6291456 | tf_op jit(solution)/shard_map/last/pallas_call | solution.py:338
  (32 shorter events, 0.2 us)
Async XLA Ops:
  0.0 11.2 %copy-start = (f32[1,8,384,128]{3,2,1,0:T(8,128)S(1)}, f32[1,8,384,128]{3,2,1,0:T(8,128)}, u32[]{:S(2)}) copy-start(f32[1,8,384,128]{3,2,1,0:T(8,128)} %param.13) | copy-start | bytes 4718596
  0.0 50.4 %all-to-all-start = ((f32[16,192,128]{2,1,0:T(8,128)}), f32[16,192,128]{2,1,0:T(8,128)}, u32[]{:S(2)}, u32[]{:S(2)}) async-start(f32[16,192,128]{2,1,0:T(8,128)} %bitcast.13), calls=%async_computation | async-start | bytes 3145728 | tf_op jit(solution)/shard_map/all_to_all | solution.py:237
  11.2 18.8 %copy-start.14 = (f32[2,384]{1,0:T(2,128)S(1)}, f32[2,384]{1,0:T(2,128)}, u32[]{:S(2)}) copy-start(f32[2,384]{1,0:T(2,128)} %constant.31.clone) | copy-start | bytes 9220
  11.2 19.0 %copy-start.1 = (bf16[1,8,384,128]{3,2,1,0:T(8,128)(2,1)S(1)}, bf16[1,8,384,128]{3,2,1,0:T(8,128)(2,1)}, u32[]{:S(2)}) copy-start(bf16[1,8,384,128]{3,2,1,0:T(8,128)(2,1)} %param.10) | copy-start | bytes 2359300
  11.2 19.0 %copy-start.11 = (bf16[1,8,384,128]{3,2,1,0:T(8,128)(2,1)S(1)}, bf16[1,8,384,128]{3,2,1,0:T(8,128)(2,1)}, u32[]{:S(2)}) copy-start(bf16[1,8,384,128]{3,2,1,0:T(8,128)(2,1)} %param.11) | copy-start | bytes 2359300
  11.2 18.8 %collective-permute-start.1 = (f32[8,384,128]{2,1,0:T(8,128)S(1)}, f32[8,384,128]{2,1,0:T(8,128)}, u32[]{:S(2)}, u32[]{:S(2)}) collective-permute-start(f32[8,384,128]{2,1,0:T(8,128)S(1)} %bitcast.14), channel_id=1, source_target_pairs={{0,1},{1,0},{2,3},{3,2},{4,5},{5,4},{6,7},{7,6},{8,9},{9,8},{10,11... | collective-permute-start | bytes 4718600 | tf_op jit(solution)/shard_map/ppermute | solution.py:246
  11.3 48.2 %collective-permute-start.2 = (f32[8,384,128]{2,1,0:T(8,128)S(1)}, f32[8,384,128]{2,1,0:T(8,128)}, u32[]{:S(2)}, u32[]{:S(2)}) collective-permute-start(f32[8,384,128]{2,1,0:T(8,128)S(1)} %bitcast.15), channel_id=1, source_target_pairs={{0,2},{1,3},{2,4},{3,5},{4,6},{5,7},{6,0},{7,1},{8,10},{9,11},{10,... | collective-permute-start | bytes 4718600 | tf_op jit(solution)/shard_map/ppermute | solution.py:244
  11.6 48.0 %collective-permute-start.3 = (f32[8,384,128]{2,1,0:T(8,128)S(1)}, f32[8,384,128]{2,1,0:T(8,128)}, u32[]{:S(2)}, u32[]{:S(2)}) collective-permute-start(f32[8,384,128]{2,1,0:T(8,128)S(1)} %bitcast.16), channel_id=1, source_target_pairs={{2,0},{3,1},{4,2},{5,3},{6,4},{7,5},{0,6},{1,7},{10,8},{11,9},{12,... | collective-permute-start | bytes 4718600 | tf_op jit(solution)/shard_map/ppermute | solution.py:245
  14.2 15.8 %collective-permute-start = (f32[2,384,128]{2,1,0:T(8,128)}, f32[2,384,128]{2,1,0:T(8,128)S(1)}, u32[]{:S(2)}, u32[]{:S(2)}) collective-permute-start(f32[2,384,128]{2,1,0:T(8,128)} %pad_maximum_fusion), channel_id=1, source_target_pairs={{0,8},{8,0},{1,9},{9,1},{2,10},{10,2},{3,11},{11,3},{4,12},{12,4},... | collective-permute-start | bytes 1179656 | tf_op jit(solution)/shard_map/ppermute | solution.py:250
  30.2 1.5 %copy-start.3 = (bf16[768,1152]{1,0:T(8,128)(2,1)S(1)}, bf16[768,1152]{1,0:T(8,128)(2,1)}, u32[]{:S(2)}) copy-start(bf16[768,1152]{1,0:T(8,128)(2,1)} %constant.30.clone.wall_ref) | copy-start | bytes 5308420
  31.7 1.4 %copy-start.9 = (f32[1,8,384,128]{3,2,1,0:T(8,128)S(1)}, f32[1,8,384,128]{3,2,1,0:T(8,128)}, u32[]{:S(2)}) copy-start(f32[1,8,384,128]{3,2,1,0:T(8,128)} %param.14) | copy-start | bytes 4718596
  33.1 1.1 %copy-start.12 = (bf16[1,8,384,128]{3,2,1,0:T(8,128)(2,1)S(1)}, bf16[1,8,384,128]{3,2,1,0:T(8,128)(2,1)}, u32[]{:S(2)}) copy-start(bf16[1,8,384,128]{3,2,1,0:T(8,128)(2,1)} %param.12) | copy-start | bytes 2359300
  34.2 1.1 %copy-start.13 = (bf16[2,768,256]{2,1,0:T(8,128)(2,1)S(1)}, bf16[2,768,256]{2,1,0:T(8,128)(2,1)}, u32[]{:S(2)}) copy-start(bf16[2,768,256]{2,1,0:T(8,128)(2,1)} %constant.27.clone.line_ref) | copy-start | bytes 2359300
  41.2 1.1 %copy-start.5 = (f32[8,384,128]{2,1,0:T(8,128)}, f32[8,384,128]{2,1,0:T(8,128)S(1)}, u32[]{:S(2)}) copy-start(f32[8,384,128]{2,1,0:T(8,128)S(1)} %get-tuple-element.19.refs_5_) | copy-start | bytes 4718596
  42.3 1.2 %copy-start.7 = (f32[8,384,128]{2,1,0:T(8,128)}, f32[8,384,128]{2,1,0:T(8,128)S(1)}, u32[]{:S(2)}) copy-start(f32[8,384,128]{2,1,0:T(8,128)S(1)} %get-tuple-element.15.inv_ref) | copy-start | bytes 4718596
  53.0 1.1 %copy-start.2 = (f32[16,192,128]{2,1,0:T(8,128)}, f32[16,192,128]{2,1,0:T(8,128)S(1)}, u32[]{:S(2)}) copy-start(f32[16,192,128]{2,1,0:T(8,128)S(1)} %time_term.1) | copy-start | bytes 4718596
  54.1 44.5 %all-to-all-start.1 = ((f32[16,192,128]{2,1,0:T(8,128)}), f32[16,192,128]{2,1,0:T(8,128)}, u32[]{:S(2)}, u32[]{:S(2)}) async-start(f32[16,192,128]{2,1,0:T(8,128)} %copy-done.2), calls=%async_computation.1 | async-start | bytes 3145728 | tf_op jit(solution)/shard_map/all_to_all | solution.py:311
  59.5 6.1 %copy-start.4 = (bf16[2,1536,256]{2,1,0:T(8,128)(2,1)S(1)}, bf16[2,1536,256]{2,1,0:T(8,128)(2,1)}, u32[]{:S(2)}) copy-start(bf16[2,1536,256]{2,1,0:T(8,128)(2,1)} %constant.28.clone.table_ref) | copy-start | bytes 4718596
  59.5 6.1 %copy-start.6 = (f32[8,384,128]{2,1,0:T(8,128)S(1)}, f32[8,384,128]{2,1,0:T(8,128)}, u32[]{:S(2)}) copy-start(f32[8,384,128]{2,1,0:T(8,128)} %copy-done.5) | copy-start | bytes 4718596
  59.5 6.1 %collective-permute-start.6 = (f32[8,384,128]{2,1,0:T(8,128)}, f32[8,384,128]{2,1,0:T(8,128)S(1)}, u32[]{:S(2)}, u32[]{:S(2)}) collective-permute-start(f32[8,384,128]{2,1,0:T(8,128)} %collective-permute-done.2.before_ref.refs_0_), channel_id=1, source_target_pairs={{0,1},{1,0},{2,3},{3,2},{4,5},{5,4},{6,7},{7,6},{8,9},{9,8},{10,11... | collective-permute-start | bytes 4718600 | tf_op jit(solution)/shard_map/ppermute | solution.py:313
  59.6 6.0 %collective-permute-start.7 = (f32[8,384,128]{2,1,0:T(8,128)}, f32[8,384,128]{2,1,0:T(8,128)S(1)}, u32[]{:S(2)}, u32[]{:S(2)}) collective-permute-start(f32[8,384,128]{2,1,0:T(8,128)} %collective-permute-done.3.after_ref.refs_2_), channel_id=1, source_target_pairs={{0,1},{1,0},{2,3},{3,2},{4,5},{5,4},{6,7},{7,6},{8,9},{9,8},{10,11... | collective-permute-start | bytes 4718600 | tf_op jit(solution)/shard_map/ppermute | solution.py:313
  63.5 19.3 %collective-permute-start.4 = (f32[4,384,128]{2,1,0:T(8,128)S(1)}, f32[4,384,128]{2,1,0:T(8,128)S(1)}, u32[]{:S(2)}, u32[]{:S(2)}) collective-permute-start(f32[4,384,128]{2,1,0:T(8,128)S(1)} %get-tuple-element.17), channel_id=1, source_target_pairs={{0,2},{1,3},{2,4},{3,5},{4,6},{5,7},{6,0},{7,1},{8,10},{9,11},{10,... | collective-permute-start | bytes 2359304 | tf_op jit(solution)/shard_map/ppermute | solution.py:296
  63.8 20.3 %collective-permute-start.5 = (f32[4,384,128]{2,1,0:T(8,128)S(1)}, f32[4,384,128]{2,1,0:T(8,128)S(1)}, u32[]{:S(2)}, u32[]{:S(2)}) collective-permute-start(f32[4,384,128]{2,1,0:T(8,128)S(1)} %get-tuple-element.18), channel_id=1, source_target_pairs={{2,0},{3,1},{4,2},{5,3},{6,4},{7,5},{0,6},{1,7},{10,8},{11,9},{12,... | collective-permute-start | bytes 2359304 | tf_op jit(solution)/shard_map/ppermute | solution.py:297
  70.4 17.1 %copy-start.10 = (bf16[2,768,256]{2,1,0:T(8,128)(2,1)S(1)}, bf16[2,768,256]{2,1,0:T(8,128)(2,1)}, u32[]{:S(2)}) copy-start(bf16[2,768,256]{2,1,0:T(8,128)(2,1)} %constant.29.clone.table_ref) | copy-start | bytes 2359300
  84.1 2.3 %collective-permute-start.8 = (f32[4,384,128]{2,1,0:T(8,128)S(1)}, f32[4,384,128]{2,1,0:T(8,128)S(1)}, u32[]{:S(2)}, u32[]{:S(2)}) collective-permute-start(f32[4,384,128]{2,1,0:T(8,128)S(1)} %get-tuple-element.21.refs_0_), channel_id=1, source_target_pairs={{0,1},{1,0},{2,3},{3,2},{4,5},{5,4},{6,7},{7,6},{8,9},{9,8},{10,11... | collective-permute-start | bytes 2359304 | tf_op jit(solution)/shard_map/ppermute | solution.py:313
  84.1 3.4 %collective-permute-start.9 = (f32[4,384,128]{2,1,0:T(8,128)S(1)}, f32[4,384,128]{2,1,0:T(8,128)S(1)}, u32[]{:S(2)}, u32[]{:S(2)}) collective-permute-start(f32[4,384,128]{2,1,0:T(8,128)S(1)} %get-tuple-element.22.refs_2_), channel_id=1, source_target_pairs={{0,1},{1,0},{2,3},{3,2},{4,5},{5,4},{6,7},{7,6},{8,9},{9,8},{10,11... | collective-permute-start | bytes 2359304 | tf_op jit(solution)/shard_map/ppermute | solution.py:313
  87.5 11.1 %copy-start.8 = (f32[8,384,128]{2,1,0:T(8,128)S(1)}, f32[8,384,128]{2,1,0:T(8,128)}, u32[]{:S(2)}) copy-start(f32[8,384,128]{2,1,0:T(8,128)} %copy-done.7) | copy-start | bytes 4718596

commit v7 on v5

--- a/solution.py
+++ b/solution.py
@@ -153,8 +153,8 @@
 
 
 class TimePart:
-    def __init__(self, weights, size, source, result):
-        self.weights, self.size, self.source, self.result = weights, size, source, result
+    def __init__(self, weights, order, size, source, result):
+        self.weights, self.order, self.size, self.source, self.result = weights, order, size, source, result
 
     def where(self, k):
         return (slice(None), pl.ds(k * self.size, self.size))
@@ -165,7 +165,7 @@
 
         def body(step, carry):
             rows = pl.ds(pl.multiple_of(k * self.size + step * 8, 8), 8)
-            b = [self.source[i, rows, :] for i in range(count)]
+            b = [self.source[self.order.index(i), rows, :] for i in range(count)]
             totals = [weights[half] * b[(i + half) % count] for i in range(count)]
             for i in range(half):
                 for d in range(1, half):
@@ -173,7 +173,7 @@
                     totals[i] = totals[i] + weights[d] * differ
                     totals[i + half] = totals[i + half] - weights[half - d] * differ
             for i in range(count):
-                self.result[i, rows, :] = totals[i]
+                self.result[self.order.index(i), rows, :] = totals[i]
             return carry
 
         lax.fori_loop(0, self.size // 8, body, 0)
@@ -191,9 +191,9 @@
         self.result[at] = (self.steps[at] - self.time[at]) * self.inv[at]
 
 
-def time_kernel(weights, parts, in_ref, *refs):
+def time_kernel(weights, order, parts, in_ref, *refs):
     out_ref, source, result, in_sems, out_sems = refs[-5:]
-    work = TimePart(weights, in_ref.shape[1] // parts, source, result)
+    work = TimePart(weights, order, in_ref.shape[1] // parts, source, result)
     in_parts(parts, [in_ref], [source], result, out_ref, in_sems, out_sems, work)
 
 
@@ -233,7 +233,10 @@
     b, u, v, w, n = (x[0] for x in (adjoint_buoy, stream_vel, normal_vel, span_vel, adjoint_normal))
 
     share = planes * rows // count_i
-    exchange = functools.partial(lax.all_to_all, axis_name="inst", split_axis=0, concat_axis=0, tiled=True)
+    order = [i for i in reversed(range(count_i))]
+    exchange = functools.partial(
+        lax.all_to_all, axis_name="inst", split_axis=0, concat_axis=0, axis_index_groups=[order], tiled=True
+    )
     sent = exchange(b.reshape(count_i, share, width))
 
     members = range(count_x)
@@ -298,7 +301,7 @@
 
     parts = 8
     applied = pl.pallas_call(
-        functools.partial(time_kernel, weights, parts),
+        functools.partial(time_kernel, weights, order, parts),
         out_shape=jax.ShapeDtypeStruct(sent.shape, f32),
         in_specs=[in_memory, anywhere],
         out_specs=in_memory,

time: 102 us -> 101 us (level)
  waiting for transfers between devices: 46.3 us -> 40.8 us
  starting transfers between devices: 22.5 us -> 26.4 us
    all_to_all x1, waiting for transfers between devices: 6.32 us -> 2.93 us  [on_device(): sent = exchange(b.reshape(count_i, share, width))]
    all_to_all x1, waiting for transfers between devices: 8.14 us -> 5.1 us  [on_device(): time_term = exchange(applied).reshape(planes, rows, width)]
    all_to_all x1, starting transfers between devices: 5.35 us -> 8.17 us  [on_device(): time_term = exchange(applied).reshape(planes, rows, width)]
    all_to_all x1, starting transfers between devices: 11.2 us -> 12.2 us  [on_device(): sent = exchange(b.reshape(count_i, share, width))]
where the time goes in v7:
time: 101 us; the launch traced here: 99.1 us
  waiting for transfers between devices  40.8 us (40%)
  starting transfers between devices  26.4 us (26%)
  Pallas kernels  22.7 us (22%)
  local copies, waits for them, and re-layouts  8.27 us (8%)
    ppermute x1, waiting for transfers between devices, on_device(): edge = lax.ppermute(jnp.stack([b[0], b[planes - 1]]), 'px', swap)  16.1 us
    ppermute x1, waiting for transfers between devices, on_device(): far_0 = lax.ppermute(onward_half, 'pz', onward)  12.5 us
    all_to_all x1, starting transfers between devices, on_device(): sent = exchange(b.reshape(count_i, share, width))  12.2 us
    all_to_all x1, starting transfers between devices, on_device(): time_term = exchange(applied).reshape(planes, rows, width)  8.17 us
    unnamed x30, local copies, waits for them, and re-layouts  8.09 us
    pallas_call x2, Pallas kernels, line_terms(): pl.pallas_call(kernel, out_shape=[jax.ShapeDtypeStruct(b.shape, f32), jax...  7.68 us
    pallas_call x1, Pallas kernels, on_device(): pl.pallas_call(functools.partial(wall_kernel, dx), out_shape=[jax.ShapeDt...  5.79 us
    all_to_all x1, waiting for transfers between devices, on_device(): time_term = exchange(applied).reshape(planes, rows, width)  5.1 us
  transfers between devices with their start and end apart: 12, of which 7 were waited for; matrix products, arithmetic and copies ran while one was open for 1% of the time, Pallas kernels for 20%

profile of v7, /device:TPU:56, one launch (start us, length us, event | category | flops | bytes accessed | tf_op | source)
XLA Modules:
  0.0 99.1 jit_solution(2196744117336678559)
XLA Ops:
  0.0 12.2 %all-to-all-start = ((f32[16,192,128]{2,1,0:T(8,128)}), f32[16,192,128]{2,1,0:T(8,128)}, u32[]{:S(2)}, u32[]{:S(2)}) async-start(f32[16,192,128]{2,1,0:T(8,128)} %bitcast.13), calls=%async_computation | async-start | bytes 3145728 | tf_op jit(solution)/shard_map/all_to_all | solution.py:240
  12.3 0.1 collective-permute-start.1
  12.4 0.3 collective-permute-start.2
  12.7 1.8 %collective-permute-start.3 = (f32[8,384,128]{2,1,0:T(8,128)S(1)}, f32[8,384,128]{2,1,0:T(8,128)}, u32[]{:S(2)}, u32[]{:S(2)}) collective-permute-start(f32[8,384,128]{2,1,0:T(8,128)S(1)} %bitcast.16), channel_id=1, source_target_pairs={{2,0},{3,1},{4,2},{5,3},{6,4},{7,5},{0,6},{1,7},{10,8},{11,9},{12,... | collective-permute-start | bytes 4718600 | tf_op jit(solution)/shard_map/ppermute | solution.py:248
  14.5 0.8 pad_maximum_fusion
  15.3 0.6 collective-permute-start
  15.9 16.1 %collective-permute-done.edge_ref = f32[2,384,128]{2,1,0:T(8,128)S(1)} collective-permute-done((f32[2,384,128]{2,1,0:T(8,128)}, f32[2,384,128]{2,1,0:T(8,128)S(1)}, u32[]{:S(2)}, u32[]{:S(2)}) %collective-permute-start) | collective-permute-done | bytes 393248 | tf_op jit(solution)/shard_map/ppermute | solution.py:253
  32.0 0.2 jit_solution_.3.scale_ref
  32.2 1.5 %copy-done.2 = bf16[768,1152]{1,0:T(8,128)(2,1)S(1)} copy-done((bf16[768,1152]{1,0:T(8,128)(2,1)S(1)}, bf16[768,1152]{1,0:T(8,128)(2,1)}, u32[]{:S(2)}) %copy-start.2) | copy-done | bytes 1769496
  33.7 1.4 %copy-done.8 = f32[1,8,384,128]{3,2,1,0:T(8,128)S(1)} copy-done((f32[1,8,384,128]{3,2,1,0:T(8,128)S(1)}, f32[1,8,384,128]{3,2,1,0:T(8,128)}, u32[]{:S(2)}) %copy-start.8) | copy-done | bytes 1572888
  35.1 1.1 %copy-done.11 = bf16[1,8,384,128]{3,2,1,0:T(8,128)(2,1)S(1)} copy-done((bf16[1,8,384,128]{3,2,1,0:T(8,128)(2,1)S(1)}, bf16[1,8,384,128]{3,2,1,0:T(8,128)(2,1)}, u32[]{:S(2)}) %copy-start.11) | copy-done | bytes 786456
  36.2 1.1 %copy-done.12 = bf16[2,768,256]{2,1,0:T(8,128)(2,1)S(1)} copy-done((bf16[2,768,256]{2,1,0:T(8,128)(2,1)S(1)}, bf16[2,768,256]{2,1,0:T(8,128)(2,1)}, u32[]{:S(2)}) %copy-start.12) | copy-done | bytes 786456
  37.3 5.8 %wall_terms.1 = (f32[8,384,128]{2,1,0:T(8,128)S(1)}, f32[8,384,128]{2,1,0:T(8,128)S(1)}, f32[8,128]{1,0:T(8,128)S(1)}) custom-call(s32[1]{0:T(128)} %bitcast.core_ref, bf16[768,1152]{1,0:T(8,128)(2,1)S(1)} %copy-done.2, bf16[2,768,256]{2,1,0:T(8,128)(2,1)S(1)} %copy-done.12, f32[2,384,128]{2,1,0:T(8,128)S(1)} %jit_solution_.3.scale_ref, ...), custom_call_target="tpu_custom_call" | custom-call | flops 2415919104 | bytes 11010048 | tf_op jit(solution)/shard_map/wall_terms/pallas_call | solution.py:264
  43.2 1.1 %copy-done.4 = f32[8,384,128]{2,1,0:T(8,128)} copy-done((f32[8,384,128]{2,1,0:T(8,128)}, f32[8,384,128]{2,1,0:T(8,128)S(1)}, u32[]{:S(2)}) %copy-start.4) | copy-done | bytes 1572888
  44.3 1.2 %copy-done.6 = f32[8,384,128]{2,1,0:T(8,128)} copy-done((f32[8,384,128]{2,1,0:T(8,128)}, f32[8,384,128]{2,1,0:T(8,128)S(1)}, u32[]{:S(2)}) %copy-start.6) | copy-done | bytes 1572888
  45.5 0.6 copy-done.13
  46.1 2.9 %all-to-all-done.in_ref = f32[16,192,128]{2,1,0:T(8,128)} async-done(((f32[16,192,128]{2,1,0:T(8,128)}), f32[16,192,128]{2,1,0:T(8,128)}, u32[]{:S(2)}, u32[]{:S(2)}) %all-to-all-start) | async-done | bytes 1572896 | tf_op jit(solution)/shard_map/all_to_all | solution.py:240
  49.0 3.0 %time_term.1 = f32[16,192,128]{2,1,0:T(8,128)} custom-call(f32[16,192,128]{2,1,0:T(8,128)} %all-to-all-done.in_ref, f32[8,128]{1,0:T(8,128)} %copy-done.13), custom_call_target="tpu_custom_call" | custom-call | flops 6291456 | bytes 3145728 | tf_op jit(solution)/shard_map/time_term/pallas_call | solution.py:303
  52.0 8.2 %all-to-all-start.1 = ((f32[16,192,128]{2,1,0:T(8,128)}), f32[16,192,128]{2,1,0:T(8,128)}, u32[]{:S(2)}, u32[]{:S(2)}) async-start(f32[16,192,128]{2,1,0:T(8,128)} %time_term.1), calls=%async_computation.1 | async-start | bytes 3145728 | tf_op jit(solution)/shard_map/all_to_all | solution.py:314
  60.3 0.5 collective-permute-start.7
  60.8 3.4 %halves.1 = (f32[4,384,128]{2,1,0:T(8,128)S(1)}, f32[4,384,128]{2,1,0:T(8,128)S(1)}) custom-call(f32[8,384,128]{2,1,0:T(8,128)} %collective-permute-done.2.before_ref.refs_0_, f32[8,384,128]{2,1,0:T(8,128)} %collective-permute-done.3.after_ref.refs_2_), custom_call_target="tpu_custom_call" | custom-call | bytes 3145728 | tf_op jit(solution)/shard_map/halves/pallas_call | solution.py:289
  64.2 0.3 collective-permute-start.4
  64.5 1.8 %collective-permute-start.5 = (f32[4,384,128]{2,1,0:T(8,128)S(1)}, f32[4,384,128]{2,1,0:T(8,128)S(1)}, u32[]{:S(2)}, u32[]{:S(2)}) collective-permute-start(f32[4,384,128]{2,1,0:T(8,128)S(1)} %get-tuple-element.18), channel_id=1, source_target_pairs={{2,0},{3,1},{4,2},{5,3},{6,4},{7,5},{0,6},{1,7},{10,8},{11,9},{12,... | collective-permute-start | bytes 2359304 | tf_op jit(solution)/shard_map/ppermute | solution.py:300
  66.3 4.7 %early_terms.1 = (f32[8,384,128]{2,1,0:T(8,128)S(1)}, f32[8,128]{1,0:T(8,128)S(1)}) custom-call(s32[1]{0:T(128)} %bitcast.core_ref, bf16[2,1536,256]{2,1,0:T(8,128)(2,1)S(1)} %copy-done.3, f32[8,384,128]{2,1,0:T(8,128)} %collective-permute-done.2.before_ref.refs_0_, f32[8,384,128]{2,1,0:T(8,128)S(1)} %collective-permute-done.6.refs_1_, ...), custom_call_target="tpu_custom_call" | custom-call | flops 2415919104 | bytes 11010048 | tf_op jit(solution)/shard_map/early_terms/pallas_call | solution.py:321
  71.0 12.5 %collective-permute-done.4.refs_0_ = f32[4,384,128]{2,1,0:T(8,128)S(1)} collective-permute-done((f32[4,384,128]{2,1,0:T(8,128)S(1)}, f32[4,384,128]{2,1,0:T(8,128)S(1)}, u32[]{:S(2)}, u32[]{:S(2)}) %collective-permute-start.4) | collective-permute-done | bytes 786464 | tf_op jit(solution)/shard_map/ppermute | solution.py:299
  83.5 1.3 %collective-permute-done.5.refs_1_ = f32[4,384,128]{2,1,0:T(8,128)S(1)} collective-permute-done((f32[4,384,128]{2,1,0:T(8,128)S(1)}, f32[4,384,128]{2,1,0:T(8,128)S(1)}, u32[]{:S(2)}, u32[]{:S(2)}) %collective-permute-start.5) | collective-permute-done | bytes 786464 | tf_op jit(solution)/shard_map/ppermute | solution.py:300
  84.8 0.5 collective-permute-start.9
  85.3 1.8 %collective-permute-done.8.refs_1_ = f32[4,384,128]{2,1,0:T(8,128)S(1)} collective-permute-done((f32[4,384,128]{2,1,0:T(8,128)S(1)}, f32[4,384,128]{2,1,0:T(8,128)S(1)}, u32[]{:S(2)}, u32[]{:S(2)}) %collective-permute-start.8) | collective-permute-done | bytes 786464 | tf_op jit(solution)/shard_map/ppermute | solution.py:316
  87.1 1.1 %collective-permute-done.9.refs_3_ = f32[4,384,128]{2,1,0:T(8,128)S(1)} collective-permute-done((f32[4,384,128]{2,1,0:T(8,128)S(1)}, f32[4,384,128]{2,1,0:T(8,128)S(1)}, u32[]{:S(2)}, u32[]{:S(2)}) %collective-permute-start.9) | collective-permute-done | bytes 786464 | tf_op jit(solution)/shard_map/ppermute | solution.py:316
  88.2 3.0 %late_terms.1 = (f32[8,384,128]{2,1,0:T(8,128)}, f32[8,128]{1,0:T(8,128)}) custom-call(s32[1]{0:T(128)} %bitcast.core_ref, bf16[2,768,256]{2,1,0:T(8,128)(2,1)S(1)} %copy-done.9, f32[4,384,128]{2,1,0:T(8,128)S(1)} %get-tuple-element.21.refs_0_, f32[4,384,128]{2,1,0:T(8,128)S(1)} %collective-permute-done.8.refs_1_, ...), custom_call_target="tpu_custom_call" | custom-call | flops 1207959552 | bytes 7864320 | tf_op jit(solution)/shard_map/late_terms/pallas_call | solution.py:321
  91.2 5.1 %all-to-all-done.1 = f32[16,192,128]{2,1,0:T(8,128)} async-done(((f32[16,192,128]{2,1,0:T(8,128)}), f32[16,192,128]{2,1,0:T(8,128)}, u32[]{:S(2)}, u32[]{:S(2)}) %all-to-all-start.1) | async-done | bytes 1572896 | tf_op jit(solution)/shard_map/all_to_all | solution.py:314
  96.3 2.8 %last.1 = f32[8,384,128]{2,1,0:T(8,128)} custom-call(f32[8,384,128]{2,1,0:T(8,128)S(1)} %copy-done.7, f32[8,384,128]{2,1,0:T(8,128)} %bitcast.9.time_ref, f32[8,384,128]{2,1,0:T(8,128)} %get-tuple-element.24.steps_ref), custom_call_target="tpu_custom_call", output_to_operand_aliasing={{}: (2, {})} | custom-call | flops 786432 | bytes 6291456 | tf_op jit(solution)/shard_map/last/pallas_call | solution.py:341
  (32 shorter events, 0.2 us)
Async XLA Ops:
  0.0 12.3 %copy-start = (f32[1,8,384,128]{3,2,1,0:T(8,128)S(1)}, f32[1,8,384,128]{3,2,1,0:T(8,128)}, u32[]{:S(2)}) copy-start(f32[1,8,384,128]{3,2,1,0:T(8,128)} %param.13) | copy-start | bytes 4718596
  0.0 49.0 %all-to-all-start = ((f32[16,192,128]{2,1,0:T(8,128)}), f32[16,192,128]{2,1,0:T(8,128)}, u32[]{:S(2)}, u32[]{:S(2)}) async-start(f32[16,192,128]{2,1,0:T(8,128)} %bitcast.13), calls=%async_computation | async-start | bytes 3145728 | tf_op jit(solution)/shard_map/all_to_all | solution.py:240
  12.2 19.8 %copy-start.14 = (f32[2,384]{1,0:T(2,128)S(1)}, f32[2,384]{1,0:T(2,128)}, u32[]{:S(2)}) copy-start(f32[2,384]{1,0:T(2,128)} %constant.31.clone) | copy-start | bytes 9220
  12.2 19.9 %copy-start.1 = (bf16[1,8,384,128]{3,2,1,0:T(8,128)(2,1)S(1)}, bf16[1,8,384,128]{3,2,1,0:T(8,128)(2,1)}, u32[]{:S(2)}) copy-start(bf16[1,8,384,128]{3,2,1,0:T(8,128)(2,1)} %param.10) | copy-start | bytes 2359300
  12.2 19.9 %copy-start.10 = (bf16[1,8,384,128]{3,2,1,0:T(8,128)(2,1)S(1)}, bf16[1,8,384,128]{3,2,1,0:T(8,128)(2,1)}, u32[]{:S(2)}) copy-start(bf16[1,8,384,128]{3,2,1,0:T(8,128)(2,1)} %param.11) | copy-start | bytes 2359300
  12.3 19.7 %collective-permute-start.1 = (f32[8,384,128]{2,1,0:T(8,128)S(1)}, f32[8,384,128]{2,1,0:T(8,128)}, u32[]{:S(2)}, u32[]{:S(2)}) collective-permute-start(f32[8,384,128]{2,1,0:T(8,128)S(1)} %bitcast.14), channel_id=1, source_target_pairs={{0,1},{1,0},{2,3},{3,2},{4,5},{5,4},{6,7},{7,6},{8,9},{9,8},{10,11... | collective-permute-start | bytes 4718600 | tf_op jit(solution)/shard_map/ppermute | solution.py:249
  12.4 47.8 %collective-permute-start.2 = (f32[8,384,128]{2,1,0:T(8,128)S(1)}, f32[8,384,128]{2,1,0:T(8,128)}, u32[]{:S(2)}, u32[]{:S(2)}) collective-permute-start(f32[8,384,128]{2,1,0:T(8,128)S(1)} %bitcast.15), channel_id=1, source_target_pairs={{0,2},{1,3},{2,4},{3,5},{4,6},{5,7},{6,0},{7,1},{8,10},{9,11},{10,... | collective-permute-start | bytes 4718600 | tf_op jit(solution)/shard_map/ppermute | solution.py:247
  12.7 47.6 %collective-permute-start.3 = (f32[8,384,128]{2,1,0:T(8,128)S(1)}, f32[8,384,128]{2,1,0:T(8,128)}, u32[]{:S(2)}, u32[]{:S(2)}) collective-permute-start(f32[8,384,128]{2,1,0:T(8,128)S(1)} %bitcast.16), channel_id=1, source_target_pairs={{2,0},{3,1},{4,2},{5,3},{6,4},{7,5},{0,6},{1,7},{10,8},{11,9},{12,... | collective-permute-start | bytes 4718600 | tf_op jit(solution)/shard_map/ppermute | solution.py:248
  15.3 16.7 %collective-permute-start = (f32[2,384,128]{2,1,0:T(8,128)}, f32[2,384,128]{2,1,0:T(8,128)S(1)}, u32[]{:S(2)}, u32[]{:S(2)}) collective-permute-start(f32[2,384,128]{2,1,0:T(8,128)} %pad_maximum_fusion), channel_id=1, source_target_pairs={{0,8},{8,0},{1,9},{9,1},{2,10},{10,2},{3,11},{11,3},{4,12},{12,4},... | collective-permute-start | bytes 1179656 | tf_op jit(solution)/shard_map/ppermute | solution.py:253
  32.2 1.5 %copy-start.2 = (bf16[768,1152]{1,0:T(8,128)(2,1)S(1)}, bf16[768,1152]{1,0:T(8,128)(2,1)}, u32[]{:S(2)}) copy-start(bf16[768,1152]{1,0:T(8,128)(2,1)} %constant.30.clone.wall_ref) | copy-start | bytes 5308420
  33.7 1.4 %copy-start.8 = (f32[1,8,384,128]{3,2,1,0:T(8,128)S(1)}, f32[1,8,384,128]{3,2,1,0:T(8,128)}, u32[]{:S(2)}) copy-start(f32[1,8,384,128]{3,2,1,0:T(8,128)} %param.14) | copy-start | bytes 4718596
  35.1 1.1 %copy-start.11 = (bf16[1,8,384,128]{3,2,1,0:T(8,128)(2,1)S(1)}, bf16[1,8,384,128]{3,2,1,0:T(8,128)(2,1)}, u32[]{:S(2)}) copy-start(bf16[1,8,384,128]{3,2,1,0:T(8,128)(2,1)} %param.12) | copy-start | bytes 2359300
  36.2 1.1 %copy-start.12 = (bf16[2,768,256]{2,1,0:T(8,128)(2,1)S(1)}, bf16[2,768,256]{2,1,0:T(8,128)(2,1)}, u32[]{:S(2)}) copy-start(bf16[2,768,256]{2,1,0:T(8,128)(2,1)} %constant.27.clone.line_ref) | copy-start | bytes 2359300
  43.1 1.1 %copy-start.4 = (f32[8,384,128]{2,1,0:T(8,128)}, f32[8,384,128]{2,1,0:T(8,128)S(1)}, u32[]{:S(2)}) copy-start(f32[8,384,128]{2,1,0:T(8,128)S(1)} %get-tuple-element.19.refs_5_) | copy-start | bytes 4718596
  44.3 1.2 %copy-start.6 = (f32[8,384,128]{2,1,0:T(8,128)}, f32[8,384,128]{2,1,0:T(8,128)S(1)}, u32[]{:S(2)}) copy-start(f32[8,384,128]{2,1,0:T(8,128)S(1)} %get-tuple-element.15.inv_ref) | copy-start | bytes 4718596
  45.5 0.6 copy-start.13
  52.0 44.3 %all-to-all-start.1 = ((f32[16,192,128]{2,1,0:T(8,128)}), f32[16,192,128]{2,1,0:T(8,128)}, u32[]{:S(2)}, u32[]{:S(2)}) async-start(f32[16,192,128]{2,1,0:T(8,128)} %time_term.1), calls=%async_computation.1 | async-start | bytes 3145728 | tf_op jit(solution)/shard_map/all_to_all | solution.py:314
  60.1 6.1 %copy-start.3 = (bf16[2,1536,256]{2,1,0:T(8,128)(2,1)S(1)}, bf16[2,1536,256]{2,1,0:T(8,128)(2,1)}, u32[]{:S(2)}) copy-start(bf16[2,1536,256]{2,1,0:T(8,128)(2,1)} %constant.28.clone.table_ref) | copy-start | bytes 4718596
  60.1 6.1 %copy-start.5 = (f32[8,384,128]{2,1,0:T(8,128)S(1)}, f32[8,384,128]{2,1,0:T(8,128)}, u32[]{:S(2)}) copy-start(f32[8,384,128]{2,1,0:T(8,128)} %copy-done.4) | copy-start | bytes 4718596
  60.2 6.1 %collective-permute-start.6 = (f32[8,384,128]{2,1,0:T(8,128)}, f32[8,384,128]{2,1,0:T(8,128)S(1)}, u32[]{:S(2)}, u32[]{:S(2)}) collective-permute-start(f32[8,384,128]{2,1,0:T(8,128)} %collective-permute-done.2.before_ref.refs_0_), channel_id=1, source_target_pairs={{0,1},{1,0},{2,3},{3,2},{4,5},{5,4},{6,7},{7,6},{8,9},{9,8},{10,11... | collective-permute-start | bytes 4718600 | tf_op jit(solution)/shard_map/ppermute | solution.py:316
  60.3 6.0 %collective-permute-start.7 = (f32[8,384,128]{2,1,0:T(8,128)}, f32[8,384,128]{2,1,0:T(8,128)S(1)}, u32[]{:S(2)}, u32[]{:S(2)}) collective-permute-start(f32[8,384,128]{2,1,0:T(8,128)} %collective-permute-done.3.after_ref.refs_2_), channel_id=1, source_target_pairs={{0,1},{1,0},{2,3},{3,2},{4,5},{5,4},{6,7},{7,6},{8,9},{9,8},{10,11... | collective-permute-start | bytes 4718600 | tf_op jit(solution)/shard_map/ppermute | solution.py:316
  64.2 19.3 %collective-permute-start.4 = (f32[4,384,128]{2,1,0:T(8,128)S(1)}, f32[4,384,128]{2,1,0:T(8,128)S(1)}, u32[]{:S(2)}, u32[]{:S(2)}) collective-permute-start(f32[4,384,128]{2,1,0:T(8,128)S(1)} %get-tuple-element.17), channel_id=1, source_target_pairs={{0,2},{1,3},{2,4},{3,5},{4,6},{5,7},{6,0},{7,1},{8,10},{9,11},{10,... | collective-permute-start | bytes 2359304 | tf_op jit(solution)/shard_map/ppermute | solution.py:299
  64.5 20.3 %collective-permute-start.5 = (f32[4,384,128]{2,1,0:T(8,128)S(1)}, f32[4,384,128]{2,1,0:T(8,128)S(1)}, u32[]{:S(2)}, u32[]{:S(2)}) collective-permute-start(f32[4,384,128]{2,1,0:T(8,128)S(1)} %get-tuple-element.18), channel_id=1, source_target_pairs={{2,0},{3,1},{4,2},{5,3},{6,4},{7,5},{0,6},{1,7},{10,8},{11,9},{12,... | collective-permute-start | bytes 2359304 | tf_op jit(solution)/shard_map/ppermute | solution.py:300
  71.0 17.2 %copy-start.9 = (bf16[2,768,256]{2,1,0:T(8,128)(2,1)S(1)}, bf16[2,768,256]{2,1,0:T(8,128)(2,1)}, u32[]{:S(2)}) copy-start(bf16[2,768,256]{2,1,0:T(8,128)(2,1)} %constant.29.clone.table_ref) | copy-start | bytes 2359300
  84.8 2.3 %collective-permute-start.8 = (f32[4,384,128]{2,1,0:T(8,128)S(1)}, f32[4,384,128]{2,1,0:T(8,128)S(1)}, u32[]{:S(2)}, u32[]{:S(2)}) collective-permute-start(f32[4,384,128]{2,1,0:T(8,128)S(1)} %get-tuple-element.21.refs_0_), channel_id=1, source_target_pairs={{0,1},{1,0},{2,3},{3,2},{4,5},{5,4},{6,7},{7,6},{8,9},{9,8},{10,11... | collective-permute-start | bytes 2359304 | tf_op jit(solution)/shard_map/ppermute | solution.py:316
  84.8 3.4 %collective-permute-start.9 = (f32[4,384,128]{2,1,0:T(8,128)S(1)}, f32[4,384,128]{2,1,0:T(8,128)S(1)}, u32[]{:S(2)}, u32[]{:S(2)}) collective-permute-start(f32[4,384,128]{2,1,0:T(8,128)S(1)} %get-tuple-element.22.refs_2_), channel_id=1, source_target_pairs={{0,1},{1,0},{2,3},{3,2},{4,5},{5,4},{6,7},{7,6},{8,9},{9,8},{10,11... | collective-permute-start | bytes 2359304 | tf_op jit(solution)/shard_map/ppermute | solution.py:316
  88.2 8.1 %copy-start.7 = (f32[8,384,128]{2,1,0:T(8,128)S(1)}, f32[8,384,128]{2,1,0:T(8,128)}, u32[]{:S(2)}) copy-start(f32[8,384,128]{2,1,0:T(8,128)} %copy-done.6) | copy-start | bytes 4718596
